TPU v7x, 32 devices: a whole 2x2x4 slice. The times are simulated.
32 devices in a mesh: seq: 8 (over z, x), mp: 2 (over y), role: 2 (over core).
Axes of the slice: x: 2, y: 2, z: 4, core: 2. Of those that a mesh axis runs over, the one named last changes fastest.
Arguments:
- gen_hidden: bfloat16 [8, 16, 3072], P('seq', None, ('mp', 'role')), may hold values from -6 to 6
- gen_out_weight: bfloat16 [3072, 128], P(('mp', 'role')), may hold values from -0.109375 to 0.109375
- patch_order: int32 [8], replicated, may hold values from 0 to 7, each once
- frame_block: int32 [16], replicated, may hold values from 0 to 8, as said below
- embed_weight: bfloat16 [128, 3072], replicated, may hold values from -0.5 to 0.5
- pos_table: bfloat16 [8, 3072], replicated, may hold values from -3 to 3
- norm_gain: bfloat16 [3072], replicated, may hold values from 0.099609375 to 1.8984375
- qkv_weight: bfloat16 [3072, 3, 2048], P(None, None, ('mp', 'role')), may hold values from -0.109375 to 0.109375
- out_weight: bfloat16 [2048, 3072], P(('mp', 'role')), may hold values from -0.125 to 0.125
Outputs:
- disc_out: bfloat16 [128, 3072], P(('seq', 'mp', 'role'))
Inputs may be any that keep to these rules, and one draw needn't show every extreme that they name: `patch_order`: each patch position appears in exactly one slot. `frame_block`: blocks are runs of consecutive frames with indices never falling, each of 1 to 4 frames, at least one of exactly 4; frames share a block iff their indices are equal.
All inputs are finite; a program needn't handle non-finite values.
Results may differ from a plain program's by a relative error of at most 0.006.
Values may be sent and summed in bfloat16 or wider, within the bound.
No kernel may reach another device: no remote copies, remote signals or barrier semaphores. Data moves between devices by JAX's collectives and lax.ppermute only.
A program may use at most 64 MiB of HBM per device.

v0:
```python
import functools

import jax
import jax.numpy as jnp
from jax import lax
from jax.experimental import pallas as pl
from jax.experimental.pallas import tpu as pltpu
from jax.sharding import PartitionSpec as P

HS = 128
MOSTB = 4
REACH = MOSTB - 1
GROUP = ("mp", "role")
EVERY = ("seq", "mp", "role")
LANES = 128
STEP_ROWS = 256
MIB = 1024 * 1024
VMEM = pl.BlockSpec(memory_space=pltpu.VMEM)
SMEM = pl.BlockSpec(memory_space=pltpu.SMEM)
HBM = pl.BlockSpec(memory_space=pltpu.HBM)


def dot(a, b):
    return jnp.dot(a, b, preferred_element_type=jnp.float32)


def latent_kernel(
    frame_dev, hidden_hbm, weight_hbm, out_ref, hidden_ref, weight_ref, padded_ref, sems
):
    copies = [
        pltpu.make_async_copy(hidden_hbm, hidden_ref, sems.at[0]),
        pltpu.make_async_copy(weight_hbm, weight_ref, sems.at[1]),
    ]
    for copy in copies:
        copy.start()
    slots, frames, depth = hidden_ref.shape
    seqs, group, _, window, channels = out_ref.shape
    padded_ref[...] = jnp.zeros_like(padded_ref)
    for copy in copies:
        copy.wait()
    for slot in range(slots):
        padded_ref[slot, REACH : REACH + frames] = dot(hidden_ref[slot], weight_ref[...])
    for to in range(seqs):
        piece = padded_ref[:, to * frame_dev : to * frame_dev + window]
        for member in range(group):
            out_ref[to, member] = piece.astype(out_ref.dtype)


def attend_kernel(
    frame_dev,
    order_ref,
    block_ref,
    partial_ref,
    embed_ref,
    pos_ref,
    gain_ref,
    weight_ref,
    out_weight_ref,
    mixed_ref,
    mine_ref,
    latent_ref,
    embedded_ref,
    normed_ref,
    key_ref,
    value_ref,
    own_ref,
):
    seqs, group, slots, window, channels = partial_ref.shape
    patches = seqs * slots
    rows = patches * window
    own_rows = frame_dev * patches
    share = own_rows // group
    model = embed_ref.shape[1]
    cols = out_weight_ref.shape[0]
    frames = block_ref.shape[0]
    device = lax.axis_index("seq")
    member = lax.axis_index(GROUP)

    def place(slot):
        total = partial_ref[slot // slots, 0, slot % slots].astype(jnp.float32)
        for other in range(1, group):
            total = total + partial_ref[slot // slots, other, slot % slots].astype(jnp.float32)
        at = order_ref[slot]
        for frame in range(window):
            latent_ref[frame, pl.ds(at, 1), :] = total[frame : frame + 1]

    if patches <= 16:
        for slot in range(patches):
            place(slot)
    else:
        pl.loop(0, patches)(place)

    gain = jnp.concatenate(
        [gain_ref[at : at + 1, :].astype(jnp.float32) for at in range(model // LANES)], axis=1
    )
    pos = pos_ref[...].astype(jnp.float32)
    chunk = max(1, min(window, STEP_ROWS // patches))

    def project(step):
        start = step * chunk
        part = latent_ref[pl.ds(start, chunk)].reshape(chunk * patches, channels)
        embedded = dot(part.astype(jnp.bfloat16), embed_ref[...])
        embedded = embedded.reshape(chunk, patches, model) + pos[None]
        embedded_ref[pl.ds(start, chunk)] = embedded
        mean = jnp.sum(embedded * embedded, axis=-1, keepdims=True) / model
        normed = embedded * lax.rsqrt(mean + 1e-06) * gain[None]
        normed = normed.reshape(chunk * patches, model).astype(jnp.bfloat16)
        at = pl.ds(start * patches, chunk * patches)
        normed_ref[at] = normed
        key_ref[at] = dot(normed, weight_ref[1]).astype(jnp.bfloat16)
        value_ref[at] = dot(normed, weight_ref[2]).astype(jnp.bfloat16)

    if chunk == window:
        project(0)
    else:
        pl.loop(0, window // chunk)(project)

    query = dot(normed_ref[REACH * patches : REACH * patches + own_rows], weight_ref[0])
    query = query.astype(jnp.bfloat16)
    key, value = key_ref[...], value_ref[...]

    def block_of(frame):
        inside = jnp.logical_and(frame >= 0, frame < frames)
        return jnp.where(inside, block_ref[jnp.clip(frame, 0, frames - 1)], -1)

    row_frame = lax.broadcasted_iota(jnp.int32, (own_rows, rows), 0) // patches
    col_frame = lax.broadcasted_iota(jnp.int32, (own_rows, rows), 1) // patches
    row_block = jnp.full((own_rows, rows), -2, jnp.int32)
    col_block = jnp.full((own_rows, rows), -1, jnp.int32)
    for frame in range(frame_dev):
        row_block = jnp.where(row_frame == frame, block_of(device * frame_dev + frame), row_block)
    for frame in range(window):
        col_block = jnp.where(
            col_frame == frame, block_of(device * frame_dev - REACH + frame), col_block
        )
    mask = row_block == col_block

    heads = []
    for head in range(cols // HS):
        at = slice(head * HS, (head + 1) * HS)
        scores = lax.dot_general(
            query[:, at], key[:, at], (((1,), (1,)), ((), ())), preferred_element_type=jnp.float32
        ) * (HS**-0.5)
        scores = jnp.where(mask, scores, -1e30)
        top = jnp.max(scores, axis=-1, keepdims=True)
        expo = jnp.where(mask, jnp.exp(scores - top), 0.0)
        probs = (expo / jnp.sum(expo, axis=-1, keepdims=True)).astype(jnp.bfloat16)
        heads.append(dot(probs, value[:, at]).astype(jnp.bfloat16))
    mixed = dot(jnp.concatenate(heads, axis=1), out_weight_ref[...])
    own = embedded_ref[REACH : REACH + frame_dev].reshape(own_rows, model)
    for other in range(group):
        at = slice(other * share, (other + 1) * share)
        mixed_ref[other] = mixed[at].astype(jnp.bfloat16)
        own_ref[other] = own[at]
    mine_ref[...] = own_ref[member]


def sum_kernel(mine_ref, mixed_ref, out_ref):
    total = mine_ref[...]
    for member in range(mixed_ref.shape[0]):
        total = total + mixed_ref[member].astype(jnp.float32)
    out_ref[...] = total.astype(jnp.bfloat16)


def on_device(
    gen_hidden,
    gen_out_weight,
    patch_order,
    frame_block,
    embed_weight,
    pos_table,
    norm_gain,
    qkv_weight,
    out_weight,
):
    slots, frames, depth = gen_hidden.shape
    channels, model = embed_weight.shape
    cols = qkv_weight.shape[2]
    seqs = lax.axis_size("seq")
    group = lax.axis_size(GROUP)
    patches = seqs * slots
    frame_dev = frames // seqs
    window = frame_dev + 2 * REACH
    rows = window * patches
    own_rows = frame_dev * patches
    share = own_rows // group

    windows = pl.pallas_call(
        functools.partial(latent_kernel, frame_dev),
        out_shape=jax.ShapeDtypeStruct((seqs, group, slots, window, channels), jnp.bfloat16),
        in_specs=[HBM] * 2,
        out_specs=VMEM,
        scratch_shapes=[
            pltpu.VMEM((slots, frames, depth), jnp.bfloat16),
            pltpu.VMEM((depth, channels), jnp.bfloat16),
            pltpu.VMEM((slots, frames + 2 * REACH, channels), jnp.float32),
            pltpu.SemaphoreType.DMA((2,)),
        ],
        compiler_params=pltpu.CompilerParams(vmem_limit_bytes=12 * MIB),
        cost_estimate=pl.CostEstimate(
            flops=20_000_000_000, bytes_accessed=40_000_000, transcendentals=0
        ),
        name="partial_latents",
    )(
        pltpu.with_memory_space_constraint(gen_hidden, pltpu.HBM),
        pltpu.with_memory_space_constraint(gen_out_weight, pltpu.HBM),
    )
    moved = lax.all_to_all(
        windows.reshape(seqs * group, slots, window, channels),
        EVERY,
        split_axis=0,
        concat_axis=0,
        tiled=True,
    ).reshape(seqs, group, slots, window, channels)

    mixed, mine = pl.pallas_call(
        functools.partial(attend_kernel, frame_dev),
        out_shape=(
            jax.ShapeDtypeStruct((group, share, model), jnp.bfloat16),
            jax.ShapeDtypeStruct((share, model), jnp.float32),
        ),
        in_specs=[SMEM] * 2 + [VMEM] * 6,
        out_specs=(VMEM, VMEM),
        scratch_shapes=[
            pltpu.VMEM((window, patches, channels), jnp.float32),
            pltpu.VMEM((window, patches, model), jnp.float32),
            pltpu.VMEM((rows, model), jnp.bfloat16),
            pltpu.VMEM((rows, cols), jnp.bfloat16),
            pltpu.VMEM((rows, cols), jnp.bfloat16),
            pltpu.VMEM((group, share, model), jnp.float32),
        ],
        compiler_params=pltpu.CompilerParams(
            vmem_limit_bytes=(24 if rows <= STEP_ROWS else 56) * MIB
        ),
        name="attend",
    )(
        patch_order,
        frame_block,
        moved,
        embed_weight,
        pos_table,
        norm_gain.reshape(model // LANES, LANES),
        jnp.transpose(qkv_weight, (1, 0, 2)),
        out_weight,
    )
    mixed = lax.all_to_all(mixed, GROUP, split_axis=0, concat_axis=0, tiled=True)
    return pl.pallas_call(
        sum_kernel,
        out_shape=jax.ShapeDtypeStruct((share, model), jnp.bfloat16),
        in_specs=[VMEM] * 2,
        out_specs=VMEM,
        compiler_params=pltpu.CompilerParams(vmem_limit_bytes=8 * MIB),
        name="final_sum",
    )(mine, mixed)


def solution(mesh):
    in_specs = (
        P("seq", None, ("mp", "role")),
        P(("mp", "role"), None),
        P(),
        P(),
        P(),
        P(),
        P(),
        P(None, None, ("mp", "role")),
        P(("mp", "role"), None),
    )
    out_specs = P(("seq", "mp", "role"), None)
    return jax.shard_map(
        on_device, mesh=mesh, in_specs=in_specs, out_specs=out_specs, check_vma=False
    )
```

profile of v0, /device:TPU:0, one launch (start us, length us, event | category | flops | bytes accessed | tf_op | source)
XLA Modules:
  0.0 27.4 jit_solution(5201332490437895460)
XLA Ops:
  0.0 0.0 copy-start.1
  0.0 0.0 copy-start
  0.0 0.0 copy-start.4
  0.0 0.0 copy-start.3
  0.0 0.0 copy-start.2
  0.0 0.0 copy-start.6
  0.0 0.0 copy-start.5
  0.0 1.3 %partial_latents.1 = bf16[8,4,1,8,128]{4,3,2,1,0:T(8,128)(2,1)S(1)} custom-call(bf16[1,16,768]{2,1,0:T(8,128)(2,1)} %hidden_hbm.1, bf16[768,128]{1,0:T(8,128)(2,1)} %weight_hbm.1), custom_call_target="tpu_custom_call" | custom-call | flops 20000000000 | bytes 40000000 | tf_op jit(solution)/shard_map/partial_latents/pallas_call | solution.py:188
  1.3 14.5 %all_to_all.10 = bf16[32,1,8,128]{3,2,1,0:T(8,128)(2,1)S(1)} all-to-all(bf16[32,1,8,128]{3,2,1,0:T(8,128)(2,1)S(1)} %bitcast.8), channel_id=1, replica_groups=mesh['seq'=8,'mp'=2,'role'=2] {'seq','mp','role'}, dimensions={0} | all-to-all | bytes 131072 | tf_op jit(solution)/shard_map/all_to_all | solution.py:208
  15.8 0.0 copy-done.1
  15.8 0.0 copy-done
  15.8 0.0 copy-done.4
  15.9 0.0 copy-done.3
  15.9 0.0 copy-done.2
  15.9 0.0 copy-done.6
  15.9 0.0 copy-done.5
  15.9 4.2 %attend.1 = (bf16[4,4,3072]{2,1,0:T(4,128)(2,1)S(1)}, f32[4,3072]{1,0:T(4,128)S(1)}) custom-call(s32[8]{0:T(128)S(1)} %copy-done.5, s32[16]{0:T(128)S(1)} %copy-done.6, bf16[8,4,1,8,128]{4,3,2,1,0:T(8,128)(2,1)S(1)} %bitcast.7, bf16[128,3072]{1,0:T(8,128)(2,1)S(1)} %copy-done.2, bf16[8,3072]{1,0:T(8,128)(2,1)S(1)} %copy-done.3, bf16[24,128]{1,0:T(8,128)(2,1)S(1)} %bitcast.9, ...), custom_call_target="tpu_custom_call" | custom-call | tf_op jit(solution)/shard_map/attend/pallas_call | solution.py:216
  20.1 6.7 %all_to_all.11.mixed_ref = bf16[4,4,3072]{2,1,0:T(4,128)(2,1)S(1)} all-to-all(bf16[4,4,3072]{2,1,0:T(4,128)(2,1)S(1)} %get-tuple-element.8), channel_id=1, replica_groups=mesh['seq'=8,'mp'=2,'role'=2] {'mp','role'}, dimensions={0} | all-to-all | bytes 196608 | tf_op jit(solution)/shard_map/all_to_all | solution.py:246
  26.8 0.6 %final_sum.1 = bf16[4,3072]{1,0:T(4,128)(2,1)} custom-call(f32[4,3072]{1,0:T(4,128)S(1)} %get-tuple-element.7.mine_ref, bf16[4,4,3072]{2,1,0:T(4,128)(2,1)S(1)} %all_to_all.11.mixed_ref), custom_call_target="tpu_custom_call" | custom-call | tf_op jit(solution)/shard_map/final_sum/pallas_call | solution.py:247
Async XLA Ops:
  0.0 15.8 %copy-start.1 = (bf16[512,3072]{1,0:T(8,128)(2,1)S(1)}, bf16[512,3072]{1,0:T(8,128)(2,1)}, u32[]{:S(2)}) copy-start(bf16[512,3072]{1,0:T(8,128)(2,1)} %out_weight_ref.1) | copy-start | bytes 9437188
  0.0 15.8 %copy-start = (bf16[3072,3,512]{2,0,1:T(8,128)(2,1)S(1)}, bf16[3072,3,512]{2,0,1:T(8,128)(2,1)}, u32[]{:S(2)}) copy-start(bf16[3072,3,512]{2,0,1:T(8,128)(2,1)} %param.16) | copy-start | bytes 28311556
  0.0 15.8 %copy-start.4 = (bf16[3072]{0:T(1024)(128)(2,1)S(1)}, bf16[3072]{0:T(1024)(128)(2,1)}, u32[]{:S(2)}) copy-start(bf16[3072]{0:T(1024)(128)(2,1)} %param.15) | copy-start | bytes 18436
  0.0 15.8 %copy-start.3 = (bf16[8,3072]{1,0:T(8,128)(2,1)S(1)}, bf16[8,3072]{1,0:T(8,128)(2,1)}, u32[]{:S(2)}) copy-start(bf16[8,3072]{1,0:T(8,128)(2,1)} %pos_ref.1) | copy-start | bytes 147460
  0.0 15.9 %copy-start.2 = (bf16[128,3072]{1,0:T(8,128)(2,1)S(1)}, bf16[128,3072]{1,0:T(8,128)(2,1)}, u32[]{:S(2)}) copy-start(bf16[128,3072]{1,0:T(8,128)(2,1)} %embed_ref.1) | copy-start | bytes 2359300
  0.0 15.9 %copy-start.6 = (s32[16]{0:T(128)S(1)}, s32[16]{0:T(128)}, u32[]{:S(2)}) copy-start(s32[16]{0:T(128)} %block_ref.1) | copy-start | bytes 196
  0.0 15.9 %copy-start.5 = (s32[8]{0:T(128)S(1)}, s32[8]{0:T(128)}, u32[]{:S(2)}) copy-start(s32[8]{0:T(128)} %order_ref.1) | copy-start | bytes 100
where the time goes:
time: 27.6 us; the launch traced here: 27.4 us
  blocking collectives  21.2 us (77%)
  Pallas kernels  6.14 us (22%)
    all_to_all x1, blocking collectives, on_device(): lax.all_to_all(windows.reshape(seqs * group, slots, window, channels), EV...  14.5 us
    all_to_all x1, blocking collectives, on_device(): lax.all_to_all(mixed, GROUP, split_axis=0, concat_axis=0, tiled=True)  6.67 us
    pallas_call x1, Pallas kernels, on_device(): pl.pallas_call(functools.partial(attend_kernel, frame_dev), out_shape=(ja...  4.23 us
    pallas_call x1, Pallas kernels, on_device(): pl.pallas_call(functools.partial(latent_kernel, frame_dev), out_shape=jax...  1.27 us
    pallas_call x1, Pallas kernels, on_device(): pl.pallas_call(sum_kernel, out_shape=jax.ShapeDtypeStruct((share, model),...  0.63 us

commit v1 on v0

v1 whole, which is shorter than its diff:
```python
import functools

import jax
import jax.numpy as jnp
from jax import lax
from jax.experimental import pallas as pl
from jax.experimental.pallas import tpu as pltpu
from jax.sharding import PartitionSpec as P

HS = 128
MOSTB = 4
REACH = MOSTB - 1
GROUP = ("mp", "role")
EVERY = ("seq", "mp", "role")
LANES = 128
STEP_ROWS = 256
MIB = 1024 * 1024
VMEM = pl.BlockSpec(memory_space=pltpu.VMEM)
SMEM = pl.BlockSpec(memory_space=pltpu.SMEM)
HBM = pl.BlockSpec(memory_space=pltpu.HBM)


def dot(a, b):
    return jnp.dot(a, b, preferred_element_type=jnp.float32)


def latent_kernel(
    frame_dev, hidden_hbm, weight_hbm, out_ref, hidden_ref, weight_ref, padded_ref, sems
):
    copies = [
        pltpu.make_async_copy(hidden_hbm, hidden_ref, sems.at[0]),
        pltpu.make_async_copy(weight_hbm, weight_ref, sems.at[1]),
    ]
    for copy in copies:
        copy.start()
    slots, frames, depth = hidden_ref.shape
    seqs, group, _, window, channels = out_ref.shape
    padded_ref[...] = jnp.zeros_like(padded_ref)
    for copy in copies:
        copy.wait()
    for slot in range(slots):
        padded_ref[slot, REACH : REACH + frames] = dot(hidden_ref[slot], weight_ref[...])
    for to in range(seqs):
        piece = padded_ref[:, to * frame_dev : to * frame_dev + window]
        for member in range(group):
            out_ref[to, member] = piece.astype(out_ref.dtype)


def weights_kernel(
    frame_dev,
    window,
    order_ref,
    block_ref,
    embed_ref,
    pos_ref,
    gain_ref,
    weight_ref,
    scaled_ref,
    offset_ref,
    pos_slot_ref,
    pos_mine_ref,
    select_ref,
    select_mine_ref,
    bias_ref,
    natural_ref,
    pos_all_ref,
):
    channels, model = embed_ref.shape
    patches = pos_ref.shape[0]
    frames = block_ref.shape[0]
    own_rows, rows = bias_ref.shape
    share = select_mine_ref.shape[0]
    device = lax.axis_index("seq")
    member = lax.axis_index(GROUP)

    gain = jnp.concatenate(
        [gain_ref[at : at + 1, :].astype(jnp.float32) for at in range(model // LANES)], axis=1
    )
    pos = pos_ref[...].astype(jnp.float32)
    left = jnp.concatenate([embed_ref[...].astype(jnp.float32) * gain, pos * gain], axis=0)
    left = left.astype(jnp.bfloat16)
    for index in range(3):
        both = dot(left, weight_ref[index])
        scaled = both[:channels]
        high = scaled.astype(jnp.bfloat16)
        scaled_ref[index, :channels] = high
        scaled_ref[index, channels:] = (scaled - high.astype(jnp.float32)).astype(jnp.bfloat16)
        natural_ref[index] = both[channels:]
    pos_all_ref[...] = pos

    def place(slot):
        at = pl.ds(order_ref[slot], 1)
        pos_slot_ref[pl.ds(slot, 1), :] = pos_all_ref[at, :]
        for index in range(3):
            offset_ref[index, pl.ds(slot, 1), :] = natural_ref[index, at, :]

    if patches <= 16:
        for slot in range(patches):
            place(slot)
    else:
        pl.loop(0, patches)(place)

    column = lax.broadcasted_iota(jnp.int32, (1, rows), 1)
    column_slot, column_frame = column // window, column % window

    def patch_at(slot, found):
        return jnp.where(column_slot == slot, order_ref[slot], found)

    column_patch = jnp.zeros((1, rows), jnp.int32)
    if patches <= 16:
        for slot in range(patches):
            column_patch = patch_at(slot, column_patch)
    else:
        column_patch = lax.fori_loop(0, patches, patch_at, column_patch)

    def select(count, first):
        row = lax.broadcasted_iota(jnp.int32, (count, rows), 0) + first
        hit = jnp.logical_and(
            column_patch == row % patches, column_frame == row // patches + REACH
        )
        return jnp.where(hit, 1.0, 0.0).astype(jnp.bfloat16)

    select_ref[...] = select(own_rows, 0)
    select_mine_ref[...] = select(share, member * share)
    for frame in range(frame_dev * patches // share):
        row = frame * share

        @pl.when(member == frame)
        def _():
            for at in range(share):
                mine = (row + at) % patches
                pos_mine_ref[at : at + 1, :] = pos_all_ref[mine : mine + 1, :]

    def block_of(frame):
        inside = jnp.logical_and(frame >= 0, frame < frames)
        return jnp.where(inside, block_ref[jnp.clip(frame, 0, frames - 1)], -1)

    column_block = jnp.full((1, rows), -1, jnp.int32)
    for frame in range(window):
        found = block_of(device * frame_dev - REACH + frame)
        column_block = jnp.where(column_frame == frame, found, column_block)
    row_frame = lax.broadcasted_iota(jnp.int32, (own_rows, rows), 0) // patches
    row_block = jnp.full((own_rows, rows), -2, jnp.int32)
    for frame in range(frame_dev):
        row_block = jnp.where(row_frame == frame, block_of(device * frame_dev + frame), row_block)
    bias_ref[...] = jnp.where(row_block == column_block, 0.0, -1e30)


def attend_kernel(
    partial_ref,
    embed_ref,
    scaled_ref,
    offset_ref,
    pos_slot_ref,
    pos_mine_ref,
    select_ref,
    select_mine_ref,
    bias_ref,
    out_weight_ref,
    mixed_ref,
    mine_ref,
    latent_ref,
    scale_ref,
):
    seqs, group, slots, window, channels = partial_ref.shape
    patches = seqs * slots
    rows = patches * window
    share, model = mine_ref.shape
    cols = out_weight_ref.shape[0]

    total = partial_ref[:, 0].astype(jnp.float32)
    for other in range(1, group):
        total = total + partial_ref[:, other].astype(jnp.float32)
    latent_ref[...] = total.reshape(patches, window, channels)
    chunk = min(patches, STEP_ROWS // window)

    def measure(step):
        at = pl.ds(step * chunk, chunk)
        part = latent_ref[at].reshape(chunk * window, channels).astype(jnp.bfloat16)
        embedded = dot(part, embed_ref[...]).reshape(chunk, window, model)
        embedded = embedded + pos_slot_ref[at][:, None]
        mean = jnp.sum(embedded * embedded, axis=-1, keepdims=True) / model
        scale_ref[at] = jnp.broadcast_to(lax.rsqrt(mean + 1e-06), (chunk, window, LANES))

    if chunk == patches:
        measure(0)
    else:
        pl.loop(0, patches // chunk)(measure)

    latents = latent_ref[...].reshape(rows, channels).astype(jnp.bfloat16)
    twice = jnp.concatenate([latents, latents], axis=1)
    scale = scale_ref[...].reshape(rows, LANES)[:, :1]

    def project(index):
        flat = dot(twice, scaled_ref[index]).reshape(patches, window, cols)
        flat = (flat + offset_ref[index][:, None]).reshape(rows, cols)
        return (flat * scale).astype(jnp.bfloat16)

    query = dot(select_ref[...], project(0)).astype(jnp.bfloat16)
    key, value = project(1), project(2)
    bias = bias_ref[...]
    heads = []
    for head in range(cols // HS):
        at = slice(head * HS, (head + 1) * HS)
        scores = lax.dot_general(
            query[:, at], key[:, at], (((1,), (1,)), ((), ())), preferred_element_type=jnp.float32
        )
        scores = scores * (HS**-0.5) + bias
        expo = jnp.exp(scores - jnp.max(scores, axis=-1, keepdims=True))
        probs = (expo / jnp.sum(expo, axis=-1, keepdims=True)).astype(jnp.bfloat16)
        heads.append(dot(probs, value[:, at]).astype(jnp.bfloat16))
    mixed = dot(jnp.concatenate(heads, axis=1), out_weight_ref[...])
    for other in range(group):
        mixed_ref[other] = mixed[other * share : (other + 1) * share].astype(jnp.bfloat16)
    mine = dot(select_mine_ref[...], latents).astype(jnp.bfloat16)
    mine_ref[...] = dot(mine, embed_ref[...]) + pos_mine_ref[...]


def sum_kernel(mine_ref, mixed_ref, out_ref):
    total = mine_ref[...]
    for member in range(mixed_ref.shape[0]):
        total = total + mixed_ref[member].astype(jnp.float32)
    out_ref[...] = total.astype(jnp.bfloat16)


def on_device(
    gen_hidden,
    gen_out_weight,
    patch_order,
    frame_block,
    embed_weight,
    pos_table,
    norm_gain,
    qkv_weight,
    out_weight,
):
    slots, frames, depth = gen_hidden.shape
    channels, model = embed_weight.shape
    cols = qkv_weight.shape[2]
    seqs = lax.axis_size("seq")
    group = lax.axis_size(GROUP)
    patches = seqs * slots
    frame_dev = frames // seqs
    window = frame_dev + 2 * REACH
    rows = window * patches
    own_rows = frame_dev * patches
    share = own_rows // group
    f32, bf16 = jnp.float32, jnp.bfloat16
    array = jax.ShapeDtypeStruct
    grant = (16 if rows <= STEP_ROWS else 40) * MIB

    windows = pl.pallas_call(
        functools.partial(latent_kernel, frame_dev),
        out_shape=array((seqs, group, slots, window, channels), bf16),
        in_specs=[HBM] * 2,
        out_specs=VMEM,
        scratch_shapes=[
            pltpu.VMEM((slots, frames, depth), bf16),
            pltpu.VMEM((depth, channels), bf16),
            pltpu.VMEM((slots, frames + 2 * REACH, channels), f32),
            pltpu.SemaphoreType.DMA((2,)),
        ],
        compiler_params=pltpu.CompilerParams(vmem_limit_bytes=12 * MIB),
        cost_estimate=pl.CostEstimate(
            flops=20_000_000_000, bytes_accessed=40_000_000, transcendentals=0
        ),
        name="partial_latents",
    )(
        pltpu.with_memory_space_constraint(gen_hidden, pltpu.HBM),
        pltpu.with_memory_space_constraint(gen_out_weight, pltpu.HBM),
    )
    moved = lax.all_to_all(
        windows.reshape(seqs * group, slots, window, channels),
        EVERY,
        split_axis=0,
        concat_axis=0,
        tiled=True,
    ).reshape(seqs, group, slots, window, channels)

    products = pl.pallas_call(
        functools.partial(weights_kernel, frame_dev, window),
        out_shape=(
            array((3, 2 * channels, cols), bf16),
            array((3, patches, cols), f32),
            array((patches, model), f32),
            array((share, model), f32),
            array((own_rows, rows), bf16),
            array((share, rows), bf16),
            array((own_rows, rows), f32),
        ),
        in_specs=[SMEM] * 2 + [VMEM] * 4,
        out_specs=(VMEM,) * 7,
        scratch_shapes=[pltpu.VMEM((3, patches, cols), f32), pltpu.VMEM((patches, model), f32)],
        compiler_params=pltpu.CompilerParams(vmem_limit_bytes=24 * MIB),
        cost_estimate=pl.CostEstimate(
            flops=2 * (channels + patches) * model * 3 * cols,
            bytes_accessed=2 * model * 3 * cols,
            transcendentals=0,
        ),
        name="weight_products",
    )(
        patch_order,
        frame_block,
        embed_weight,
        pos_table,
        norm_gain.reshape(model // LANES, LANES),
        jnp.transpose(qkv_weight, (1, 0, 2)),
    )

    mixed, mine = pl.pallas_call(
        attend_kernel,
        out_shape=(array((group, share, model), bf16), array((share, model), f32)),
        in_specs=[VMEM] * 10,
        out_specs=(VMEM, VMEM),
        scratch_shapes=[
            pltpu.VMEM((patches, window, channels), f32),
            pltpu.VMEM((patches, window, LANES), f32),
        ],
        compiler_params=pltpu.CompilerParams(vmem_limit_bytes=grant),
        name="attend",
    )(moved, embed_weight, *products, out_weight)
    mixed = lax.all_to_all(mixed, GROUP, split_axis=0, concat_axis=0, tiled=True)
    return pl.pallas_call(
        sum_kernel,
        out_shape=array((share, model), bf16),
        in_specs=[VMEM] * 2,
        out_specs=VMEM,
        compiler_params=pltpu.CompilerParams(vmem_limit_bytes=8 * MIB),
        name="final_sum",
    )(mine, mixed)


def solution(mesh):
    in_specs = (
        P("seq", None, ("mp", "role")),
        P(("mp", "role"), None),
        P(),
        P(),
        P(),
        P(),
        P(),
        P(None, None, ("mp", "role")),
        P(("mp", "role"), None),
    )
    out_specs = P(("seq", "mp", "role"), None)
    return jax.shard_map(
        on_device, mesh=mesh, in_specs=in_specs, out_specs=out_specs, check_vma=False
    )
```

time: 27.6 us -> 29.8 us (1.080)
  blocking collectives: 21.2 us -> 7.14 us
  local copies, waits for them, and re-layouts: 0.03 us -> 7.98 us
  starting transfers between devices: 0 us -> 7.32 us
  Pallas kernels: 6.14 us -> 6.96 us
    all_to_all x1 -> x0, blocking collectives: 14.5 us -> none  [on_device(): lax.all_to_all(windows.reshape(seqs * group, slots, window, channels), EV...]
    unnamed x14 -> x20, local copies, waits for them, and re-layouts: 0.03 us -> 7.98 us
    all_to_all x0 -> x1, starting transfers between devices: none -> 7.32 us  [on_device(): lax.all_to_all(windows.reshape(seqs * group, slots, window, channels), EV...]
    pallas_call x3 -> x4, Pallas kernels: 6.14 us -> 6.96 us  [the longest x1 2.28 us: on_device(): pl.pallas_call(attend_kernel, out_shape=(array((group, share, model), bf1...]
    all_to_all x1, blocking collectives: 6.67 us -> 7.14 us  [on_device(): lax.all_to_all(mixed, GROUP, split_axis=0, concat_axis=0, tiled=True)]
  transfers between devices with their start and end apart: 0 -> 1, of which waited for: 0 -> 0; matrix products, arithmetic and copies ran while one was open for 0% -> 0% of each run, Pallas kernels for 0% -> 7%
where the time goes in v1:
time: 29.8 us; the launch traced here: 29.5 us
  local copies, waits for them, and re-layouts  7.98 us (27%)
  starting transfers between devices  7.32 us (25%)
  blocking collectives  7.14 us (24%)
  Pallas kernels  6.96 us (23%)
    unnamed x20, local copies, waits for them, and re-layouts  7.98 us
    all_to_all x1, starting transfers between devices, on_device(): lax.all_to_all(windows.reshape(seqs * group, slots, window, channels), EV...  7.32 us
    all_to_all x1, blocking collectives, on_device(): lax.all_to_all(mixed, GROUP, split_axis=0, concat_axis=0, tiled=True)  7.14 us
    pallas_call x1, Pallas kernels, on_device(): pl.pallas_call(attend_kernel, out_shape=(array((group, share, model), bf1...  2.28 us
    pallas_call x1, Pallas kernels, on_device(): pl.pallas_call(functools.partial(weights_kernel, frame_dev, window), out_...  2.17 us
    pallas_call x1, Pallas kernels, on_device(): pl.pallas_call(functools.partial(latent_kernel, frame_dev), out_shape=arr...  1.88 us
    pallas_call x1, Pallas kernels, on_device(): pl.pallas_call(sum_kernel, out_shape=array((share, model), bf16), in_spec...  0.63 us
  transfers between devices with their start and end apart: 1, of which 0 were waited for; matrix products, arithmetic and copies ran while one was open for 0% of the time, Pallas kernels for 7%

profile of v1, /device:TPU:0, one launch (start us, length us, event | category | flops | bytes accessed | tf_op | source)
XLA Modules:
  0.0 29.5 jit_solution(9322609635848549824)
XLA Ops:
  0.0 0.0 copy-start.7
  0.0 0.0 copy-start.6
  0.0 0.0 copy-start.9
  0.0 0.0 copy-start.8
  0.0 0.0 copy-start.1
  0.0 1.9 %partial_latents.1 = bf16[8,4,1,8,128]{4,3,2,1,0:T(8,128)(2,1)} custom-call(bf16[1,16,768]{2,1,0:T(8,128)(2,1)} %hidden_hbm.1, bf16[768,128]{1,0:T(8,128)(2,1)} %weight_hbm.1), custom_call_target="tpu_custom_call" | custom-call | flops 20000000000 | bytes 40000000 | tf_op jit(solution)/shard_map/partial_latents/pallas_call | solution.py:252
  1.9 7.3 %all-to-all-start = ((bf16[32,1,8,128]{3,2,1,0:T(8,128)(2,1)}), bf16[32,1,8,128]{3,2,1,0:T(8,128)(2,1)S(1)}, u32[]{:S(2)}, u32[]{:S(2)}) async-start(bf16[32,1,8,128]{3,2,1,0:T(8,128)(2,1)} %bitcast.1), calls=%async_computation | async-start | bytes 131072 | tf_op jit(solution)/shard_map/all_to_all | solution.py:272
  9.2 0.0 copy-done.7
  9.2 0.0 copy-done.6
  9.3 0.0 copy-done.9
  9.3 0.0 copy-done.8
  9.3 0.0 copy-start
  9.3 3.7 %copy-done = bf16[3072,3,512]{2,0,1:T(8,128)(2,1)S(1)} copy-done((bf16[3072,3,512]{2,0,1:T(8,128)(2,1)S(1)}, bf16[3072,3,512]{2,0,1:T(8,128)(2,1)}, u32[]{:S(2)}) %copy-start) | copy-done | bytes 9437208
  13.0 0.0 copy-start.2
  13.0 1.1 %copy-done.2 = bf16[128,3072]{1,0:T(8,128)(2,1)S(1)} copy-done((bf16[128,3072]{1,0:T(8,128)(2,1)S(1)}, bf16[128,3072]{1,0:T(8,128)(2,1)}, u32[]{:S(2)}) %copy-start.2) | copy-done | bytes 786456
  14.1 2.2 %weight_products.1 = (bf16[3,256,512]{2,1,0:T(8,128)(2,1)S(1)}, f32[3,8,512]{2,1,0:T(8,128)S(1)}, f32[8,3072]{1,0:T(8,128)S(1)}, f32[4,3072]{1,0:T(4,128)S(1)}, ...) custom-call(s32[8]{0:T(128)S(1)} %copy-done.8, s32[16]{0:T(128)S(1)} %copy-done.9, ...), custom_call_target="tpu_custom_call" | custom-call | flops 1283457024 | bytes 9437184 | tf_op jit(solution)/shard_map/weight_products/pallas_call | solution.py:280
  16.3 0.0 copy-start.4
  16.3 0.9 %copy-done.4 = bf16[3,256,512]{2,1,0:T(8,128)(2,1)} copy-done((bf16[3,256,512]{2,1,0:T(8,128)(2,1)}, bf16[3,256,512]{2,1,0:T(8,128)(2,1)S(1)}, u32[]{:S(2)}) %copy-start.4) | copy-done | bytes 786456
  17.2 0.0 all-to-all-done
  17.2 0.0 copy-done.1
  17.2 0.0 copy-start.3
  17.2 1.1 %copy-done.3 = bf16[128,3072]{1,0:T(8,128)(2,1)S(1)} copy-done((bf16[128,3072]{1,0:T(8,128)(2,1)S(1)}, bf16[128,3072]{1,0:T(8,128)(2,1)}, u32[]{:S(2)}) %copy-start.3) | copy-done | bytes 786456
  18.3 0.0 copy-start.5
  18.3 1.1 %copy-done.5 = bf16[3,256,512]{2,1,0:T(8,128)(2,1)S(1)} copy-done((bf16[3,256,512]{2,1,0:T(8,128)(2,1)S(1)}, bf16[3,256,512]{2,1,0:T(8,128)(2,1)}, u32[]{:S(2)}) %copy-start.5) | copy-done | bytes 786456
  19.4 2.3 %attend.1 = (bf16[4,4,3072]{2,1,0:T(4,128)(2,1)S(1)}, f32[4,3072]{1,0:T(4,128)S(1)}) custom-call(bf16[8,4,1,8,128]{4,3,2,1,0:T(8,128)(2,1)S(1)} %bitcast.7, bf16[128,3072]{1,0:T(8,128)(2,1)S(1)} %copy-done.3, bf16[3,256,512]{2,1,0:T(8,128)(2,1)S(1)} %copy-done.5, f32[3,8,512]{2,1,0:T(8,128)S(1)} %get-tuple-element.15.offset_ref, ...), custom_call_target="tpu_custom_call" | custom-call | tf_op jit(solution)/shard_map/attend/pallas_call | solution.py:310
  21.7 7.1 %all_to_all.10.mixed_ref = bf16[4,4,3072]{2,1,0:T(4,128)(2,1)S(1)} all-to-all(bf16[4,4,3072]{2,1,0:T(4,128)(2,1)S(1)} %get-tuple-element.22), channel_id=1, replica_groups=mesh['seq'=8,'mp'=2,'role'=2] {'mp','role'}, dimensions={0} | all-to-all | bytes 196608 | tf_op jit(solution)/shard_map/all_to_all | solution.py:322
  28.9 0.6 %final_sum.1 = bf16[4,3072]{1,0:T(4,128)(2,1)} custom-call(f32[4,3072]{1,0:T(4,128)S(1)} %get-tuple-element.21.mine_ref, bf16[4,4,3072]{2,1,0:T(4,128)(2,1)S(1)} %all_to_all.10.mixed_ref), custom_call_target="tpu_custom_call" | custom-call | tf_op jit(solution)/shard_map/final_sum/pallas_call | solution.py:323
Async XLA Ops:
  0.0 9.2 %copy-start.7 = (bf16[3072]{0:T(1024)(128)(2,1)S(1)}, bf16[3072]{0:T(1024)(128)(2,1)}, u32[]{:S(2)}) copy-start(bf16[3072]{0:T(1024)(128)(2,1)} %param.15) | copy-start | bytes 18436
  0.0 9.2 %copy-start.6 = (bf16[8,3072]{1,0:T(8,128)(2,1)S(1)}, bf16[8,3072]{1,0:T(8,128)(2,1)}, u32[]{:S(2)}) copy-start(bf16[8,3072]{1,0:T(8,128)(2,1)} %pos_ref.1) | copy-start | bytes 147460
  0.0 9.2 %copy-start.9 = (s32[16]{0:T(128)S(1)}, s32[16]{0:T(128)}, u32[]{:S(2)}) copy-start(s32[16]{0:T(128)} %block_ref.1) | copy-start | bytes 196
  0.0 9.3 %copy-start.8 = (s32[8]{0:T(128)S(1)}, s32[8]{0:T(128)}, u32[]{:S(2)}) copy-start(s32[8]{0:T(128)} %order_ref.1) | copy-start | bytes 100
  0.0 17.2 %copy-start.1 = (bf16[512,3072]{1,0:T(8,128)(2,1)S(1)}, bf16[512,3072]{1,0:T(8,128)(2,1)}, u32[]{:S(2)}) copy-start(bf16[512,3072]{1,0:T(8,128)(2,1)} %out_weight_ref.1) | copy-start | bytes 9437188
  1.9 15.3 %all-to-all-start = ((bf16[32,1,8,128]{3,2,1,0:T(8,128)(2,1)}), bf16[32,1,8,128]{3,2,1,0:T(8,128)(2,1)S(1)}, u32[]{:S(2)}, u32[]{:S(2)}) async-start(bf16[32,1,8,128]{3,2,1,0:T(8,128)(2,1)} %bitcast.1), calls=%async_computation | async-start | bytes 131072 | tf_op jit(solution)/shard_map/all_to_all | solution.py:272
  9.3 3.7 %copy-start = (bf16[3072,3,512]{2,0,1:T(8,128)(2,1)S(1)}, bf16[3072,3,512]{2,0,1:T(8,128)(2,1)}, u32[]{:S(2)}) copy-start(bf16[3072,3,512]{2,0,1:T(8,128)(2,1)} %param.16) | copy-start | bytes 28311556
  13.0 1.1 %copy-start.2 = (bf16[128,3072]{1,0:T(8,128)(2,1)S(1)}, bf16[128,3072]{1,0:T(8,128)(2,1)}, u32[]{:S(2)}) copy-start(bf16[128,3072]{1,0:T(8,128)(2,1)} %embed_ref.3) | copy-start | bytes 2359300
  16.3 0.9 %copy-start.4 = (bf16[3,256,512]{2,1,0:T(8,128)(2,1)}, bf16[3,256,512]{2,1,0:T(8,128)(2,1)S(1)}, u32[]{:S(2)}) copy-start(bf16[3,256,512]{2,1,0:T(8,128)(2,1)S(1)} %get-tuple-element.14.scaled_ref) | copy-start | bytes 2359300
  17.2 1.1 %copy-start.3 = (bf16[128,3072]{1,0:T(8,128)(2,1)S(1)}, bf16[128,3072]{1,0:T(8,128)(2,1)}, u32[]{:S(2)}) copy-start(bf16[128,3072]{1,0:T(8,128)(2,1)} %embed_ref.3) | copy-start | bytes 2359300
  18.3 1.1 %copy-start.5 = (bf16[3,256,512]{2,1,0:T(8,128)(2,1)S(1)}, bf16[3,256,512]{2,1,0:T(8,128)(2,1)}, u32[]{:S(2)}) copy-start(bf16[3,256,512]{2,1,0:T(8,128)(2,1)} %copy-done.4) | copy-start | bytes 2359300

commit v2 on v1

--- a/solution.py
+++ b/solution.py
@@ -14,6 +14,8 @@
 EVERY = ("seq", "mp", "role")
 LANES = 128
 STEP_ROWS = 256
+WIDTH = 256
+AHEAD = 3
 MIB = 1024 * 1024
 VMEM = pl.BlockSpec(memory_space=pltpu.VMEM)
 SMEM = pl.BlockSpec(memory_space=pltpu.SMEM)
@@ -54,7 +56,7 @@
     embed_ref,
     pos_ref,
     gain_ref,
-    weight_ref,
+    weight_hbm,
     scaled_ref,
     offset_ref,
     pos_slot_ref,
@@ -64,6 +66,8 @@
     bias_ref,
     natural_ref,
     pos_all_ref,
+    weight_ref,
+    sems,
 ):
     channels, model = embed_ref.shape
     patches = pos_ref.shape[0]
@@ -73,19 +77,35 @@
     device = lax.axis_index("seq")
     member = lax.axis_index(GROUP)
 
+    cols = weight_ref.shape[2]
+    width = min(cols, WIDTH)
+    parts = [(index, at) for index in range(3) for at in range(0, cols, width)]
+
+    def arrival(part):
+        index, at = parts[part]
+        place = (index, slice(None), pl.ds(at, width))
+        return pltpu.make_async_copy(weight_hbm.at[place], weight_ref.at[place], sems.at[part])
+
+    for part in range(AHEAD):
+        arrival(part).start()
+
     gain = jnp.concatenate(
         [gain_ref[at : at + 1, :].astype(jnp.float32) for at in range(model // LANES)], axis=1
     )
     pos = pos_ref[...].astype(jnp.float32)
     left = jnp.concatenate([embed_ref[...].astype(jnp.float32) * gain, pos * gain], axis=0)
     left = left.astype(jnp.bfloat16)
-    for index in range(3):
-        both = dot(left, weight_ref[index])
+    for part, (index, at) in enumerate(parts):
+        arrival(part).wait()
+        if part + AHEAD < len(parts):
+            arrival(part + AHEAD).start()
+        here = slice(at, at + width)
+        both = dot(left, weight_ref[index, :, here])
         scaled = both[:channels]
         high = scaled.astype(jnp.bfloat16)
-        scaled_ref[index, :channels] = high
-        scaled_ref[index, channels:] = (scaled - high.astype(jnp.float32)).astype(jnp.bfloat16)
-        natural_ref[index] = both[channels:]
+        scaled_ref[index, :channels, here] = high
+        scaled_ref[index, channels:, here] = (scaled - high.astype(jnp.float32)).astype(jnp.bfloat16)
+        natural_ref[index, :, here] = both[channels:]
     pos_all_ref[...] = pos
 
     def place(slot):
@@ -156,12 +176,16 @@
     select_ref,
     select_mine_ref,
     bias_ref,
-    out_weight_ref,
+    out_weight_hbm,
     mixed_ref,
     mine_ref,
     latent_ref,
     scale_ref,
+    out_weight_ref,
+    sem,
 ):
+    arrival = pltpu.make_async_copy(out_weight_hbm, out_weight_ref, sem)
+    arrival.start()
     seqs, group, slots, window, channels = partial_ref.shape
     patches = seqs * slots
     rows = patches * window
@@ -209,11 +233,12 @@
         expo = jnp.exp(scores - jnp.max(scores, axis=-1, keepdims=True))
         probs = (expo / jnp.sum(expo, axis=-1, keepdims=True)).astype(jnp.bfloat16)
         heads.append(dot(probs, value[:, at]).astype(jnp.bfloat16))
+    mine = dot(select_mine_ref[...], latents).astype(jnp.bfloat16)
+    mine_ref[...] = dot(mine, embed_ref[...]) + pos_mine_ref[...]
+    arrival.wait()
     mixed = dot(jnp.concatenate(heads, axis=1), out_weight_ref[...])
     for other in range(group):
         mixed_ref[other] = mixed[other * share : (other + 1) * share].astype(jnp.bfloat16)
-    mine = dot(select_mine_ref[...], latents).astype(jnp.bfloat16)
-    mine_ref[...] = dot(mine, embed_ref[...]) + pos_mine_ref[...]
 
 
 def sum_kernel(mine_ref, mixed_ref, out_ref):
@@ -288,9 +313,14 @@
             array((share, rows), bf16),
             array((own_rows, rows), f32),
         ),
-        in_specs=[SMEM] * 2 + [VMEM] * 4,
+        in_specs=[SMEM] * 2 + [VMEM] * 3 + [HBM],
         out_specs=(VMEM,) * 7,
-        scratch_shapes=[pltpu.VMEM((3, patches, cols), f32), pltpu.VMEM((patches, model), f32)],
+        scratch_shapes=[
+            pltpu.VMEM((3, patches, cols), f32),
+            pltpu.VMEM((patches, model), f32),
+            pltpu.VMEM((3, model, cols), bf16),
+            pltpu.SemaphoreType.DMA((3 * (cols // min(cols, WIDTH)),)),
+        ],
         compiler_params=pltpu.CompilerParams(vmem_limit_bytes=24 * MIB),
         cost_estimate=pl.CostEstimate(
             flops=2 * (channels + patches) * model * 3 * cols,
@@ -304,21 +334,28 @@
         embed_weight,
         pos_table,
         norm_gain.reshape(model // LANES, LANES),
-        jnp.transpose(qkv_weight, (1, 0, 2)),
+        pltpu.with_memory_space_constraint(jnp.transpose(qkv_weight, (1, 0, 2)), pltpu.HBM),
     )
 
     mixed, mine = pl.pallas_call(
         attend_kernel,
         out_shape=(array((group, share, model), bf16), array((share, model), f32)),
-        in_specs=[VMEM] * 10,
+        in_specs=[VMEM] * 9 + [HBM],
         out_specs=(VMEM, VMEM),
         scratch_shapes=[
             pltpu.VMEM((patches, window, channels), f32),
             pltpu.VMEM((patches, window, LANES), f32),
+            pltpu.VMEM((cols, model), bf16),
+            pltpu.SemaphoreType.DMA(()),
         ],
         compiler_params=pltpu.CompilerParams(vmem_limit_bytes=grant),
         name="attend",
-    )(moved, embed_weight, *products, out_weight)
+    )(
+        moved,
+        embed_weight,
+        *products,
+        pltpu.with_memory_space_constraint(out_weight, pltpu.HBM),
+    )
     mixed = lax.all_to_all(mixed, GROUP, split_axis=0, concat_axis=0, tiled=True)
     return pl.pallas_call(
         sum_kernel,

time: 29.8 us -> 26.6 us (0.89)
  local copies, waits for them, and re-layouts: 7.98 us -> 0.02 us
  Pallas kernels: 6.96 us -> 10.6 us
  waiting for transfers between devices: 0.01 us -> 1.65 us
  blocking collectives: 7.14 us -> 6.67 us
    unnamed x20 -> x10, local copies, waits for them, and re-layouts: 7.98 us -> 0.02 us
    pallas_call x1, Pallas kernels: 2.17 us -> 5.7 us  [on_device(): pl.pallas_call(functools.partial(weights_kernel, frame_dev, window), out_...]
    all_to_all x1, waiting for transfers between devices: 0.01 us -> 1.65 us  [on_device(): lax.all_to_all(windows.reshape(seqs * group, slots, window, channels), EV...]
    all_to_all x1, blocking collectives: 7.14 us -> 6.67 us  [on_device(): lax.all_to_all(mixed, GROUP, split_axis=0, concat_axis=0, tiled=True)]
  transfers between devices with their start and end apart: 1 -> 1, of which waited for: 0 -> 1; matrix products, arithmetic and copies ran while one was open for 0% -> 0% of each run, Pallas kernels for 7% -> 22%
where the time goes in v2:
time: 26.6 us; the launch traced here: 26.3 us
  Pallas kernels  10.6 us (40%)
  starting transfers between devices  7.32 us (28%)
  blocking collectives  6.67 us (25%)
  waiting for transfers between devices  1.65 us (6%)
    all_to_all x1, starting transfers between devices, on_device(): lax.all_to_all(windows.reshape(seqs * group, slots, window, channels), EV...  7.32 us
    all_to_all x1, blocking collectives, on_device(): lax.all_to_all(mixed, GROUP, split_axis=0, concat_axis=0, tiled=True)  6.67 us
    pallas_call x1, Pallas kernels, on_device(): pl.pallas_call(functools.partial(weights_kernel, frame_dev, window), out_...  5.7 us
    pallas_call x1, Pallas kernels, on_device(): pl.pallas_call(attend_kernel, out_shape=(array((group, share, model), bf1...  2.43 us
    pallas_call x1, Pallas kernels, on_device(): pl.pallas_call(functools.partial(latent_kernel, frame_dev), out_shape=arr...  1.82 us
    all_to_all x1, waiting for transfers between devices, on_device(): lax.all_to_all(windows.reshape(seqs * group, slots, window, channels), EV...  1.65 us
    pallas_call x1, Pallas kernels, on_device(): pl.pallas_call(sum_kernel, out_shape=array((share, model), bf16), in_spec...  0.63 us
  transfers between devices with their start and end apart: 1, of which 1 were waited for; matrix products, arithmetic and copies ran while one was open for 0% of the time, Pallas kernels for 22%

profile of v2, /device:TPU:0, one launch (start us, length us, event | category | flops | bytes accessed | tf_op | source)
XLA Modules:
  0.0 26.3 jit_solution(18302027229331128336)
XLA Ops:
  0.0 0.0 copy-start
  0.0 0.0 copy-start.2
  0.0 0.0 copy-start.1
  0.0 0.0 copy-start.4
  0.0 0.0 copy-start.3
  0.0 1.8 %partial_latents.1 = bf16[8,4,1,8,128]{4,3,2,1,0:T(8,128)(2,1)} custom-call(bf16[1,16,768]{2,1,0:T(8,128)(2,1)} %hidden_hbm.1, bf16[768,128]{1,0:T(8,128)(2,1)} %weight_hbm.1), custom_call_target="tpu_custom_call" | custom-call | flops 20000000000 | bytes 40000000 | tf_op jit(solution)/shard_map/partial_latents/pallas_call | solution.py:277
  1.8 7.3 %all-to-all-start = ((bf16[32,1,8,128]{3,2,1,0:T(8,128)(2,1)}), bf16[32,1,8,128]{3,2,1,0:T(8,128)(2,1)S(1)}, u32[]{:S(2)}, u32[]{:S(2)}) async-start(bf16[32,1,8,128]{3,2,1,0:T(8,128)(2,1)} %bitcast.1), calls=%async_computation | async-start | bytes 131072 | tf_op jit(solution)/shard_map/all_to_all | solution.py:297
  9.2 0.0 copy-done
  9.2 0.0 copy-done.2
  9.2 0.0 copy-done.1
  9.2 0.0 copy-done.4
  9.2 0.0 copy-done.3
  9.2 5.7 %weight_products.1 = (bf16[3,256,512]{2,1,0:T(8,128)(2,1)S(1)}, f32[3,8,512]{2,1,0:T(8,128)S(1)}, f32[8,3072]{1,0:T(8,128)S(1)}, f32[4,3072]{1,0:T(4,128)S(1)}, ...) custom-call(s32[8]{0:T(128)S(1)} %copy-done.3, s32[16]{0:T(128)S(1)} %copy-done.4, ...), custom_call_target="tpu_custom_call" | custom-call | flops 1283457024 | bytes 9437184 | tf_op jit(solution)/shard_map/weight_products/pallas_call | solution.py:305
  14.9 1.7 %all-to-all-done = bf16[32,1,8,128]{3,2,1,0:T(8,128)(2,1)S(1)} async-done(((bf16[32,1,8,128]{3,2,1,0:T(8,128)(2,1)}), bf16[32,1,8,128]{3,2,1,0:T(8,128)(2,1)S(1)}, u32[]{:S(2)}, u32[]{:S(2)}) %all-to-all-start) | async-done | bytes 65568 | tf_op jit(solution)/shard_map/all_to_all | solution.py:297
  16.6 2.4 %attend.1 = (bf16[4,4,3072]{2,1,0:T(4,128)(2,1)S(1)}, f32[4,3072]{1,0:T(4,128)S(1)}) custom-call(bf16[8,4,1,8,128]{4,3,2,1,0:T(8,128)(2,1)S(1)} %bitcast.6, bf16[128,3072]{1,0:T(8,128)(2,1)S(1)} %copy-done, bf16[3,256,512]{2,1,0:T(8,128)(2,1)S(1)} %get-tuple-element.14.scaled_ref, f32[3,8,512]{2,1,0:T(8,128)S(1)} %get-tuple-element.15.offset_ref, ...), custom_call_target="tpu_custom_call" | custom-call | tf_op jit(solution)/shard_map/attend/pallas_call | solution.py:340
  19.0 6.7 %all_to_all.10.mixed_ref = bf16[4,4,3072]{2,1,0:T(4,128)(2,1)S(1)} all-to-all(bf16[4,4,3072]{2,1,0:T(4,128)(2,1)S(1)} %get-tuple-element.22), channel_id=1, replica_groups=mesh['seq'=8,'mp'=2,'role'=2] {'mp','role'}, dimensions={0} | all-to-all | bytes 196608 | tf_op jit(solution)/shard_map/all_to_all | solution.py:359
  25.7 0.6 %final_sum.1 = bf16[4,3072]{1,0:T(4,128)(2,1)} custom-call(f32[4,3072]{1,0:T(4,128)S(1)} %get-tuple-element.21.mine_ref, bf16[4,4,3072]{2,1,0:T(4,128)(2,1)S(1)} %all_to_all.10.mixed_ref), custom_call_target="tpu_custom_call" | custom-call | tf_op jit(solution)/shard_map/final_sum/pallas_call | solution.py:360
Async XLA Ops:
  0.0 9.2 %copy-start = (bf16[128,3072]{1,0:T(8,128)(2,1)S(1)}, bf16[128,3072]{1,0:T(8,128)(2,1)}, u32[]{:S(2)}) copy-start(bf16[128,3072]{1,0:T(8,128)(2,1)} %embed_ref.3) | copy-start | bytes 2359300
  0.0 9.2 %copy-start.2 = (bf16[3072]{0:T(1024)(128)(2,1)S(1)}, bf16[3072]{0:T(1024)(128)(2,1)}, u32[]{:S(2)}) copy-start(bf16[3072]{0:T(1024)(128)(2,1)} %param.15) | copy-start | bytes 18436
  0.0 9.2 %copy-start.1 = (bf16[8,3072]{1,0:T(8,128)(2,1)S(1)}, bf16[8,3072]{1,0:T(8,128)(2,1)}, u32[]{:S(2)}) copy-start(bf16[8,3072]{1,0:T(8,128)(2,1)} %pos_ref.1) | copy-start | bytes 147460
  0.0 9.2 %copy-start.4 = (s32[16]{0:T(128)S(1)}, s32[16]{0:T(128)}, u32[]{:S(2)}) copy-start(s32[16]{0:T(128)} %block_ref.1) | copy-start | bytes 196
  0.0 9.2 %copy-start.3 = (s32[8]{0:T(128)S(1)}, s32[8]{0:T(128)}, u32[]{:S(2)}) copy-start(s32[8]{0:T(128)} %order_ref.1) | copy-start | bytes 100
  1.8 14.7 %all-to-all-start = ((bf16[32,1,8,128]{3,2,1,0:T(8,128)(2,1)}), bf16[32,1,8,128]{3,2,1,0:T(8,128)(2,1)S(1)}, u32[]{:S(2)}, u32[]{:S(2)}) async-start(bf16[32,1,8,128]{3,2,1,0:T(8,128)(2,1)} %bitcast.1), calls=%async_computation | async-start | bytes 131072 | tf_op jit(solution)/shard_map/all_to_all | solution.py:297

commit v3 on v2

--- a/solution.py
+++ b/solution.py
@@ -11,7 +11,7 @@
 MOSTB = 4
 REACH = MOSTB - 1
 GROUP = ("mp", "role")
-EVERY = ("seq", "mp", "role")
+SCATTERED = ("role", "mp", "seq")
 LANES = 128
 STEP_ROWS = 256
 WIDTH = 256
@@ -36,7 +36,7 @@
     for copy in copies:
         copy.start()
     slots, frames, depth = hidden_ref.shape
-    seqs, group, _, window, channels = out_ref.shape
+    group, seqs, _, window, channels = out_ref.shape
     padded_ref[...] = jnp.zeros_like(padded_ref)
     for copy in copies:
         copy.wait()
@@ -45,7 +45,7 @@
     for to in range(seqs):
         piece = padded_ref[:, to * frame_dev : to * frame_dev + window]
         for member in range(group):
-            out_ref[to, member] = piece.astype(out_ref.dtype)
+            out_ref[member, to] = piece.astype(out_ref.dtype)
 
 
 def weights_kernel(
@@ -57,6 +57,7 @@
     pos_ref,
     gain_ref,
     weight_hbm,
+    out_weight_hbm,
     scaled_ref,
     offset_ref,
     pos_slot_ref,
@@ -64,10 +65,12 @@
     select_ref,
     select_mine_ref,
     bias_ref,
+    first_ref,
     natural_ref,
     pos_all_ref,
     weight_ref,
     sems,
+    first_sem,
 ):
     channels, model = embed_ref.shape
     patches = pos_ref.shape[0]
@@ -86,6 +89,9 @@
         place = (index, slice(None), pl.ds(at, width))
         return pltpu.make_async_copy(weight_hbm.at[place], weight_ref.at[place], sems.at[part])
 
+    first = pltpu.make_async_copy(
+        out_weight_hbm.at[pl.ds(0, first_ref.shape[0])], first_ref, first_sem
+    )
     for part in range(AHEAD):
         arrival(part).start()
 
@@ -95,30 +101,7 @@
     pos = pos_ref[...].astype(jnp.float32)
     left = jnp.concatenate([embed_ref[...].astype(jnp.float32) * gain, pos * gain], axis=0)
     left = left.astype(jnp.bfloat16)
-    for part, (index, at) in enumerate(parts):
-        arrival(part).wait()
-        if part + AHEAD < len(parts):
-            arrival(part + AHEAD).start()
-        here = slice(at, at + width)
-        both = dot(left, weight_ref[index, :, here])
-        scaled = both[:channels]
-        high = scaled.astype(jnp.bfloat16)
-        scaled_ref[index, :channels, here] = high
-        scaled_ref[index, channels:, here] = (scaled - high.astype(jnp.float32)).astype(jnp.bfloat16)
-        natural_ref[index, :, here] = both[channels:]
     pos_all_ref[...] = pos
-
-    def place(slot):
-        at = pl.ds(order_ref[slot], 1)
-        pos_slot_ref[pl.ds(slot, 1), :] = pos_all_ref[at, :]
-        for index in range(3):
-            offset_ref[index, pl.ds(slot, 1), :] = natural_ref[index, at, :]
-
-    if patches <= 16:
-        for slot in range(patches):
-            place(slot)
-    else:
-        pl.loop(0, patches)(place)
 
     column = lax.broadcasted_iota(jnp.int32, (1, rows), 1)
     column_slot, column_frame = column // window, column % window
@@ -164,6 +147,33 @@
     for frame in range(frame_dev):
         row_block = jnp.where(row_frame == frame, block_of(device * frame_dev + frame), row_block)
     bias_ref[...] = jnp.where(row_block == column_block, 0.0, -1e30)
+
+    for part, (index, at) in enumerate(parts):
+        arrival(part).wait()
+        if part + AHEAD < len(parts):
+            arrival(part + AHEAD).start()
+        if part + AHEAD == len(parts) - 1:
+            first.start()
+        here = slice(at, at + width)
+        both = dot(left, weight_ref[index, :, here])
+        scaled = both[:channels]
+        high = scaled.astype(jnp.bfloat16)
+        scaled_ref[index, :channels, here] = high
+        scaled_ref[index, channels:, here] = (scaled - high.astype(jnp.float32)).astype(jnp.bfloat16)
+        natural_ref[index, :, here] = both[channels:]
+
+    def place(slot):
+        at = pl.ds(order_ref[slot], 1)
+        pos_slot_ref[pl.ds(slot, 1), :] = pos_all_ref[at, :]
+        for index in range(3):
+            offset_ref[index, pl.ds(slot, 1), :] = natural_ref[index, at, :]
+
+    if patches <= 16:
+        for slot in range(patches):
+            place(slot)
+    else:
+        pl.loop(0, patches)(place)
+    first.wait()
 
 
 def attend_kernel(
@@ -176,42 +186,56 @@
     select_ref,
     select_mine_ref,
     bias_ref,
+    first_ref,
     out_weight_hbm,
     mixed_ref,
     mine_ref,
     latent_ref,
     scale_ref,
-    out_weight_ref,
+    second_ref,
     sem,
 ):
-    arrival = pltpu.make_async_copy(out_weight_hbm, out_weight_ref, sem)
+    half = first_ref.shape[0]
+    arrival = pltpu.make_async_copy(out_weight_hbm.at[pl.ds(half, half)], second_ref, sem)
     arrival.start()
-    seqs, group, slots, window, channels = partial_ref.shape
+    everyone, slots, window, channels = partial_ref.shape
+    group = mixed_ref.shape[0]
+    seqs = everyone // group
     patches = seqs * slots
     rows = patches * window
     share, model = mine_ref.shape
-    cols = out_weight_ref.shape[0]
-
-    total = partial_ref[:, 0].astype(jnp.float32)
+    cols = out_weight_hbm.shape[0]
+
+    total = partial_ref[:seqs].astype(jnp.float32)
     for other in range(1, group):
-        total = total + partial_ref[:, other].astype(jnp.float32)
+        total = total + partial_ref[other * seqs : (other + 1) * seqs].astype(jnp.float32)
     latent_ref[...] = total.reshape(patches, window, channels)
     chunk = min(patches, STEP_ROWS // window)
 
-    def measure(step):
-        at = pl.ds(step * chunk, chunk)
-        part = latent_ref[at].reshape(chunk * window, channels).astype(jnp.bfloat16)
-        embedded = dot(part, embed_ref[...]).reshape(chunk, window, model)
-        embedded = embedded + pos_slot_ref[at][:, None]
+    latents = latent_ref[...].reshape(rows, channels).astype(jnp.bfloat16)
+    mine = dot(select_mine_ref[...], latents).astype(jnp.bfloat16)
+
+    def measure(start, part):
+        embedded = embedded_rows(part)[: chunk * window].reshape(chunk, window, model)
+        embedded = embedded + pos_slot_ref[pl.ds(start, chunk)][:, None]
         mean = jnp.sum(embedded * embedded, axis=-1, keepdims=True) / model
-        scale_ref[at] = jnp.broadcast_to(lax.rsqrt(mean + 1e-06), (chunk, window, LANES))
+        scale = jnp.broadcast_to(lax.rsqrt(mean + 1e-06), (chunk, window, LANES))
+        scale_ref[pl.ds(start, chunk)] = scale
+
+    def embedded_rows(part):
+        both = dot(jnp.concatenate([part, mine], axis=0), embed_ref[...])
+        mine_ref[...] = both[part.shape[0] :] + pos_mine_ref[...]
+        return both
 
     if chunk == patches:
-        measure(0)
+        measure(0, latents)
     else:
-        pl.loop(0, patches // chunk)(measure)
-
-    latents = latent_ref[...].reshape(rows, channels).astype(jnp.bfloat16)
+
+        @pl.loop(0, patches // chunk)
+        def _(step):
+            part = latent_ref[pl.ds(step * chunk, chunk)]
+            measure(step * chunk, part.reshape(chunk * window, channels).astype(jnp.bfloat16))
+
     twice = jnp.concatenate([latents, latents], axis=1)
     scale = scale_ref[...].reshape(rows, LANES)[:, :1]
 
@@ -233,10 +257,10 @@
         expo = jnp.exp(scores - jnp.max(scores, axis=-1, keepdims=True))
         probs = (expo / jnp.sum(expo, axis=-1, keepdims=True)).astype(jnp.bfloat16)
         heads.append(dot(probs, value[:, at]).astype(jnp.bfloat16))
-    mine = dot(select_mine_ref[...], latents).astype(jnp.bfloat16)
-    mine_ref[...] = dot(mine, embed_ref[...]) + pos_mine_ref[...]
+    heads = jnp.concatenate(heads, axis=1)
+    mixed = dot(heads[:, :half], first_ref[...])
     arrival.wait()
-    mixed = dot(jnp.concatenate(heads, axis=1), out_weight_ref[...])
+    mixed = mixed + dot(heads[:, half:], second_ref[...])
     for other in range(group):
         mixed_ref[other] = mixed[other * share : (other + 1) * share].astype(jnp.bfloat16)
 
@@ -262,6 +286,7 @@
     slots, frames, depth = gen_hidden.shape
     channels, model = embed_weight.shape
     cols = qkv_weight.shape[2]
+    out_weight = pltpu.with_memory_space_constraint(out_weight, pltpu.HBM)
     seqs = lax.axis_size("seq")
     group = lax.axis_size(GROUP)
     patches = seqs * slots
@@ -276,7 +301,7 @@
 
     windows = pl.pallas_call(
         functools.partial(latent_kernel, frame_dev),
-        out_shape=array((seqs, group, slots, window, channels), bf16),
+        out_shape=array((group, seqs, slots, window, channels), bf16),
         in_specs=[HBM] * 2,
         out_specs=VMEM,
         scratch_shapes=[
@@ -295,12 +320,14 @@
         pltpu.with_memory_space_constraint(gen_out_weight, pltpu.HBM),
     )
     moved = lax.all_to_all(
-        windows.reshape(seqs * group, slots, window, channels),
-        EVERY,
+        pltpu.with_memory_space_constraint(
+            windows.reshape(group * seqs, slots, window, channels), pltpu.VMEM
+        ),
+        SCATTERED,
         split_axis=0,
         concat_axis=0,
         tiled=True,
-    ).reshape(seqs, group, slots, window, channels)
+    )
 
     products = pl.pallas_call(
         functools.partial(weights_kernel, frame_dev, window),
@@ -312,14 +339,16 @@
             array((own_rows, rows), bf16),
             array((share, rows), bf16),
             array((own_rows, rows), f32),
+            array((cols // 2, model), bf16),
         ),
-        in_specs=[SMEM] * 2 + [VMEM] * 3 + [HBM],
-        out_specs=(VMEM,) * 7,
+        in_specs=[SMEM] * 2 + [VMEM] * 3 + [HBM] * 2,
+        out_specs=(VMEM,) * 8,
         scratch_shapes=[
             pltpu.VMEM((3, patches, cols), f32),
             pltpu.VMEM((patches, model), f32),
             pltpu.VMEM((3, model, cols), bf16),
             pltpu.SemaphoreType.DMA((3 * (cols // min(cols, WIDTH)),)),
+            pltpu.SemaphoreType.DMA(()),
         ],
         compiler_params=pltpu.CompilerParams(vmem_limit_bytes=24 * MIB),
         cost_estimate=pl.CostEstimate(
@@ -335,17 +364,18 @@
         pos_table,
         norm_gain.reshape(model // LANES, LANES),
         pltpu.with_memory_space_constraint(jnp.transpose(qkv_weight, (1, 0, 2)), pltpu.HBM),
+        out_weight,
     )
 
     mixed, mine = pl.pallas_call(
         attend_kernel,
         out_shape=(array((group, share, model), bf16), array((share, model), f32)),
-        in_specs=[VMEM] * 9 + [HBM],
+        in_specs=[VMEM] * 10 + [HBM],
         out_specs=(VMEM, VMEM),
         scratch_shapes=[
             pltpu.VMEM((patches, window, channels), f32),
             pltpu.VMEM((patches, window, LANES), f32),
-            pltpu.VMEM((cols, model), bf16),
+            pltpu.VMEM((cols - cols // 2, model), bf16),
             pltpu.SemaphoreType.DMA(()),
         ],
         compiler_params=pltpu.CompilerParams(vmem_limit_bytes=grant),
@@ -354,7 +384,7 @@
         moved,
         embed_weight,
         *products,
-        pltpu.with_memory_space_constraint(out_weight, pltpu.HBM),
+        out_weight,
     )
     mixed = lax.all_to_all(mixed, GROUP, split_axis=0, concat_axis=0, tiled=True)
     return pl.pallas_call(

time: 26.6 us -> 26.8 us (level)
    pallas_call x1, Pallas kernels: 2.43 us -> 2.7 us  [on_device(): pl.pallas_call(attend_kernel, out_shape=(array((group, share, model), bf1...]
  transfers between devices with their start and end apart: 1 -> 1, of which waited for: 1 -> 1; matrix products, arithmetic and copies ran while one was open for 0% -> 0% of each run, Pallas kernels for 22% -> 21%
where the time goes in v3:
time: 26.8 us; the launch traced here: 26.5 us
  Pallas kernels  10.8 us (40%)
  starting transfers between devices  7.32 us (27%)
  blocking collectives  6.67 us (25%)
  waiting for transfers between devices  1.62 us (6%)
    all_to_all x1, starting transfers between devices, on_device(): lax.all_to_all(pltpu.with_memory_space_constraint(windows.reshape(group *...  7.32 us
    all_to_all x1, blocking collectives, on_device(): lax.all_to_all(mixed, GROUP, split_axis=0, concat_axis=0, tiled=True)  6.67 us
    pallas_call x1, Pallas kernels, on_device(): pl.pallas_call(functools.partial(weights_kernel, frame_dev, window), out_...  5.67 us
    pallas_call x1, Pallas kernels, on_device(): pl.pallas_call(attend_kernel, out_shape=(array((group, share, model), bf1...  2.7 us
    pallas_call x1, Pallas kernels, on_device(): pl.pallas_call(functools.partial(latent_kernel, frame_dev), out_shape=arr...  1.83 us
    all_to_all x1, waiting for transfers between devices, on_device(): lax.all_to_all(pltpu.with_memory_space_constraint(windows.reshape(group *...  1.62 us
    pallas_call x1, Pallas kernels, on_device(): pl.pallas_call(sum_kernel, out_shape=array((share, model), bf16), in_spec...  0.63 us
  transfers between devices with their start and end apart: 1, of which 1 were waited for; matrix products, arithmetic and copies ran while one was open for 0% of the time, Pallas kernels for 21%

profile of v3, /device:TPU:0, one launch (start us, length us, event | category | flops | bytes accessed | tf_op | source)
XLA Modules:
  0.0 26.5 jit_solution(13199192718160130714)
XLA Ops:
  0.0 0.0 copy-start
  0.0 0.0 copy-start.2
  0.0 0.0 copy-start.1
  0.0 0.0 copy-start.4
  0.0 0.0 copy-start.3
  0.0 1.8 %partial_latents.1 = bf16[4,8,1,8,128]{4,3,2,1,0:T(8,128)(2,1)} custom-call(bf16[1,16,768]{2,1,0:T(8,128)(2,1)} %hidden_hbm.1, bf16[768,128]{1,0:T(8,128)(2,1)} %weight_hbm.1), custom_call_target="tpu_custom_call" | custom-call | flops 20000000000 | bytes 40000000 | tf_op jit(solution)/shard_map/partial_latents/pallas_call | solution.py:302
  1.9 7.3 %all-to-all-start = ((bf16[32,1,8,128]{3,2,1,0:T(8,128)(2,1)}), bf16[32,1,8,128]{3,2,1,0:T(8,128)(2,1)S(1)}, u32[]{:S(2)}, u32[]{:S(2)}) async-start(bf16[32,1,8,128]{3,2,1,0:T(8,128)(2,1)} %bitcast), calls=%async_computation | async-start | bytes 131072 | tf_op jit(solution)/shard_map/all_to_all | solution.py:322
  9.2 0.0 copy-done
  9.2 0.0 copy-done.2
  9.2 0.0 copy-done.1
  9.2 0.0 copy-done.4
  9.2 0.0 copy-done.3
  9.2 5.7 %weight_products.1 = (bf16[3,256,512]{2,1,0:T(8,128)(2,1)S(1)}, f32[3,8,512]{2,1,0:T(8,128)S(1)}, f32[8,3072]{1,0:T(8,128)S(1)}, f32[4,3072]{1,0:T(4,128)S(1)}, ...) custom-call(s32[8]{0:T(128)S(1)} %copy-done.3, ...), custom_call_target="tpu_custom_call" | custom-call | flops 1283457024 | bytes 9437184 | tf_op jit(solution)/shard_map/weight_products/pallas_call | solution.py:332
  14.9 1.6 %all-to-all-done.partial_ref = bf16[32,1,8,128]{3,2,1,0:T(8,128)(2,1)S(1)} async-done(((bf16[32,1,8,128]{3,2,1,0:T(8,128)(2,1)}), bf16[32,1,8,128]{3,2,1,0:T(8,128)(2,1)S(1)}, u32[]{:S(2)}, u32[]{:S(2)}) %all-to-all-start) | async-done | bytes 65568 | tf_op jit(solution)/shard_map/all_to_all | solution.py:322
  16.5 2.7 %attend.1 = (bf16[4,4,3072]{2,1,0:T(4,128)(2,1)S(1)}, f32[4,3072]{1,0:T(4,128)S(1)}) custom-call(bf16[32,1,8,128]{3,2,1,0:T(8,128)(2,1)S(1)} %all-to-all-done.partial_ref, bf16[128,3072]{1,0:T(8,128)(2,1)S(1)} %copy-done, bf16[3,256,512]{2,1,0:T(8,128)(2,1)S(1)} %get-tuple-element.15.scaled_ref, f32[3,8,512]{2,1,0:T(8,128)S(1)} %get-tuple-element.16.offset_ref, ...), custom_call_target="tpu_custom_call" | custom-call | tf_op jit(solution)/shard_map/attend/pallas_call | solution.py:370
  19.2 6.7 %all_to_all.10.mixed_ref = bf16[4,4,3072]{2,1,0:T(4,128)(2,1)S(1)} all-to-all(bf16[4,4,3072]{2,1,0:T(4,128)(2,1)S(1)} %get-tuple-element.24), channel_id=1, replica_groups=mesh['seq'=8,'mp'=2,'role'=2] {'mp','role'}, dimensions={0} | all-to-all | bytes 196608 | tf_op jit(solution)/shard_map/all_to_all | solution.py:389
  25.9 0.6 %final_sum.1 = bf16[4,3072]{1,0:T(4,128)(2,1)} custom-call(f32[4,3072]{1,0:T(4,128)S(1)} %get-tuple-element.23.mine_ref, bf16[4,4,3072]{2,1,0:T(4,128)(2,1)S(1)} %all_to_all.10.mixed_ref), custom_call_target="tpu_custom_call" | custom-call | tf_op jit(solution)/shard_map/final_sum/pallas_call | solution.py:390
Async XLA Ops:
  0.0 9.2 %copy-start = (bf16[128,3072]{1,0:T(8,128)(2,1)S(1)}, bf16[128,3072]{1,0:T(8,128)(2,1)}, u32[]{:S(2)}) copy-start(bf16[128,3072]{1,0:T(8,128)(2,1)} %embed_ref.3) | copy-start | bytes 2359300
  0.0 9.2 %copy-start.2 = (bf16[3072]{0:T(1024)(128)(2,1)S(1)}, bf16[3072]{0:T(1024)(128)(2,1)}, u32[]{:S(2)}) copy-start(bf16[3072]{0:T(1024)(128)(2,1)} %param.15) | copy-start | bytes 18436
  0.0 9.2 %copy-start.1 = (bf16[8,3072]{1,0:T(8,128)(2,1)S(1)}, bf16[8,3072]{1,0:T(8,128)(2,1)}, u32[]{:S(2)}) copy-start(bf16[8,3072]{1,0:T(8,128)(2,1)} %pos_ref.1) | copy-start | bytes 147460
  0.0 9.2 %copy-start.4 = (s32[16]{0:T(128)S(1)}, s32[16]{0:T(128)}, u32[]{:S(2)}) copy-start(s32[16]{0:T(128)} %block_ref.1) | copy-start | bytes 196
  0.0 9.2 %copy-start.3 = (s32[8]{0:T(128)S(1)}, s32[8]{0:T(128)}, u32[]{:S(2)}) copy-start(s32[8]{0:T(128)} %order_ref.1) | copy-start | bytes 100
  1.9 14.7 %all-to-all-start = ((bf16[32,1,8,128]{3,2,1,0:T(8,128)(2,1)}), bf16[32,1,8,128]{3,2,1,0:T(8,128)(2,1)S(1)}, u32[]{:S(2)}, u32[]{:S(2)}) async-start(bf16[32,1,8,128]{3,2,1,0:T(8,128)(2,1)} %bitcast), calls=%async_computation | async-start | bytes 131072 | tf_op jit(solution)/shard_map/all_to_all | solution.py:322

commit v4 on v3

--- a/solution.py
+++ b/solution.py
@@ -36,7 +36,8 @@
     for copy in copies:
         copy.start()
     slots, frames, depth = hidden_ref.shape
-    group, seqs, _, window, channels = out_ref.shape
+    everyone, _, window, channels = out_ref.shape
+    seqs = frames // frame_dev
     padded_ref[...] = jnp.zeros_like(padded_ref)
     for copy in copies:
         copy.wait()
@@ -44,8 +45,8 @@
         padded_ref[slot, REACH : REACH + frames] = dot(hidden_ref[slot], weight_ref[...])
     for to in range(seqs):
         piece = padded_ref[:, to * frame_dev : to * frame_dev + window]
-        for member in range(group):
-            out_ref[member, to] = piece.astype(out_ref.dtype)
+        for at in range(to, everyone, seqs):
+            out_ref[at] = piece.astype(out_ref.dtype)
 
 
 def weights_kernel(
@@ -53,11 +54,10 @@
     window,
     order_ref,
     block_ref,
-    embed_ref,
     pos_ref,
     gain_ref,
+    embed_hbm,
     weight_hbm,
-    out_weight_hbm,
     scaled_ref,
     offset_ref,
     pos_slot_ref,
@@ -65,12 +65,12 @@
     select_ref,
     select_mine_ref,
     bias_ref,
-    first_ref,
+    embed_ref,
     natural_ref,
     pos_all_ref,
     weight_ref,
     sems,
-    first_sem,
+    embed_sem,
 ):
     channels, model = embed_ref.shape
     patches = pos_ref.shape[0]
@@ -89,18 +89,12 @@
         place = (index, slice(None), pl.ds(at, width))
         return pltpu.make_async_copy(weight_hbm.at[place], weight_ref.at[place], sems.at[part])
 
-    first = pltpu.make_async_copy(
-        out_weight_hbm.at[pl.ds(0, first_ref.shape[0])], first_ref, first_sem
-    )
+    embed_arrival = pltpu.make_async_copy(embed_hbm, embed_ref, embed_sem)
+    embed_arrival.start()
     for part in range(AHEAD):
         arrival(part).start()
 
-    gain = jnp.concatenate(
-        [gain_ref[at : at + 1, :].astype(jnp.float32) for at in range(model // LANES)], axis=1
-    )
     pos = pos_ref[...].astype(jnp.float32)
-    left = jnp.concatenate([embed_ref[...].astype(jnp.float32) * gain, pos * gain], axis=0)
-    left = left.astype(jnp.bfloat16)
     pos_all_ref[...] = pos
 
     column = lax.broadcasted_iota(jnp.int32, (1, rows), 1)
@@ -148,12 +142,16 @@
         row_block = jnp.where(row_frame == frame, block_of(device * frame_dev + frame), row_block)
     bias_ref[...] = jnp.where(row_block == column_block, 0.0, -1e30)
 
+    gain = jnp.concatenate(
+        [gain_ref[at : at + 1, :].astype(jnp.float32) for at in range(model // LANES)], axis=1
+    )
+    embed_arrival.wait()
+    left = jnp.concatenate([embed_ref[...].astype(jnp.float32) * gain, pos * gain], axis=0)
+    left = left.astype(jnp.bfloat16)
     for part, (index, at) in enumerate(parts):
         arrival(part).wait()
         if part + AHEAD < len(parts):
             arrival(part + AHEAD).start()
-        if part + AHEAD == len(parts) - 1:
-            first.start()
         here = slice(at, at + width)
         both = dot(left, weight_ref[index, :, here])
         scaled = both[:channels]
@@ -173,12 +171,10 @@
             place(slot)
     else:
         pl.loop(0, patches)(place)
-    first.wait()
 
 
 def attend_kernel(
     partial_ref,
-    embed_ref,
     scaled_ref,
     offset_ref,
     pos_slot_ref,
@@ -186,17 +182,16 @@
     select_ref,
     select_mine_ref,
     bias_ref,
-    first_ref,
+    embed_ref,
     out_weight_hbm,
     mixed_ref,
     mine_ref,
     latent_ref,
     scale_ref,
-    second_ref,
+    out_weight_ref,
     sem,
 ):
-    half = first_ref.shape[0]
-    arrival = pltpu.make_async_copy(out_weight_hbm.at[pl.ds(half, half)], second_ref, sem)
+    arrival = pltpu.make_async_copy(out_weight_hbm, out_weight_ref, sem)
     arrival.start()
     everyone, slots, window, channels = partial_ref.shape
     group = mixed_ref.shape[0]
@@ -204,7 +199,7 @@
     patches = seqs * slots
     rows = patches * window
     share, model = mine_ref.shape
-    cols = out_weight_hbm.shape[0]
+    cols = out_weight_ref.shape[0]
 
     total = partial_ref[:seqs].astype(jnp.float32)
     for other in range(1, group):
@@ -212,30 +207,20 @@
     latent_ref[...] = total.reshape(patches, window, channels)
     chunk = min(patches, STEP_ROWS // window)
 
+    def measure(step):
+        at = pl.ds(step * chunk, chunk)
+        part = latent_ref[at].reshape(chunk * window, channels).astype(jnp.bfloat16)
+        embedded = dot(part, embed_ref[...]).reshape(chunk, window, model)
+        embedded = embedded + pos_slot_ref[at][:, None]
+        mean = jnp.sum(embedded * embedded, axis=-1, keepdims=True) / model
+        scale_ref[at] = jnp.broadcast_to(lax.rsqrt(mean + 1e-06), (chunk, window, LANES))
+
+    if chunk == patches:
+        measure(0)
+    else:
+        pl.loop(0, patches // chunk)(measure)
+
     latents = latent_ref[...].reshape(rows, channels).astype(jnp.bfloat16)
-    mine = dot(select_mine_ref[...], latents).astype(jnp.bfloat16)
-
-    def measure(start, part):
-        embedded = embedded_rows(part)[: chunk * window].reshape(chunk, window, model)
-        embedded = embedded + pos_slot_ref[pl.ds(start, chunk)][:, None]
-        mean = jnp.sum(embedded * embedded, axis=-1, keepdims=True) / model
-        scale = jnp.broadcast_to(lax.rsqrt(mean + 1e-06), (chunk, window, LANES))
-        scale_ref[pl.ds(start, chunk)] = scale
-
-    def embedded_rows(part):
-        both = dot(jnp.concatenate([part, mine], axis=0), embed_ref[...])
-        mine_ref[...] = both[part.shape[0] :] + pos_mine_ref[...]
-        return both
-
-    if chunk == patches:
-        measure(0, latents)
-    else:
-
-        @pl.loop(0, patches // chunk)
-        def _(step):
-            part = latent_ref[pl.ds(step * chunk, chunk)]
-            measure(step * chunk, part.reshape(chunk * window, channels).astype(jnp.bfloat16))
-
     twice = jnp.concatenate([latents, latents], axis=1)
     scale = scale_ref[...].reshape(rows, LANES)[:, :1]
 
@@ -257,10 +242,10 @@
         expo = jnp.exp(scores - jnp.max(scores, axis=-1, keepdims=True))
         probs = (expo / jnp.sum(expo, axis=-1, keepdims=True)).astype(jnp.bfloat16)
         heads.append(dot(probs, value[:, at]).astype(jnp.bfloat16))
-    heads = jnp.concatenate(heads, axis=1)
-    mixed = dot(heads[:, :half], first_ref[...])
+    mine = dot(select_mine_ref[...], latents).astype(jnp.bfloat16)
+    mine_ref[...] = dot(mine, embed_ref[...]) + pos_mine_ref[...]
     arrival.wait()
-    mixed = mixed + dot(heads[:, half:], second_ref[...])
+    mixed = dot(jnp.concatenate(heads, axis=1), out_weight_ref[...])
     for other in range(group):
         mixed_ref[other] = mixed[other * share : (other + 1) * share].astype(jnp.bfloat16)
 
@@ -301,7 +286,7 @@
 
     windows = pl.pallas_call(
         functools.partial(latent_kernel, frame_dev),
-        out_shape=array((group, seqs, slots, window, channels), bf16),
+        out_shape=pltpu.VMEM((group * seqs, slots, window, channels), bf16),
         in_specs=[HBM] * 2,
         out_specs=VMEM,
         scratch_shapes=[
@@ -320,9 +305,7 @@
         pltpu.with_memory_space_constraint(gen_out_weight, pltpu.HBM),
     )
     moved = lax.all_to_all(
-        pltpu.with_memory_space_constraint(
-            windows.reshape(group * seqs, slots, window, channels), pltpu.VMEM
-        ),
+        windows,
         SCATTERED,
         split_axis=0,
         concat_axis=0,
@@ -339,9 +322,9 @@
             array((own_rows, rows), bf16),
             array((share, rows), bf16),
             array((own_rows, rows), f32),
-            array((cols // 2, model), bf16),
+            array((channels, model), bf16),
         ),
-        in_specs=[SMEM] * 2 + [VMEM] * 3 + [HBM] * 2,
+        in_specs=[SMEM] * 2 + [VMEM] * 2 + [HBM] * 2,
         out_specs=(VMEM,) * 8,
         scratch_shapes=[
             pltpu.VMEM((3, patches, cols), f32),
@@ -360,29 +343,27 @@
     )(
         patch_order,
         frame_block,
-        embed_weight,
         pos_table,
         norm_gain.reshape(model // LANES, LANES),
+        pltpu.with_memory_space_constraint(embed_weight, pltpu.HBM),
         pltpu.with_memory_space_constraint(jnp.transpose(qkv_weight, (1, 0, 2)), pltpu.HBM),
-        out_weight,
     )
 
     mixed, mine = pl.pallas_call(
         attend_kernel,
         out_shape=(array((group, share, model), bf16), array((share, model), f32)),
-        in_specs=[VMEM] * 10 + [HBM],
+        in_specs=[VMEM] * 9 + [HBM],
         out_specs=(VMEM, VMEM),
         scratch_shapes=[
             pltpu.VMEM((patches, window, channels), f32),
             pltpu.VMEM((patches, window, LANES), f32),
-            pltpu.VMEM((cols - cols // 2, model), bf16),
+            pltpu.VMEM((cols, model), bf16),
             pltpu.SemaphoreType.DMA(()),
         ],
         compiler_params=pltpu.CompilerParams(vmem_limit_bytes=grant),
         name="attend",
     )(
         moved,
-        embed_weight,
         *products,
         out_weight,
     )

time: 26.8 us -> 26.5 us (0.989)
  waiting for transfers between devices: 1.62 us -> 1.14 us
    pallas_call x1, Pallas kernels: 5.67 us -> 6.16 us  [on_device(): pl.pallas_call(functools.partial(weights_kernel, frame_dev, window), out_...]
    all_to_all x1, waiting for transfers between devices: 1.62 us -> 1.14 us  [on_device(): lax.all_to_all(windows, SCATTERED, split_axis=0, concat_axis=0, tiled=True)]
    pallas_call x1, Pallas kernels: 2.7 us -> 2.43 us  [on_device(): pl.pallas_call(attend_kernel, out_shape=(array((group, share, model), bf1...]
  transfers between devices with their start and end apart: 1 -> 1, of which waited for: 1 -> 1; matrix products, arithmetic and copies ran while one was open for 0% -> 0% of each run, Pallas kernels for 21% -> 23%
where the time goes in v4:
time: 26.5 us; the launch traced here: 26.2 us
  Pallas kernels  11 us (42%)
  starting transfers between devices  7.34 us (28%)
  blocking collectives  6.67 us (25%)
  waiting for transfers between devices  1.14 us (4%)
    all_to_all x1, starting transfers between devices, on_device(): lax.all_to_all(windows, SCATTERED, split_axis=0, concat_axis=0, tiled=True)  7.34 us
    all_to_all x1, blocking collectives, on_device(): lax.all_to_all(mixed, GROUP, split_axis=0, concat_axis=0, tiled=True)  6.67 us
    pallas_call x1, Pallas kernels, on_device(): pl.pallas_call(functools.partial(weights_kernel, frame_dev, window), out_...  6.16 us
    pallas_call x1, Pallas kernels, on_device(): pl.pallas_call(attend_kernel, out_shape=(array((group, share, model), bf1...  2.43 us
    pallas_call x1, Pallas kernels, on_device(): pl.pallas_call(functools.partial(latent_kernel, frame_dev), out_shape=plt...  1.77 us
    all_to_all x1, waiting for transfers between devices, on_device(): lax.all_to_all(windows, SCATTERED, split_axis=0, concat_axis=0, tiled=True)  1.14 us
    pallas_call x1, Pallas kernels, on_device(): pl.pallas_call(sum_kernel, out_shape=array((share, model), bf16), in_spec...  0.63 us
  transfers between devices with their start and end apart: 1, of which 1 were waited for; matrix products, arithmetic and copies ran while one was open for 0% of the time, Pallas kernels for 23%

profile of v4, /device:TPU:0, one launch (start us, length us, event | category | flops | bytes accessed | tf_op | source)
XLA Modules:
  0.0 26.2 jit_solution(5239162669043353680)
XLA Ops:
  0.0 0.0 copy-start.1
  0.0 0.0 copy-start
  0.0 0.0 copy-start.3
  0.0 0.0 copy-start.2
  0.0 1.8 %partial_latents.1 = bf16[32,1,8,128]{3,2,1,0:T(8,128)(2,1)} custom-call(bf16[1,16,768]{2,1,0:T(8,128)(2,1)} %hidden_hbm.1, bf16[768,128]{1,0:T(8,128)(2,1)} %weight_hbm.1), custom_call_target="tpu_custom_call" | custom-call | flops 20000000000 | bytes 40000000 | tf_op jit(solution)/shard_map/partial_latents/pallas_call | solution.py:287
  1.8 7.3 %all-to-all-start = ((bf16[32,1,8,128]{3,2,1,0:T(8,128)(2,1)}), bf16[32,1,8,128]{3,2,1,0:T(8,128)(2,1)S(1)}, u32[]{:S(2)}, u32[]{:S(2)}) async-start(bf16[32,1,8,128]{3,2,1,0:T(8,128)(2,1)} %partial_latents.1), calls=%async_computation | async-start | bytes 131072 | tf_op jit(solution)/shard_map/all_to_all | solution.py:307
  9.1 0.0 copy-done.1
  9.1 0.0 copy-done
  9.2 0.0 copy-done.3
  9.2 0.0 copy-done.2
  9.2 6.2 %weight_products.1 = (bf16[3,256,512]{2,1,0:T(8,128)(2,1)S(1)}, f32[3,8,512]{2,1,0:T(8,128)S(1)}, f32[8,3072]{1,0:T(8,128)S(1)}, f32[4,3072]{1,0:T(4,128)S(1)}, ...) custom-call(s32[8]{0:T(128)S(1)} %copy-done.2, ...), custom_call_target="tpu_custom_call" | custom-call | flops 1283457024 | bytes 9437184 | tf_op jit(solution)/shard_map/weight_products/pallas_call | solution.py:315
  15.3 1.1 %all-to-all-done.partial_ref = bf16[32,1,8,128]{3,2,1,0:T(8,128)(2,1)S(1)} async-done(((bf16[32,1,8,128]{3,2,1,0:T(8,128)(2,1)}), bf16[32,1,8,128]{3,2,1,0:T(8,128)(2,1)S(1)}, u32[]{:S(2)}, u32[]{:S(2)}) %all-to-all-start) | async-done | bytes 65568 | tf_op jit(solution)/shard_map/all_to_all | solution.py:307
  16.5 2.4 %attend.1 = (bf16[4,4,3072]{2,1,0:T(4,128)(2,1)S(1)}, f32[4,3072]{1,0:T(4,128)S(1)}) custom-call(bf16[32,1,8,128]{3,2,1,0:T(8,128)(2,1)S(1)} %all-to-all-done.partial_ref, bf16[3,256,512]{2,1,0:T(8,128)(2,1)S(1)} %get-tuple-element.15.scaled_ref, f32[3,8,512]{2,1,0:T(8,128)S(1)} %get-tuple-element.16.offset_ref, ...), custom_call_target="tpu_custom_call" | custom-call | tf_op jit(solution)/shard_map/attend/pallas_call | solution.py:352
  18.9 6.7 %all_to_all.10.mixed_ref = bf16[4,4,3072]{2,1,0:T(4,128)(2,1)S(1)} all-to-all(bf16[4,4,3072]{2,1,0:T(4,128)(2,1)S(1)} %get-tuple-element.24), channel_id=1, replica_groups=mesh['seq'=8,'mp'=2,'role'=2] {'mp','role'}, dimensions={0} | all-to-all | bytes 196608 | tf_op jit(solution)/shard_map/all_to_all | solution.py:370
  25.6 0.6 %final_sum.1 = bf16[4,3072]{1,0:T(4,128)(2,1)} custom-call(f32[4,3072]{1,0:T(4,128)S(1)} %get-tuple-element.23.mine_ref, bf16[4,4,3072]{2,1,0:T(4,128)(2,1)S(1)} %all_to_all.10.mixed_ref), custom_call_target="tpu_custom_call" | custom-call | tf_op jit(solution)/shard_map/final_sum/pallas_call | solution.py:371
Async XLA Ops:
  0.0 9.1 %copy-start.1 = (bf16[3072]{0:T(1024)(128)(2,1)S(1)}, bf16[3072]{0:T(1024)(128)(2,1)}, u32[]{:S(2)}) copy-start(bf16[3072]{0:T(1024)(128)(2,1)} %param.15) | copy-start | bytes 18436
  0.0 9.1 %copy-start = (bf16[8,3072]{1,0:T(8,128)(2,1)S(1)}, bf16[8,3072]{1,0:T(8,128)(2,1)}, u32[]{:S(2)}) copy-start(bf16[8,3072]{1,0:T(8,128)(2,1)} %pos_ref.1) | copy-start | bytes 147460
  0.0 9.2 %copy-start.3 = (s32[16]{0:T(128)S(1)}, s32[16]{0:T(128)}, u32[]{:S(2)}) copy-start(s32[16]{0:T(128)} %block_ref.1) | copy-start | bytes 196
  0.0 9.2 %copy-start.2 = (s32[8]{0:T(128)S(1)}, s32[8]{0:T(128)}, u32[]{:S(2)}) copy-start(s32[8]{0:T(128)} %order_ref.1) | copy-start | bytes 100
  1.8 14.7 %all-to-all-start = ((bf16[32,1,8,128]{3,2,1,0:T(8,128)(2,1)}), bf16[32,1,8,128]{3,2,1,0:T(8,128)(2,1)S(1)}, u32[]{:S(2)}, u32[]{:S(2)}) async-start(bf16[32,1,8,128]{3,2,1,0:T(8,128)(2,1)} %partial_latents.1), calls=%async_computation | async-start | bytes 131072 | tf_op jit(solution)/shard_map/all_to_all | solution.py:307

commit v5 on v4

--- a/solution.py
+++ b/solution.py
@@ -14,8 +14,9 @@
 SCATTERED = ("role", "mp", "seq")
 LANES = 128
 STEP_ROWS = 256
-WIDTH = 256
-AHEAD = 3
+DEPTH = 1024
+AHEAD = 4
+STRIP = 256
 MIB = 1024 * 1024
 VMEM = pl.BlockSpec(memory_space=pltpu.VMEM)
 SMEM = pl.BlockSpec(memory_space=pltpu.SMEM)
@@ -54,9 +55,9 @@
     window,
     order_ref,
     block_ref,
+    embed_ref,
     pos_ref,
     gain_ref,
-    embed_hbm,
     weight_hbm,
     scaled_ref,
     offset_ref,
@@ -65,12 +66,10 @@
     select_ref,
     select_mine_ref,
     bias_ref,
-    embed_ref,
     natural_ref,
     pos_all_ref,
     weight_ref,
     sems,
-    embed_sem,
 ):
     channels, model = embed_ref.shape
     patches = pos_ref.shape[0]
@@ -80,17 +79,14 @@
     device = lax.axis_index("seq")
     member = lax.axis_index(GROUP)
 
-    cols = weight_ref.shape[2]
-    width = min(cols, WIDTH)
-    parts = [(index, at) for index in range(3) for at in range(0, cols, width)]
+    deep = min(model, DEPTH)
+    parts = [(index, at) for index in range(3) for at in range(0, model, deep)]
 
     def arrival(part):
         index, at = parts[part]
-        place = (index, slice(None), pl.ds(at, width))
+        place = (index, pl.ds(at, deep))
         return pltpu.make_async_copy(weight_hbm.at[place], weight_ref.at[place], sems.at[part])
 
-    embed_arrival = pltpu.make_async_copy(embed_hbm, embed_ref, embed_sem)
-    embed_arrival.start()
     for part in range(AHEAD):
         arrival(part).start()
 
@@ -145,20 +141,21 @@
     gain = jnp.concatenate(
         [gain_ref[at : at + 1, :].astype(jnp.float32) for at in range(model // LANES)], axis=1
     )
-    embed_arrival.wait()
     left = jnp.concatenate([embed_ref[...].astype(jnp.float32) * gain, pos * gain], axis=0)
     left = left.astype(jnp.bfloat16)
     for part, (index, at) in enumerate(parts):
         arrival(part).wait()
         if part + AHEAD < len(parts):
             arrival(part + AHEAD).start()
-        here = slice(at, at + width)
-        both = dot(left, weight_ref[index, :, here])
-        scaled = both[:channels]
-        high = scaled.astype(jnp.bfloat16)
-        scaled_ref[index, :channels, here] = high
-        scaled_ref[index, channels:, here] = (scaled - high.astype(jnp.float32)).astype(jnp.bfloat16)
-        natural_ref[index, :, here] = both[channels:]
+        here = slice(at, at + deep)
+        product = dot(left[:, here], weight_ref[index, here])
+        both = product if at == 0 else both + product
+        if at + deep == model:
+            scaled = both[:channels]
+            high = scaled.astype(jnp.bfloat16)
+            scaled_ref[index, :channels] = high
+            scaled_ref[index, channels:] = (scaled - high.astype(jnp.float32)).astype(jnp.bfloat16)
+            natural_ref[index] = both[channels:]
 
     def place(slot):
         at = pl.ds(order_ref[slot], 1)
@@ -175,6 +172,7 @@
 
 def attend_kernel(
     partial_ref,
+    embed_ref,
     scaled_ref,
     offset_ref,
     pos_slot_ref,
@@ -182,7 +180,6 @@
     select_ref,
     select_mine_ref,
     bias_ref,
-    embed_ref,
     out_weight_hbm,
     mixed_ref,
     mine_ref,
@@ -208,12 +205,17 @@
     chunk = min(patches, STEP_ROWS // window)
 
     def measure(step):
-        at = pl.ds(step * chunk, chunk)
-        part = latent_ref[at].reshape(chunk * window, channels).astype(jnp.bfloat16)
-        embedded = dot(part, embed_ref[...]).reshape(chunk, window, model)
-        embedded = embedded + pos_slot_ref[at][:, None]
-        mean = jnp.sum(embedded * embedded, axis=-1, keepdims=True) / model
-        scale_ref[at] = jnp.broadcast_to(lax.rsqrt(mean + 1e-06), (chunk, window, LANES))
+        here = pl.ds(step * chunk, chunk)
+        part = latent_ref[here].reshape(chunk * window, channels).astype(jnp.bfloat16)
+        squares = jnp.zeros((chunk, window, LANES), jnp.float32)
+        for at in range(0, model, STRIP):
+            strip = dot(part, embed_ref[:, at : at + STRIP]).reshape(chunk, window, STRIP)
+            strip = strip + pos_slot_ref[here, at : at + STRIP][:, None]
+            for lane in range(0, STRIP, LANES):
+                piece = strip[:, :, lane : lane + LANES]
+                squares = squares + piece * piece
+        mean = jnp.sum(squares, axis=-1, keepdims=True) / model
+        scale_ref[here] = jnp.broadcast_to(lax.rsqrt(mean + 1e-06), (chunk, window, LANES))
 
     if chunk == patches:
         measure(0)
@@ -322,16 +324,14 @@
             array((own_rows, rows), bf16),
             array((share, rows), bf16),
             array((own_rows, rows), f32),
-            array((channels, model), bf16),
         ),
-        in_specs=[SMEM] * 2 + [VMEM] * 2 + [HBM] * 2,
-        out_specs=(VMEM,) * 8,
+        in_specs=[SMEM] * 2 + [VMEM] * 3 + [HBM],
+        out_specs=(VMEM,) * 7,
         scratch_shapes=[
             pltpu.VMEM((3, patches, cols), f32),
             pltpu.VMEM((patches, model), f32),
             pltpu.VMEM((3, model, cols), bf16),
-            pltpu.SemaphoreType.DMA((3 * (cols // min(cols, WIDTH)),)),
-            pltpu.SemaphoreType.DMA(()),
+            pltpu.SemaphoreType.DMA((3 * (model // min(model, DEPTH)),)),
         ],
         compiler_params=pltpu.CompilerParams(vmem_limit_bytes=24 * MIB),
         cost_estimate=pl.CostEstimate(
@@ -343,9 +343,9 @@
     )(
         patch_order,
         frame_block,
+        embed_weight,
         pos_table,
         norm_gain.reshape(model // LANES, LANES),
-        pltpu.with_memory_space_constraint(embed_weight, pltpu.HBM),
         pltpu.with_memory_space_constraint(jnp.transpose(qkv_weight, (1, 0, 2)), pltpu.HBM),
     )
 
@@ -364,6 +364,7 @@
         name="attend",
     )(
         moved,
+        embed_weight,
         *products,
         out_weight,
     )

time: 26.5 us -> 26.5 us (level)
  waiting for transfers between devices: 1.14 us -> 2.16 us
  Pallas kernels: 11 us -> 10 us
    pallas_call x1, Pallas kernels: 6.16 us -> 5.12 us  [on_device(): pl.pallas_call(functools.partial(weights_kernel, frame_dev, window), out_...]
    all_to_all x1, waiting for transfers between devices: 1.14 us -> 2.16 us  [on_device(): lax.all_to_all(windows, SCATTERED, split_axis=0, concat_axis=0, tiled=True)]
  transfers between devices with their start and end apart: 1 -> 1, of which waited for: 1 -> 1; matrix products, arithmetic and copies ran while one was open for 0% -> 0% of each run, Pallas kernels for 23% -> 19%
where the time goes in v5:
time: 26.5 us; the launch traced here: 26.3 us
  Pallas kernels  10 us (38%)
  starting transfers between devices  7.32 us (28%)
  blocking collectives  6.67 us (25%)
  waiting for transfers between devices  2.16 us (8%)
    all_to_all x1, starting transfers between devices, on_device(): lax.all_to_all(windows, SCATTERED, split_axis=0, concat_axis=0, tiled=True)  7.32 us
    all_to_all x1, blocking collectives, on_device(): lax.all_to_all(mixed, GROUP, split_axis=0, concat_axis=0, tiled=True)  6.67 us
    pallas_call x1, Pallas kernels, on_device(): pl.pallas_call(functools.partial(weights_kernel, frame_dev, window), out_...  5.12 us
    pallas_call x1, Pallas kernels, on_device(): pl.pallas_call(attend_kernel, out_shape=(array((group, share, model), bf1...  2.43 us
    all_to_all x1, waiting for transfers between devices, on_device(): lax.all_to_all(windows, SCATTERED, split_axis=0, concat_axis=0, tiled=True)  2.16 us
    pallas_call x1, Pallas kernels, on_device(): pl.pallas_call(functools.partial(latent_kernel, frame_dev), out_shape=plt...  1.83 us
    pallas_call x1, Pallas kernels, on_device(): pl.pallas_call(sum_kernel, out_shape=array((share, model), bf16), in_spec...  0.63 us
  transfers between devices with their start and end apart: 1, of which 1 were waited for; matrix products, arithmetic and copies ran while one was open for 0% of the time, Pallas kernels for 19%

profile of v5, /device:TPU:0, one launch (start us, length us, event | category | flops | bytes accessed | tf_op | source)
XLA Modules:
  0.0 26.3 jit_solution(11350564391099034916)
XLA Ops:
  0.0 0.0 copy-start
  0.0 0.0 copy-start.2
  0.0 0.0 copy-start.1
  0.0 0.0 copy-start.4
  0.0 0.0 copy-start.3
  0.0 1.8 %partial_latents.1 = bf16[32,1,8,128]{3,2,1,0:T(8,128)(2,1)} custom-call(bf16[1,16,768]{2,1,0:T(8,128)(2,1)} %hidden_hbm.1, bf16[768,128]{1,0:T(8,128)(2,1)} %weight_hbm.1), custom_call_target="tpu_custom_call" | custom-call | flops 20000000000 | bytes 40000000 | tf_op jit(solution)/shard_map/partial_latents/pallas_call | solution.py:289
  1.9 7.3 %all-to-all-start = ((bf16[32,1,8,128]{3,2,1,0:T(8,128)(2,1)}), bf16[32,1,8,128]{3,2,1,0:T(8,128)(2,1)S(1)}, u32[]{:S(2)}, u32[]{:S(2)}) async-start(bf16[32,1,8,128]{3,2,1,0:T(8,128)(2,1)} %partial_latents.1), calls=%async_computation | async-start | bytes 131072 | tf_op jit(solution)/shard_map/all_to_all | solution.py:309
  9.2 0.0 copy-done
  9.2 0.0 copy-done.2
  9.2 0.0 copy-done.1
  9.2 0.0 copy-done.4
  9.2 0.0 copy-done.3
  9.2 5.1 %weight_products.1 = (bf16[3,256,512]{2,1,0:T(8,128)(2,1)S(1)}, f32[3,8,512]{2,1,0:T(8,128)S(1)}, f32[8,3072]{1,0:T(8,128)S(1)}, f32[4,3072]{1,0:T(4,128)S(1)}, ...) custom-call(s32[8]{0:T(128)S(1)} %copy-done.3, s32[16]{0:T(128)S(1)} %copy-done.4, ...), custom_call_target="tpu_custom_call" | custom-call | flops 1283457024 | bytes 9437184 | tf_op jit(solution)/shard_map/weight_products/pallas_call | solution.py:317
  14.4 2.2 %all-to-all-done.partial_ref = bf16[32,1,8,128]{3,2,1,0:T(8,128)(2,1)S(1)} async-done(((bf16[32,1,8,128]{3,2,1,0:T(8,128)(2,1)}), bf16[32,1,8,128]{3,2,1,0:T(8,128)(2,1)S(1)}, u32[]{:S(2)}, u32[]{:S(2)}) %all-to-all-start) | async-done | bytes 65568 | tf_op jit(solution)/shard_map/all_to_all | solution.py:309
  16.5 2.4 %attend.1 = (bf16[4,4,3072]{2,1,0:T(4,128)(2,1)S(1)}, f32[4,3072]{1,0:T(4,128)S(1)}) custom-call(bf16[32,1,8,128]{3,2,1,0:T(8,128)(2,1)S(1)} %all-to-all-done.partial_ref, bf16[128,3072]{1,0:T(8,128)(2,1)S(1)} %copy-done, bf16[3,256,512]{2,1,0:T(8,128)(2,1)S(1)} %get-tuple-element.14.scaled_ref, f32[3,8,512]{2,1,0:T(8,128)S(1)} %get-tuple-element.15.offset_ref, ...), custom_call_target="tpu_custom_call" | custom-call | tf_op jit(solution)/shard_map/attend/pallas_call | solution.py:352
  19.0 6.7 %all_to_all.10.mixed_ref = bf16[4,4,3072]{2,1,0:T(4,128)(2,1)S(1)} all-to-all(bf16[4,4,3072]{2,1,0:T(4,128)(2,1)S(1)} %get-tuple-element.22), channel_id=1, replica_groups=mesh['seq'=8,'mp'=2,'role'=2] {'mp','role'}, dimensions={0} | all-to-all | bytes 196608 | tf_op jit(solution)/shard_map/all_to_all | solution.py:371
  25.6 0.6 %final_sum.1 = bf16[4,3072]{1,0:T(4,128)(2,1)} custom-call(f32[4,3072]{1,0:T(4,128)S(1)} %get-tuple-element.21.mine_ref, bf16[4,4,3072]{2,1,0:T(4,128)(2,1)S(1)} %all_to_all.10.mixed_ref), custom_call_target="tpu_custom_call" | custom-call | tf_op jit(solution)/shard_map/final_sum/pallas_call | solution.py:372
Async XLA Ops:
  0.0 9.2 %copy-start = (bf16[128,3072]{1,0:T(8,128)(2,1)S(1)}, bf16[128,3072]{1,0:T(8,128)(2,1)}, u32[]{:S(2)}) copy-start(bf16[128,3072]{1,0:T(8,128)(2,1)} %embed_ref.3) | copy-start | bytes 2359300
  0.0 9.2 %copy-start.2 = (bf16[3072]{0:T(1024)(128)(2,1)S(1)}, bf16[3072]{0:T(1024)(128)(2,1)}, u32[]{:S(2)}) copy-start(bf16[3072]{0:T(1024)(128)(2,1)} %param.15) | copy-start | bytes 18436
  0.0 9.2 %copy-start.1 = (bf16[8,3072]{1,0:T(8,128)(2,1)S(1)}, bf16[8,3072]{1,0:T(8,128)(2,1)}, u32[]{:S(2)}) copy-start(bf16[8,3072]{1,0:T(8,128)(2,1)} %pos_ref.1) | copy-start | bytes 147460
  0.0 9.2 %copy-start.4 = (s32[16]{0:T(128)S(1)}, s32[16]{0:T(128)}, u32[]{:S(2)}) copy-start(s32[16]{0:T(128)} %block_ref.1) | copy-start | bytes 196
  0.0 9.2 %copy-start.3 = (s32[8]{0:T(128)S(1)}, s32[8]{0:T(128)}, u32[]{:S(2)}) copy-start(s32[8]{0:T(128)} %order_ref.1) | copy-start | bytes 100
  1.9 14.7 %all-to-all-start = ((bf16[32,1,8,128]{3,2,1,0:T(8,128)(2,1)}), bf16[32,1,8,128]{3,2,1,0:T(8,128)(2,1)S(1)}, u32[]{:S(2)}, u32[]{:S(2)}) async-start(bf16[32,1,8,128]{3,2,1,0:T(8,128)(2,1)} %partial_latents.1), calls=%async_computation | async-start | bytes 131072 | tf_op jit(solution)/shard_map/all_to_all | solution.py:309

commit v6 on v5

--- a/solution.py
+++ b/solution.py
@@ -16,7 +16,7 @@
 STEP_ROWS = 256
 DEPTH = 1024
 AHEAD = 4
-STRIP = 256
+STRIP = 512
 MIB = 1024 * 1024
 VMEM = pl.BlockSpec(memory_space=pltpu.VMEM)
 SMEM = pl.BlockSpec(memory_space=pltpu.SMEM)
@@ -59,17 +59,24 @@
     pos_ref,
     gain_ref,
     weight_hbm,
+    out_weight_hbm,
     scaled_ref,
     offset_ref,
-    pos_slot_ref,
+    gram_ref,
+    cross_ref,
+    level_ref,
     pos_mine_ref,
     select_ref,
     select_mine_ref,
     bias_ref,
+    first_ref,
     natural_ref,
+    natural_cross_ref,
+    natural_level_ref,
     pos_all_ref,
     weight_ref,
     sems,
+    first_sem,
 ):
     channels, model = embed_ref.shape
     patches = pos_ref.shape[0]
@@ -87,6 +94,9 @@
         place = (index, pl.ds(at, deep))
         return pltpu.make_async_copy(weight_hbm.at[place], weight_ref.at[place], sems.at[part])
 
+    first = pltpu.make_async_copy(
+        out_weight_hbm.at[pl.ds(0, first_ref.shape[0])], first_ref, first_sem
+    )
     for part in range(AHEAD):
         arrival(part).start()
 
@@ -143,31 +153,46 @@
     )
     left = jnp.concatenate([embed_ref[...].astype(jnp.float32) * gain, pos * gain], axis=0)
     left = left.astype(jnp.bfloat16)
+    def keep(ref, scaled):
+        high = scaled.astype(jnp.bfloat16)
+        ref[:channels] = high
+        ref[channels:] = (scaled - high.astype(jnp.float32)).astype(jnp.bfloat16)
+
+    plain = jnp.concatenate([embed_ref[...], pos_ref[...]], axis=0)
+    both = lax.dot_general(
+        plain, embed_ref[...], (((1,), (1,)), ((), ())), preferred_element_type=jnp.float32
+    )
+    keep(gram_ref, both[:channels])
+    natural_cross_ref[...] = 2.0 * both[channels:]
+    level = jnp.sum(pos * pos, axis=-1, keepdims=True) / channels
+    natural_level_ref[...] = jnp.broadcast_to(level, (patches, channels))
+
     for part, (index, at) in enumerate(parts):
         arrival(part).wait()
         if part + AHEAD < len(parts):
             arrival(part + AHEAD).start()
+        if part + AHEAD == len(parts) - 1:
+            first.start()
         here = slice(at, at + deep)
         product = dot(left[:, here], weight_ref[index, here])
         both = product if at == 0 else both + product
         if at + deep == model:
-            scaled = both[:channels]
-            high = scaled.astype(jnp.bfloat16)
-            scaled_ref[index, :channels] = high
-            scaled_ref[index, channels:] = (scaled - high.astype(jnp.float32)).astype(jnp.bfloat16)
+            keep(scaled_ref.at[index], both[:channels])
             natural_ref[index] = both[channels:]
 
     def place(slot):
-        at = pl.ds(order_ref[slot], 1)
-        pos_slot_ref[pl.ds(slot, 1), :] = pos_all_ref[at, :]
+        to, at = pl.ds(slot, 1), pl.ds(order_ref[slot], 1)
+        cross_ref[to, :] = natural_cross_ref[at, :]
+        level_ref[to, :] = natural_level_ref[at, :]
         for index in range(3):
-            offset_ref[index, pl.ds(slot, 1), :] = natural_ref[index, at, :]
+            offset_ref[index, to, :] = natural_ref[index, at, :]
 
     if patches <= 16:
         for slot in range(patches):
             place(slot)
     else:
         pl.loop(0, patches)(place)
+    first.wait()
 
 
 def attend_kernel(
@@ -175,56 +200,41 @@
     embed_ref,
     scaled_ref,
     offset_ref,
-    pos_slot_ref,
+    gram_ref,
+    cross_ref,
+    level_ref,
     pos_mine_ref,
     select_ref,
     select_mine_ref,
     bias_ref,
+    first_ref,
     out_weight_hbm,
     mixed_ref,
     mine_ref,
-    latent_ref,
-    scale_ref,
-    out_weight_ref,
+    second_ref,
     sem,
 ):
-    arrival = pltpu.make_async_copy(out_weight_hbm, out_weight_ref, sem)
+    half = first_ref.shape[0]
+    arrival = pltpu.make_async_copy(out_weight_hbm.at[pl.ds(half, half)], second_ref, sem)
     arrival.start()
     everyone, slots, window, channels = partial_ref.shape
-    group = mixed_ref.shape[0]
+    group, share, model = mixed_ref.shape
     seqs = everyone // group
     patches = seqs * slots
     rows = patches * window
-    share, model = mine_ref.shape
-    cols = out_weight_ref.shape[0]
+    cols = out_weight_hbm.shape[0]
 
     total = partial_ref[:seqs].astype(jnp.float32)
     for other in range(1, group):
         total = total + partial_ref[other * seqs : (other + 1) * seqs].astype(jnp.float32)
-    latent_ref[...] = total.reshape(patches, window, channels)
-    chunk = min(patches, STEP_ROWS // window)
-
-    def measure(step):
-        here = pl.ds(step * chunk, chunk)
-        part = latent_ref[here].reshape(chunk * window, channels).astype(jnp.bfloat16)
-        squares = jnp.zeros((chunk, window, LANES), jnp.float32)
-        for at in range(0, model, STRIP):
-            strip = dot(part, embed_ref[:, at : at + STRIP]).reshape(chunk, window, STRIP)
-            strip = strip + pos_slot_ref[here, at : at + STRIP][:, None]
-            for lane in range(0, STRIP, LANES):
-                piece = strip[:, :, lane : lane + LANES]
-                squares = squares + piece * piece
-        mean = jnp.sum(squares, axis=-1, keepdims=True) / model
-        scale_ref[here] = jnp.broadcast_to(lax.rsqrt(mean + 1e-06), (chunk, window, LANES))
-
-    if chunk == patches:
-        measure(0)
-    else:
-        pl.loop(0, patches // chunk)(measure)
-
-    latents = latent_ref[...].reshape(rows, channels).astype(jnp.bfloat16)
+    latents = total.reshape(rows, channels).astype(jnp.bfloat16)
     twice = jnp.concatenate([latents, latents], axis=1)
-    scale = scale_ref[...].reshape(rows, LANES)[:, :1]
+    slope = dot(twice, gram_ref[...]).reshape(patches, window, channels)
+    slope = slope + cross_ref[...][:, None]
+    squares = slope * latents.astype(jnp.float32).reshape(patches, window, channels)
+    squares = (squares + level_ref[...][:, None]).reshape(rows, channels)
+    mean = jnp.maximum(jnp.sum(squares, axis=-1, keepdims=True), 0.0) / model
+    scale = lax.rsqrt(mean + 1e-06)
 
     def project(index):
         flat = dot(twice, scaled_ref[index]).reshape(patches, window, cols)
@@ -246,10 +256,14 @@
         heads.append(dot(probs, value[:, at]).astype(jnp.bfloat16))
     mine = dot(select_mine_ref[...], latents).astype(jnp.bfloat16)
     mine_ref[...] = dot(mine, embed_ref[...]) + pos_mine_ref[...]
+    heads = jnp.concatenate(heads, axis=1)
     arrival.wait()
-    mixed = dot(jnp.concatenate(heads, axis=1), out_weight_ref[...])
-    for other in range(group):
-        mixed_ref[other] = mixed[other * share : (other + 1) * share].astype(jnp.bfloat16)
+    for at in range(0, model, STRIP):
+        here = slice(at, at + STRIP)
+        mixed = dot(heads[:, :half], first_ref[:, here]) + dot(heads[:, half:], second_ref[:, here])
+        mixed = mixed.astype(jnp.bfloat16)
+        for other in range(group):
+            mixed_ref[other, :, here] = mixed[other * share : (other + 1) * share]
 
 
 def sum_kernel(mine_ref, mixed_ref, out_ref):
@@ -319,19 +333,25 @@
         out_shape=(
             array((3, 2 * channels, cols), bf16),
             array((3, patches, cols), f32),
-            array((patches, model), f32),
+            array((2 * channels, channels), bf16),
+            array((patches, channels), f32),
+            array((patches, channels), f32),
             array((share, model), f32),
             array((own_rows, rows), bf16),
             array((share, rows), bf16),
             array((own_rows, rows), f32),
+            array((cols // 2, model), bf16),
         ),
-        in_specs=[SMEM] * 2 + [VMEM] * 3 + [HBM],
-        out_specs=(VMEM,) * 7,
+        in_specs=[SMEM] * 2 + [VMEM] * 3 + [HBM] * 2,
+        out_specs=(VMEM,) * 10,
         scratch_shapes=[
             pltpu.VMEM((3, patches, cols), f32),
+            pltpu.VMEM((patches, channels), f32),
+            pltpu.VMEM((patches, channels), f32),
             pltpu.VMEM((patches, model), f32),
             pltpu.VMEM((3, model, cols), bf16),
             pltpu.SemaphoreType.DMA((3 * (model // min(model, DEPTH)),)),
+            pltpu.SemaphoreType.DMA(()),
         ],
         compiler_params=pltpu.CompilerParams(vmem_limit_bytes=24 * MIB),
         cost_estimate=pl.CostEstimate(
@@ -347,17 +367,16 @@
         pos_table,
         norm_gain.reshape(model // LANES, LANES),
         pltpu.with_memory_space_constraint(jnp.transpose(qkv_weight, (1, 0, 2)), pltpu.HBM),
+        out_weight,
     )
 
     mixed, mine = pl.pallas_call(
         attend_kernel,
         out_shape=(array((group, share, model), bf16), array((share, model), f32)),
-        in_specs=[VMEM] * 9 + [HBM],
+        in_specs=[VMEM] * 12 + [HBM],
         out_specs=(VMEM, VMEM),
         scratch_shapes=[
-            pltpu.VMEM((patches, window, channels), f32),
-            pltpu.VMEM((patches, window, LANES), f32),
-            pltpu.VMEM((cols, model), bf16),
+            pltpu.VMEM((cols - cols // 2, model), bf16),
             pltpu.SemaphoreType.DMA(()),
         ],
         compiler_params=pltpu.CompilerParams(vmem_limit_bytes=grant),

time: 26.5 us -> 26.3 us (level)
  waiting for transfers between devices: 2.16 us -> 1.61 us
  Pallas kernels: 10 us -> 10.3 us
    pallas_call x1, Pallas kernels: 5.12 us -> 5.68 us  [on_device(): pl.pallas_call(functools.partial(weights_kernel, frame_dev, window), out_...]
    all_to_all x1, waiting for transfers between devices: 2.16 us -> 1.61 us  [on_device(): lax.all_to_all(windows, SCATTERED, split_axis=0, concat_axis=0, tiled=True)]
  transfers between devices with their start and end apart: 1 -> 1, of which waited for: 1 -> 1; matrix products, arithmetic and copies ran while one was open for 0% -> 0% of each run, Pallas kernels for 19% -> 22%
where the time goes in v6:
time: 26.3 us; the launch traced here: 26 us
  Pallas kernels  10.3 us (39%)
  starting transfers between devices  7.32 us (28%)
  blocking collectives  6.67 us (25%)
  waiting for transfers between devices  1.61 us (6%)
    all_to_all x1, starting transfers between devices, on_device(): lax.all_to_all(windows, SCATTERED, split_axis=0, concat_axis=0, tiled=True)  7.32 us
    all_to_all x1, blocking collectives, on_device(): lax.all_to_all(mixed, GROUP, split_axis=0, concat_axis=0, tiled=True)  6.67 us
    pallas_call x1, Pallas kernels, on_device(): pl.pallas_call(functools.partial(weights_kernel, frame_dev, window), out_...  5.68 us
    pallas_call x1, Pallas kernels, on_device(): pl.pallas_call(attend_kernel, out_shape=(array((group, share, model), bf1...  2.2 us
    pallas_call x1, Pallas kernels, on_device(): pl.pallas_call(functools.partial(latent_kernel, frame_dev), out_shape=plt...  1.83 us
    all_to_all x1, waiting for transfers between devices, on_device(): lax.all_to_all(windows, SCATTERED, split_axis=0, concat_axis=0, tiled=True)  1.61 us
    pallas_call x1, Pallas kernels, on_device(): pl.pallas_call(sum_kernel, out_shape=array((share, model), bf16), in_spec...  0.64 us
  transfers between devices with their start and end apart: 1, of which 1 were waited for; matrix products, arithmetic and copies ran while one was open for 0% of the time, Pallas kernels for 22%

profile of v6, /device:TPU:0, one launch (start us, length us, event | category | flops | bytes accessed | tf_op | source)
XLA Modules:
  0.0 26.0 jit_solution(4503983200832729119)
XLA Ops:
  0.0 0.0 copy-start
  0.0 0.0 copy-start.2
  0.0 0.0 copy-start.1
  0.0 0.0 copy-start.4
  0.0 0.0 copy-start.3
  0.0 1.8 %partial_latents.1 = bf16[32,1,8,128]{3,2,1,0:T(8,128)(2,1)} custom-call(bf16[1,16,768]{2,1,0:T(8,128)(2,1)} %hidden_hbm.1, bf16[768,128]{1,0:T(8,128)(2,1)} %weight_hbm.1), custom_call_target="tpu_custom_call" | custom-call | flops 20000000000 | bytes 40000000 | tf_op jit(solution)/shard_map/partial_latents/pallas_call | solution.py:303
  1.9 7.3 %all-to-all-start = ((bf16[32,1,8,128]{3,2,1,0:T(8,128)(2,1)}), bf16[32,1,8,128]{3,2,1,0:T(8,128)(2,1)S(1)}, u32[]{:S(2)}, u32[]{:S(2)}) async-start(bf16[32,1,8,128]{3,2,1,0:T(8,128)(2,1)} %partial_latents.1), calls=%async_computation | async-start | bytes 131072 | tf_op jit(solution)/shard_map/all_to_all | solution.py:323
  9.2 0.0 copy-done
  9.2 0.0 copy-done.2
  9.2 0.0 copy-done.1
  9.2 0.0 copy-done.4
  9.2 0.0 copy-done.3
  9.2 5.7 %weight_products.1 = (bf16[3,256,512]{2,1,0:T(8,128)(2,1)S(1)}, f32[3,8,512]{2,1,0:T(8,128)S(1)}, bf16[256,128]{1,0:T(8,128)(2,1)S(1)}, f32[8,128]{1,0:T(8,128)S...) custom-call(s32[8]{0:T(128)S(1)} %copy-done.3, ...), custom_call_target="tpu_custom_call" | custom-call | flops 1283457024 | bytes 9437184 | tf_op jit(solution)/shard_map/weight_products/pallas_call | solution.py:331
  14.9 1.6 %all-to-all-done.partial_ref = bf16[32,1,8,128]{3,2,1,0:T(8,128)(2,1)S(1)} async-done(((bf16[32,1,8,128]{3,2,1,0:T(8,128)(2,1)}), bf16[32,1,8,128]{3,2,1,0:T(8,128)(2,1)S(1)}, u32[]{:S(2)}, u32[]{:S(2)}) %all-to-all-start) | async-done | bytes 65568 | tf_op jit(solution)/shard_map/all_to_all | solution.py:323
  16.5 2.2 %attend.1 = (bf16[4,4,3072]{2,1,0:T(4,128)(2,1)S(1)}, f32[4,3072]{1,0:T(4,128)S(1)}) custom-call(bf16[32,1,8,128]{3,2,1,0:T(8,128)(2,1)S(1)} %all-to-all-done.partial_ref, bf16[128,3072]{1,0:T(8,128)(2,1)S(1)} %copy-done, bf16[3,256,512]{2,1,0:T(8,128)(2,1)S(1)} %get-tuple-element.17.scaled_ref, f32[3,8,512]{2,1,0:T(8,128)S(1)} %get-tuple-element.18.offset_ref, ...), custom_call_target="tpu_custom_call" | custom-call | tf_op jit(solution)/shard_map/attend/pallas_call | solution.py:373
  18.7 6.7 %all_to_all.10.mixed_ref = bf16[4,4,3072]{2,1,0:T(4,128)(2,1)S(1)} all-to-all(bf16[4,4,3072]{2,1,0:T(4,128)(2,1)S(1)} %get-tuple-element.28), channel_id=1, replica_groups=mesh['seq'=8,'mp'=2,'role'=2] {'mp','role'}, dimensions={0} | all-to-all | bytes 196608 | tf_op jit(solution)/shard_map/all_to_all | solution.py:390
  25.4 0.6 %final_sum.1 = bf16[4,3072]{1,0:T(4,128)(2,1)} custom-call(f32[4,3072]{1,0:T(4,128)S(1)} %get-tuple-element.27.mine_ref, bf16[4,4,3072]{2,1,0:T(4,128)(2,1)S(1)} %all_to_all.10.mixed_ref), custom_call_target="tpu_custom_call" | custom-call | tf_op jit(solution)/shard_map/final_sum/pallas_call | solution.py:391
Async XLA Ops:
  0.0 9.2 %copy-start = (bf16[128,3072]{1,0:T(8,128)(2,1)S(1)}, bf16[128,3072]{1,0:T(8,128)(2,1)}, u32[]{:S(2)}) copy-start(bf16[128,3072]{1,0:T(8,128)(2,1)} %embed_ref.3) | copy-start | bytes 2359300
  0.0 9.2 %copy-start.2 = (bf16[3072]{0:T(1024)(128)(2,1)S(1)}, bf16[3072]{0:T(1024)(128)(2,1)}, u32[]{:S(2)}) copy-start(bf16[3072]{0:T(1024)(128)(2,1)} %param.15) | copy-start | bytes 18436
  0.0 9.2 %copy-start.1 = (bf16[8,3072]{1,0:T(8,128)(2,1)S(1)}, bf16[8,3072]{1,0:T(8,128)(2,1)}, u32[]{:S(2)}) copy-start(bf16[8,3072]{1,0:T(8,128)(2,1)} %pos_ref.1) | copy-start | bytes 147460
  0.0 9.2 %copy-start.4 = (s32[16]{0:T(128)S(1)}, s32[16]{0:T(128)}, u32[]{:S(2)}) copy-start(s32[16]{0:T(128)} %block_ref.1) | copy-start | bytes 196
  0.0 9.2 %copy-start.3 = (s32[8]{0:T(128)S(1)}, s32[8]{0:T(128)}, u32[]{:S(2)}) copy-start(s32[8]{0:T(128)} %order_ref.1) | copy-start | bytes 100
  1.9 14.7 %all-to-all-start = ((bf16[32,1,8,128]{3,2,1,0:T(8,128)(2,1)}), bf16[32,1,8,128]{3,2,1,0:T(8,128)(2,1)S(1)}, u32[]{:S(2)}, u32[]{:S(2)}) async-start(bf16[32,1,8,128]{3,2,1,0:T(8,128)(2,1)} %partial_latents.1), calls=%async_computation | async-start | bytes 131072 | tf_op jit(solution)/shard_map/all_to_all | solution.py:323

commit v7 on v6

--- a/solution.py
+++ b/solution.py
@@ -28,26 +28,50 @@
 
 
 def latent_kernel(
-    frame_dev, hidden_hbm, weight_hbm, out_ref, hidden_ref, weight_ref, padded_ref, sems
+    frame_dev,
+    hidden_hbm,
+    weight_hbm,
+    out_hbm,
+    hidden_ref,
+    weight_ref,
+    padded_ref,
+    out_ref,
+    in_sems,
+    out_sems,
 ):
-    copies = [
-        pltpu.make_async_copy(hidden_hbm, hidden_ref, sems.at[0]),
-        pltpu.make_async_copy(weight_hbm, weight_ref, sems.at[1]),
-    ]
-    for copy in copies:
-        copy.start()
     slots, frames, depth = hidden_ref.shape
     everyone, _, window, channels = out_ref.shape
     seqs = frames // frame_dev
+    arrivals = [pltpu.make_async_copy(hidden_hbm, hidden_ref, in_sems.at[0])]
+    for index, at in enumerate(range(0, depth, LANES)):
+        piece = pl.ds(at, LANES)
+        arrivals.append(
+            pltpu.make_async_copy(
+                weight_hbm.at[piece], weight_ref.at[piece], in_sems.at[index + 1]
+            )
+        )
+    for copy in arrivals:
+        copy.start()
     padded_ref[...] = jnp.zeros_like(padded_ref)
-    for copy in copies:
+    for copy in arrivals:
         copy.wait()
     for slot in range(slots):
         padded_ref[slot, REACH : REACH + frames] = dot(hidden_ref[slot], weight_ref[...])
-    for to in range(seqs):
-        piece = padded_ref[:, to * frame_dev : to * frame_dev + window]
-        for at in range(to, everyone, seqs):
-            out_ref[at] = piece.astype(out_ref.dtype)
+    pieces = [
+        padded_ref[:, to * frame_dev : to * frame_dev + window].astype(out_ref.dtype)
+        for to in range(seqs)
+    ]
+    leaving = []
+    for index, first in enumerate(range(0, everyone, seqs)):
+        for to in range(seqs):
+            out_ref[first + to] = pieces[to]
+        part = pl.ds(first, seqs)
+        leaving.append(
+            pltpu.make_async_copy(out_ref.at[part], out_hbm.at[part], out_sems.at[index])
+        )
+        leaving[-1].start()
+    for copy in leaving:
+        copy.wait()
 
 
 def weights_kernel(
@@ -65,14 +89,14 @@
     gram_ref,
     cross_ref,
     level_ref,
+    natural_cross_ref,
+    natural_level_ref,
     pos_mine_ref,
     select_ref,
     select_mine_ref,
     bias_ref,
     first_ref,
     natural_ref,
-    natural_cross_ref,
-    natural_level_ref,
     pos_all_ref,
     weight_ref,
     sems,
@@ -180,11 +204,13 @@
             keep(scaled_ref.at[index], both[:channels])
             natural_ref[index] = both[channels:]
 
+    offset_ref[0] = natural_ref[0]
+
     def place(slot):
         to, at = pl.ds(slot, 1), pl.ds(order_ref[slot], 1)
         cross_ref[to, :] = natural_cross_ref[at, :]
         level_ref[to, :] = natural_level_ref[at, :]
-        for index in range(3):
+        for index in range(1, 3):
             offset_ref[index, to, :] = natural_ref[index, at, :]
 
     if patches <= 16:
@@ -203,6 +229,8 @@
     gram_ref,
     cross_ref,
     level_ref,
+    natural_cross_ref,
+    natural_level_ref,
     pos_mine_ref,
     select_ref,
     select_mine_ref,
@@ -228,20 +256,33 @@
     for other in range(1, group):
         total = total + partial_ref[other * seqs : (other + 1) * seqs].astype(jnp.float32)
     latents = total.reshape(rows, channels).astype(jnp.bfloat16)
-    twice = jnp.concatenate([latents, latents], axis=1)
-    slope = dot(twice, gram_ref[...]).reshape(patches, window, channels)
-    slope = slope + cross_ref[...][:, None]
-    squares = slope * latents.astype(jnp.float32).reshape(patches, window, channels)
-    squares = (squares + level_ref[...][:, None]).reshape(rows, channels)
-    mean = jnp.maximum(jnp.sum(squares, axis=-1, keepdims=True), 0.0) / model
-    scale = lax.rsqrt(mean + 1e-06)
+    own = dot(select_ref[...], latents).astype(jnp.bfloat16)
+
+    def apply(part, table):
+        return dot(jnp.concatenate([part, part], axis=1), table)
+
+    def by_row(table):
+        wide = jnp.broadcast_to(table[:, None], (patches, window, table.shape[1]))
+        return wide.reshape(rows, table.shape[1])
+
+    def by_patch(table):
+        return jnp.concatenate([table] * (group * share // patches), axis=0)
+
+    def scale_of(part, cross, level):
+        slope = apply(part, gram_ref[...]) + cross
+        squares = slope * part.astype(jnp.float32) + level
+        mean = jnp.maximum(jnp.sum(squares, axis=-1, keepdims=True), 0.0) / model
+        return lax.rsqrt(mean + 1e-06)
+
+    scale = scale_of(latents, by_row(cross_ref[...]), by_row(level_ref[...]))
+    own_scale = scale_of(own, by_patch(natural_cross_ref[...]), by_patch(natural_level_ref[...]))
+    own_scale = own_scale * (HS**-0.5)
 
     def project(index):
-        flat = dot(twice, scaled_ref[index]).reshape(patches, window, cols)
-        flat = (flat + offset_ref[index][:, None]).reshape(rows, cols)
+        flat = apply(latents, scaled_ref[index]) + by_row(offset_ref[index])
         return (flat * scale).astype(jnp.bfloat16)
 
-    query = dot(select_ref[...], project(0)).astype(jnp.bfloat16)
+    query = (apply(own, scaled_ref[0]) + by_patch(offset_ref[0])).astype(jnp.bfloat16)
     key, value = project(1), project(2)
     bias = bias_ref[...]
     heads = []
@@ -250,7 +291,7 @@
         scores = lax.dot_general(
             query[:, at], key[:, at], (((1,), (1,)), ((), ())), preferred_element_type=jnp.float32
         )
-        scores = scores * (HS**-0.5) + bias
+        scores = scores * own_scale + bias
         expo = jnp.exp(scores - jnp.max(scores, axis=-1, keepdims=True))
         probs = (expo / jnp.sum(expo, axis=-1, keepdims=True)).astype(jnp.bfloat16)
         heads.append(dot(probs, value[:, at]).astype(jnp.bfloat16))
@@ -302,14 +343,16 @@
 
     windows = pl.pallas_call(
         functools.partial(latent_kernel, frame_dev),
-        out_shape=pltpu.VMEM((group * seqs, slots, window, channels), bf16),
+        out_shape=array((group * seqs, slots, window, channels), bf16),
         in_specs=[HBM] * 2,
-        out_specs=VMEM,
+        out_specs=HBM,
         scratch_shapes=[
             pltpu.VMEM((slots, frames, depth), bf16),
             pltpu.VMEM((depth, channels), bf16),
             pltpu.VMEM((slots, frames + 2 * REACH, channels), f32),
-            pltpu.SemaphoreType.DMA((2,)),
+            pltpu.VMEM((group * seqs, slots, window, channels), bf16),
+            pltpu.SemaphoreType.DMA((1 + depth // LANES,)),
+            pltpu.SemaphoreType.DMA((group,)),
         ],
         compiler_params=pltpu.CompilerParams(vmem_limit_bytes=12 * MIB),
         cost_estimate=pl.CostEstimate(
@@ -336,6 +379,8 @@
             array((2 * channels, channels), bf16),
             array((patches, channels), f32),
             array((patches, channels), f32),
+            array((patches, channels), f32),
+            array((patches, channels), f32),
             array((share, model), f32),
             array((own_rows, rows), bf16),
             array((share, rows), bf16),
@@ -343,11 +388,9 @@
             array((cols // 2, model), bf16),
         ),
         in_specs=[SMEM] * 2 + [VMEM] * 3 + [HBM] * 2,
-        out_specs=(VMEM,) * 10,
+        out_specs=(VMEM,) * 12,
         scratch_shapes=[
             pltpu.VMEM((3, patches, cols), f32),
-            pltpu.VMEM((patches, channels), f32),
-            pltpu.VMEM((patches, channels), f32),
             pltpu.VMEM((patches, model), f32),
             pltpu.VMEM((3, model, cols), bf16),
             pltpu.SemaphoreType.DMA((3 * (model // min(model, DEPTH)),)),
@@ -373,7 +416,7 @@
     mixed, mine = pl.pallas_call(
         attend_kernel,
         out_shape=(array((group, share, model), bf16), array((share, model), f32)),
-        in_specs=[VMEM] * 12 + [HBM],
+        in_specs=[VMEM] * 14 + [HBM],
         out_specs=(VMEM, VMEM),
         scratch_shapes=[
             pltpu.VMEM((cols - cols // 2, model), bf16),

time: 26.3 us -> 26.2 us (level)
  no operation moved by 1% of the time
where the time goes in v7:
time: 26.2 us; the launch traced here: 26 us
  Pallas kernels  10.3 us (39%)
  starting transfers between devices  7.32 us (28%)
  blocking collectives  6.67 us (25%)
  waiting for transfers between devices  1.61 us (6%)
    all_to_all x1, starting transfers between devices, on_device(): lax.all_to_all(windows, SCATTERED, split_axis=0, concat_axis=0, tiled=True)  7.32 us
    all_to_all x1, blocking collectives, on_device(): lax.all_to_all(mixed, GROUP, split_axis=0, concat_axis=0, tiled=True)  6.67 us
    pallas_call x1, Pallas kernels, on_device(): pl.pallas_call(functools.partial(weights_kernel, frame_dev, window), out_...  5.68 us
    pallas_call x1, Pallas kernels, on_device(): pl.pallas_call(attend_kernel, out_shape=(array((group, share, model), bf1...  2.15 us
    pallas_call x1, Pallas kernels, on_device(): pl.pallas_call(functools.partial(latent_kernel, frame_dev), out_shape=arr...  1.81 us
    all_to_all x1, waiting for transfers between devices, on_device(): lax.all_to_all(windows, SCATTERED, split_axis=0, concat_axis=0, tiled=True)  1.61 us
    pallas_call x1, Pallas kernels, on_device(): pl.pallas_call(sum_kernel, out_shape=array((share, model), bf16), in_spec...  0.63 us
  transfers between devices with their start and end apart: 1, of which 1 were waited for; matrix products, arithmetic and copies ran while one was open for 0% of the time, Pallas kernels for 22%

profile of v7, /device:TPU:0, one launch (start us, length us, event | category | flops | bytes accessed | tf_op | source)
XLA Modules:
  0.0 26.0 jit_solution(6901936620720872303)
XLA Ops:
  0.0 0.0 copy-start
  0.0 0.0 copy-start.2
  0.0 0.0 copy-start.1
  0.0 0.0 copy-start.4
  0.0 0.0 copy-start.3
  0.0 1.8 %partial_latents.1 = bf16[32,1,8,128]{3,2,1,0:T(8,128)(2,1)} custom-call(bf16[1,16,768]{2,1,0:T(8,128)(2,1)} %hidden_hbm.1, bf16[768,128]{1,0:T(8,128)(2,1)} %weight_hbm.1), custom_call_target="tpu_custom_call" | custom-call | flops 20000000000 | bytes 40000000 | tf_op jit(solution)/shard_map/partial_latents/pallas_call | solution.py:344
  1.8 7.3 %all-to-all-start = ((bf16[32,1,8,128]{3,2,1,0:T(8,128)(2,1)}), bf16[32,1,8,128]{3,2,1,0:T(8,128)(2,1)S(1)}, u32[]{:S(2)}, u32[]{:S(2)}) async-start(bf16[32,1,8,128]{3,2,1,0:T(8,128)(2,1)} %partial_latents.1), calls=%async_computation | async-start | bytes 131072 | tf_op jit(solution)/shard_map/all_to_all | solution.py:366
  9.2 0.0 copy-done
  9.2 0.0 copy-done.2
  9.2 0.0 copy-done.1
  9.2 0.0 copy-done.4
  9.2 0.0 copy-done.3
  9.2 5.7 %weight_products.1 = (bf16[3,256,512]{2,1,0:T(8,128)(2,1)S(1)}, f32[3,8,512]{2,1,0:T(8,128)S(1)}, bf16[256,128]{1,0:T(8,128)(2,1)S(1)}, f32[8,128]{1,0:T(8,128)S...) custom-call(s32[8]{0:T(128)S(1)} %copy-done.3, ...), custom_call_target="tpu_custom_call" | custom-call | flops 1283457024 | bytes 9437184 | tf_op jit(solution)/shard_map/weight_products/pallas_call | solution.py:374
  14.9 1.6 %all-to-all-done.partial_ref = bf16[32,1,8,128]{3,2,1,0:T(8,128)(2,1)S(1)} async-done(((bf16[32,1,8,128]{3,2,1,0:T(8,128)(2,1)}), bf16[32,1,8,128]{3,2,1,0:T(8,128)(2,1)S(1)}, u32[]{:S(2)}, u32[]{:S(2)}) %all-to-all-start) | async-done | bytes 65568 | tf_op jit(solution)/shard_map/all_to_all | solution.py:366
  16.5 2.1 %attend.1 = (bf16[4,4,3072]{2,1,0:T(4,128)(2,1)S(1)}, f32[4,3072]{1,0:T(4,128)S(1)}) custom-call(bf16[32,1,8,128]{3,2,1,0:T(8,128)(2,1)S(1)} %all-to-all-done.partial_ref, bf16[128,3072]{1,0:T(8,128)(2,1)S(1)} %copy-done, bf16[3,256,512]{2,1,0:T(8,128)(2,1)S(1)} %get-tuple-element.19.scaled_ref, f32[3,8,512]{2,1,0:T(8,128)S(1)} %get-tuple-element.20.offset_ref, ...), custom_call_target="tpu_custom_call" | custom-call | tf_op jit(solution)/shard_map/attend/pallas_call | solution.py:416
  18.7 6.7 %all_to_all.10.mixed_ref = bf16[4,4,3072]{2,1,0:T(4,128)(2,1)S(1)} all-to-all(bf16[4,4,3072]{2,1,0:T(4,128)(2,1)S(1)} %get-tuple-element.32), channel_id=1, replica_groups=mesh['seq'=8,'mp'=2,'role'=2] {'mp','role'}, dimensions={0} | all-to-all | bytes 196608 | tf_op jit(solution)/shard_map/all_to_all | solution.py:433
  25.3 0.6 %final_sum.1 = bf16[4,3072]{1,0:T(4,128)(2,1)} custom-call(f32[4,3072]{1,0:T(4,128)S(1)} %get-tuple-element.31.mine_ref, bf16[4,4,3072]{2,1,0:T(4,128)(2,1)S(1)} %all_to_all.10.mixed_ref), custom_call_target="tpu_custom_call" | custom-call | tf_op jit(solution)/shard_map/final_sum/pallas_call | solution.py:434
Async XLA Ops:
  0.0 9.2 %copy-start = (bf16[128,3072]{1,0:T(8,128)(2,1)S(1)}, bf16[128,3072]{1,0:T(8,128)(2,1)}, u32[]{:S(2)}) copy-start(bf16[128,3072]{1,0:T(8,128)(2,1)} %embed_ref.3) | copy-start | bytes 2359300
  0.0 9.2 %copy-start.2 = (bf16[3072]{0:T(1024)(128)(2,1)S(1)}, bf16[3072]{0:T(1024)(128)(2,1)}, u32[]{:S(2)}) copy-start(bf16[3072]{0:T(1024)(128)(2,1)} %param.15) | copy-start | bytes 18436
  0.0 9.2 %copy-start.1 = (bf16[8,3072]{1,0:T(8,128)(2,1)S(1)}, bf16[8,3072]{1,0:T(8,128)(2,1)}, u32[]{:S(2)}) copy-start(bf16[8,3072]{1,0:T(8,128)(2,1)} %pos_ref.1) | copy-start | bytes 147460
  0.0 9.2 %copy-start.4 = (s32[16]{0:T(128)S(1)}, s32[16]{0:T(128)}, u32[]{:S(2)}) copy-start(s32[16]{0:T(128)} %block_ref.1) | copy-start | bytes 196
  0.0 9.2 %copy-start.3 = (s32[8]{0:T(128)S(1)}, s32[8]{0:T(128)}, u32[]{:S(2)}) copy-start(s32[8]{0:T(128)} %order_ref.1) | copy-start | bytes 100
  1.8 14.7 %all-to-all-start = ((bf16[32,1,8,128]{3,2,1,0:T(8,128)(2,1)}), bf16[32,1,8,128]{3,2,1,0:T(8,128)(2,1)S(1)}, u32[]{:S(2)}, u32[]{:S(2)}) async-start(bf16[32,1,8,128]{3,2,1,0:T(8,128)(2,1)} %partial_latents.1), calls=%async_computation | async-start | bytes 131072 | tf_op jit(solution)/shard_map/all_to_all | solution.py:366

commit v8 on v7

--- a/solution.py
+++ b/solution.py
@@ -237,16 +237,18 @@
     bias_ref,
     first_ref,
     out_weight_hbm,
-    mixed_ref,
+    keep_ref,
     mine_ref,
-    second_ref,
-    sem,
+    *rest,
 ):
+    *send_refs, second_ref, sem = rest
     half = first_ref.shape[0]
     arrival = pltpu.make_async_copy(out_weight_hbm.at[pl.ds(half, half)], second_ref, sem)
     arrival.start()
     everyone, slots, window, channels = partial_ref.shape
-    group, share, model = mixed_ref.shape
+    mps, share, model = keep_ref.shape
+    roles = 1 + len(send_refs)
+    group = mps * roles
     seqs = everyone // group
     patches = seqs * slots
     rows = patches * window
@@ -299,19 +301,55 @@
     mine_ref[...] = dot(mine, embed_ref[...]) + pos_mine_ref[...]
     heads = jnp.concatenate(heads, axis=1)
     arrival.wait()
+    role = lax.axis_index("role")
     for at in range(0, model, STRIP):
         here = slice(at, at + STRIP)
         mixed = dot(heads[:, :half], first_ref[:, here]) + dot(heads[:, half:], second_ref[:, here])
-        mixed = mixed.astype(jnp.bfloat16)
-        for other in range(group):
-            mixed_ref[other, :, here] = mixed[other * share : (other + 1) * share]
-
-
-def sum_kernel(mine_ref, mixed_ref, out_ref):
-    total = mine_ref[...]
-    for member in range(mixed_ref.shape[0]):
-        total = total + mixed_ref[member].astype(jnp.float32)
+        for mp in range(mps):
+            parts = [
+                mixed[index * share : (index + 1) * share]
+                for index in range(mp * roles, (mp + 1) * roles)
+            ]
+
+            def of_role(step):
+                wanted, found = (role + step) % roles, parts[0]
+                for index in range(1, roles):
+                    found = jnp.where(wanted == index, parts[index], found)
+                return found
+
+            keep_ref[mp, :, here] = of_role(0)
+            for step, send_ref in enumerate(send_refs):
+                send_ref[mp, :, here] = of_role(step + 1).astype(jnp.bfloat16)
+
+
+def add_kernel(roles, mine_ref, keep_ref, *refs):
+    others, (total_ref, *send_refs) = refs[: roles - 1], refs[roles - 1 :]
+    mps = keep_ref.shape[0]
+    mp = lax.axis_index("mp")
+
+    def total(step):
+        at = (mp + step) % mps
+        rows = keep_ref[at]
+        for other in others:
+            rows = rows + other[at].astype(jnp.float32)
+        return rows
+
+    total_ref[...] = mine_ref[...] + total(0)
+    for step, send_ref in enumerate(send_refs):
+        send_ref[...] = total(step + 1).astype(jnp.bfloat16)
+
+
+def sum_kernel(total_ref, *refs):
+    *others, out_ref = refs
+    total = total_ref[...]
+    for other in others:
+        total = total + other[...].astype(jnp.float32)
     out_ref[...] = total.astype(jnp.bfloat16)
+
+
+def around(block, axis, step):
+    size = lax.axis_size(axis)
+    return lax.ppermute(block, axis, [(i, (i + step) % size) for i in range(size)])
 
 
 def on_device(
@@ -331,6 +369,7 @@
     out_weight = pltpu.with_memory_space_constraint(out_weight, pltpu.HBM)
     seqs = lax.axis_size("seq")
     group = lax.axis_size(GROUP)
+    mps, roles = lax.axis_size("mp"), lax.axis_size("role")
     patches = seqs * slots
     frame_dev = frames // seqs
     window = frame_dev + 2 * REACH
@@ -413,11 +452,15 @@
         out_weight,
     )
 
-    mixed, mine = pl.pallas_call(
+    keep, mine, *sent = pl.pallas_call(
         attend_kernel,
-        out_shape=(array((group, share, model), bf16), array((share, model), f32)),
+        out_shape=(
+            array((mps, share, model), f32),
+            array((share, model), f32),
+            *[array((mps, share, model), bf16)] * (roles - 1),
+        ),
         in_specs=[VMEM] * 14 + [HBM],
-        out_specs=(VMEM, VMEM),
+        out_specs=(VMEM,) * (1 + roles),
         scratch_shapes=[
             pltpu.VMEM((cols - cols // 2, model), bf16),
             pltpu.SemaphoreType.DMA(()),
@@ -430,15 +473,25 @@
         *products,
         out_weight,
     )
-    mixed = lax.all_to_all(mixed, GROUP, split_axis=0, concat_axis=0, tiled=True)
+    small = pltpu.CompilerParams(vmem_limit_bytes=8 * MIB)
+    sent = [around(block, "role", step + 1) for step, block in enumerate(sent)]
+    total, *sent = pl.pallas_call(
+        functools.partial(add_kernel, roles),
+        out_shape=(array((share, model), f32), *[array((share, model), bf16)] * (mps - 1)),
+        in_specs=[VMEM] * (1 + roles),
+        out_specs=(VMEM,) * mps,
+        compiler_params=small,
+        name="sum_over_role",
+    )(mine, keep, *sent)
+    sent = [around(block, "mp", step + 1) for step, block in enumerate(sent)]
     return pl.pallas_call(
         sum_kernel,
         out_shape=array((share, model), bf16),
-        in_specs=[VMEM] * 2,
+        in_specs=[VMEM] * mps,
         out_specs=VMEM,
-        compiler_params=pltpu.CompilerParams(vmem_limit_bytes=8 * MIB),
-        name="final_sum",
-    )(mine, mixed)
+        compiler_params=small,
+        name="sum_over_mp",
+    )(total, *sent)
 
 
 def solution(mesh):

time: 26.2 us -> 24.7 us (0.943)
  blocking collectives: 6.67 us -> 0 us
  waiting for transfers between devices: 1.61 us -> 6.02 us
  starting transfers between devices: 7.32 us -> 8.08 us
    all_to_all x1 -> x0, blocking collectives: 6.67 us -> none  [on_device(): lax.all_to_all(mixed, GROUP, split_axis=0, concat_axis=0, tiled=True)]
    ppermute x0 -> x2, waiting for transfers between devices: none -> 4.41 us  [around(): lax.ppermute(block, axis, [(i, (i + step) % size) for i in range(size)])]
    ppermute x0 -> x2, starting transfers between devices: none -> 0.77 us  [around(): lax.ppermute(block, axis, [(i, (i + step) % size) for i in range(size)])]
    pallas_call x1 -> x2, Pallas kernels: 2.15 us -> 2.17 us  [the longest x1 2.14 us: on_device(): pl.pallas_call(attend_kernel, out_shape=(array((mps, share, model), f32),...]
  transfers between devices with their start and end apart: 1 -> 3, of which waited for: 1 -> 3; matrix products, arithmetic and copies ran while one was open for 0% -> 0% of each run, Pallas kernels for 22% -> 23%
where the time goes in v8:
time: 24.7 us; the launch traced here: 24.5 us
  Pallas kernels  10.3 us (42%)
  starting transfers between devices  8.08 us (33%)
  waiting for transfers between devices  6.02 us (24%)
    all_to_all x1, starting transfers between devices, on_device(): lax.all_to_all(windows, SCATTERED, split_axis=0, concat_axis=0, tiled=True)  7.32 us
    pallas_call x1, Pallas kernels, on_device(): pl.pallas_call(functools.partial(weights_kernel, frame_dev, window), out_...  5.68 us
    ppermute x2, waiting for transfers between devices, around(): lax.ppermute(block, axis, [(i, (i + step) % size) for i in range(size)])  4.41 us
    pallas_call x1, Pallas kernels, on_device(): pl.pallas_call(attend_kernel, out_shape=(array((mps, share, model), f32),...  2.14 us
    pallas_call x1, Pallas kernels, on_device(): pl.pallas_call(functools.partial(latent_kernel, frame_dev), out_shape=arr...  1.8 us
    all_to_all x1, waiting for transfers between devices, on_device(): lax.all_to_all(windows, SCATTERED, split_axis=0, concat_axis=0, tiled=True)  1.61 us
    ppermute x2, starting transfers between devices, around(): lax.ppermute(block, axis, [(i, (i + step) % size) for i in range(size)])  0.77 us
    pallas_call x1, Pallas kernels, on_device(): pl.pallas_call(sum_kernel, out_shape=array((share, model), bf16), in_spec...  0.62 us
  transfers between devices with their start and end apart: 3, of which 3 were waited for; matrix products, arithmetic and copies ran while one was open for 0% of the time, Pallas kernels for 23%

profile of v8, /device:TPU:0, one launch (start us, length us, event | category | flops | bytes accessed | tf_op | source)
XLA Modules:
  0.0 24.5 jit_solution(8364037754718793176)
XLA Ops:
  0.0 0.0 copy-start
  0.0 0.0 copy-start.2
  0.0 0.0 copy-start.1
  0.0 0.0 copy-start.4
  0.0 0.0 copy-start.3
  0.0 1.8 %partial_latents.1 = bf16[32,1,8,128]{3,2,1,0:T(8,128)(2,1)} custom-call(bf16[1,16,768]{2,1,0:T(8,128)(2,1)} %hidden_hbm.1, bf16[768,128]{1,0:T(8,128)(2,1)} %weight_hbm.1), custom_call_target="tpu_custom_call" | custom-call | flops 20000000000 | bytes 40000000 | tf_op jit(solution)/shard_map/partial_latents/pallas_call | solution.py:383
  1.8 7.3 %all-to-all-start = ((bf16[32,1,8,128]{3,2,1,0:T(8,128)(2,1)}), bf16[32,1,8,128]{3,2,1,0:T(8,128)(2,1)S(1)}, u32[]{:S(2)}, u32[]{:S(2)}) async-start(bf16[32,1,8,128]{3,2,1,0:T(8,128)(2,1)} %partial_latents.1), calls=%async_computation | async-start | bytes 131072 | tf_op jit(solution)/shard_map/all_to_all | solution.py:405
  9.1 0.0 copy-done
  9.2 0.0 copy-done.2
  9.2 0.0 copy-done.1
  9.2 0.0 copy-done.4
  9.2 0.0 copy-done.3
  9.2 5.7 %weight_products.1 = (bf16[3,256,512]{2,1,0:T(8,128)(2,1)S(1)}, f32[3,8,512]{2,1,0:T(8,128)S(1)}, bf16[256,128]{1,0:T(8,128)(2,1)S(1)}, f32[8,128]{1,0:T(8,128)S...) custom-call(s32[8]{0:T(128)S(1)} %copy-done.3, ...), custom_call_target="tpu_custom_call" | custom-call | flops 1283457024 | bytes 9437184 | tf_op jit(solution)/shard_map/weight_products/pallas_call | solution.py:413
  14.9 1.6 %all-to-all-done.partial_ref = bf16[32,1,8,128]{3,2,1,0:T(8,128)(2,1)S(1)} async-done(((bf16[32,1,8,128]{3,2,1,0:T(8,128)(2,1)}), bf16[32,1,8,128]{3,2,1,0:T(8,128)(2,1)S(1)}, u32[]{:S(2)}, u32[]{:S(2)}) %all-to-all-start) | async-done | bytes 65568 | tf_op jit(solution)/shard_map/all_to_all | solution.py:405
  16.5 2.1 %attend.1 = (f32[2,4,3072]{2,1,0:T(4,128)S(1)}, f32[4,3072]{1,0:T(4,128)S(1)}, bf16[2,4,3072]{2,1,0:T(4,128)(2,1)S(1)}) custom-call(bf16[32,1,8,128]{3,2,1,0:T(8,128)(2,1)S(1)} %all-to-all-done.partial_ref, bf16[128,3072]{1,0:T(8,128)(2,1)S(1)} %copy-done, bf16[3,256,512]{2,1,0:T(8,128)(2,1)S(1)} %get-tuple-element.22.scaled_ref, ...), custom_call_target="tpu_custom_call" | custom-call | tf_op jit(solution)/shard_map/attend/pallas_call | solution.py:455
  18.6 0.1 collective-permute-start
  18.7 1.2 %collective-permute-done.refs_0_ = bf16[2,4,3072]{2,1,0:T(4,128)(2,1)S(1)} collective-permute-done((bf16[2,4,3072]{2,1,0:T(4,128)(2,1)S(1)}, bf16[2,4,3072]{2,1,0:T(4,128)(2,1)S(1)}, u32[]{:S(2)}, u32[]{:S(2)}) %collective-permute-start) | collective-permute-done | bytes 49184 | tf_op jit(solution)/shard_map/ppermute | solution.py:352
  20.0 0.7 %collective-permute-start.1 = (bf16[4,3072]{1,0:T(4,128)(2,1)S(1)}, bf16[4,3072]{1,0:T(4,128)(2,1)S(1)}, u32[]{:S(2)}, u32[]{:S(2)}) collective-permute-start(bf16[4,3072]{1,0:T(4,128)(2,1)S(1)} %get-tuple-element.38), channel_id=1, source_target_pairs={{0,2},{2,0},{1,3},{3,1},{4,6},{6,4},{5,7},{7,5},{8,10},{10,8},{9,1... | collective-permute-start | bytes 73736 | tf_op jit(solution)/shard_map/ppermute | solution.py:352
  20.7 3.2 %collective-permute-done.1.refs_0_ = bf16[4,3072]{1,0:T(4,128)(2,1)S(1)} collective-permute-done((bf16[4,3072]{1,0:T(4,128)(2,1)S(1)}, bf16[4,3072]{1,0:T(4,128)(2,1)S(1)}, u32[]{:S(2)}, u32[]{:S(2)}) %collective-permute-start.1) | collective-permute-done | bytes 24608 | tf_op jit(solution)/shard_map/ppermute | solution.py:352
  23.9 0.6 %sum_over_mp.1 = bf16[4,3072]{1,0:T(4,128)(2,1)} custom-call(f32[4,3072]{1,0:T(4,128)S(1)} %get-tuple-element.37.total_ref, bf16[4,3072]{1,0:T(4,128)(2,1)S(1)} %collective-permute-done.1.refs_0_), custom_call_target="tpu_custom_call" | custom-call | tf_op jit(solution)/shard_map/sum_over_mp/pallas_call | solution.py:487
  (1 shorter events, 0.0 us)
Async XLA Ops:
  0.0 9.1 %copy-start = (bf16[128,3072]{1,0:T(8,128)(2,1)S(1)}, bf16[128,3072]{1,0:T(8,128)(2,1)}, u32[]{:S(2)}) copy-start(bf16[128,3072]{1,0:T(8,128)(2,1)} %embed_ref.3) | copy-start | bytes 2359300
  0.0 9.2 %copy-start.2 = (bf16[3072]{0:T(1024)(128)(2,1)S(1)}, bf16[3072]{0:T(1024)(128)(2,1)}, u32[]{:S(2)}) copy-start(bf16[3072]{0:T(1024)(128)(2,1)} %param.15) | copy-start | bytes 18436
  0.0 9.2 %copy-start.1 = (bf16[8,3072]{1,0:T(8,128)(2,1)S(1)}, bf16[8,3072]{1,0:T(8,128)(2,1)}, u32[]{:S(2)}) copy-start(bf16[8,3072]{1,0:T(8,128)(2,1)} %pos_ref.1) | copy-start | bytes 147460
  0.0 9.2 %copy-start.4 = (s32[16]{0:T(128)S(1)}, s32[16]{0:T(128)}, u32[]{:S(2)}) copy-start(s32[16]{0:T(128)} %block_ref.1) | copy-start | bytes 196
  0.0 9.2 %copy-start.3 = (s32[8]{0:T(128)S(1)}, s32[8]{0:T(128)}, u32[]{:S(2)}) copy-start(s32[8]{0:T(128)} %order_ref.1) | copy-start | bytes 100
  1.8 14.7 %all-to-all-start = ((bf16[32,1,8,128]{3,2,1,0:T(8,128)(2,1)}), bf16[32,1,8,128]{3,2,1,0:T(8,128)(2,1)S(1)}, u32[]{:S(2)}, u32[]{:S(2)}) async-start(bf16[32,1,8,128]{3,2,1,0:T(8,128)(2,1)} %partial_latents.1), calls=%async_computation | async-start | bytes 131072 | tf_op jit(solution)/shard_map/all_to_all | solution.py:405
  18.6 1.3 %collective-permute-start = (bf16[2,4,3072]{2,1,0:T(4,128)(2,1)S(1)}, bf16[2,4,3072]{2,1,0:T(4,128)(2,1)S(1)}, u32[]{:S(2)}, u32[]{:S(2)}) collective-permute-start(bf16[2,4,3072]{2,1,0:T(4,128)(2,1)S(1)} %get-tuple-element.36), channel_id=1, source_target_pairs={{0,1},{1,0},{2,3},{3,2},{4,5},{5,4},{6,7},{7,6},{8,9},{9,8},{10,11... | collective-permute-start | bytes 147464 | tf_op jit(solution)/shard_map/ppermute | solution.py:352
  20.0 3.9 %collective-permute-start.1 = (bf16[4,3072]{1,0:T(4,128)(2,1)S(1)}, bf16[4,3072]{1,0:T(4,128)(2,1)S(1)}, u32[]{:S(2)}, u32[]{:S(2)}) collective-permute-start(bf16[4,3072]{1,0:T(4,128)(2,1)S(1)} %get-tuple-element.38), channel_id=1, source_target_pairs={{0,2},{2,0},{1,3},{3,1},{4,6},{6,4},{5,7},{7,5},{8,10},{10,8},{9,1... | collective-permute-start | bytes 73736 | tf_op jit(solution)/shard_map/ppermute | solution.py:352

commit v9 on v7

--- a/solution.py
+++ b/solution.py
@@ -77,6 +77,8 @@
 def weights_kernel(
     frame_dev,
     window,
+    mps,
+    roles,
     order_ref,
     block_ref,
     embed_ref,
@@ -89,14 +91,16 @@
     gram_ref,
     cross_ref,
     level_ref,
-    natural_cross_ref,
-    natural_level_ref,
+    own_offset_ref,
+    own_cross_ref,
+    own_level_ref,
     pos_mine_ref,
     select_ref,
-    select_mine_ref,
     bias_ref,
     first_ref,
     natural_ref,
+    natural_cross_ref,
+    natural_level_ref,
     pos_all_ref,
     weight_ref,
     sems,
@@ -106,9 +110,14 @@
     patches = pos_ref.shape[0]
     frames = block_ref.shape[0]
     own_rows, rows = bias_ref.shape
-    share = select_mine_ref.shape[0]
+    share = pos_mine_ref.shape[0]
     device = lax.axis_index("seq")
-    member = lax.axis_index(GROUP)
+    mp, role = lax.axis_index("mp"), lax.axis_index("role")
+    firsts = [
+        (((mp + along) % mps) * roles + (role + across) % roles) * share
+        for along in range(mps)
+        for across in range(roles)
+    ]
 
     deep = min(model, DEPTH)
     parts = [(index, at) for index in range(3) for at in range(0, model, deep)]
@@ -140,23 +149,13 @@
     else:
         column_patch = lax.fori_loop(0, patches, patch_at, column_patch)
 
-    def select(count, first):
-        row = lax.broadcasted_iota(jnp.int32, (count, rows), 0) + first
-        hit = jnp.logical_and(
-            column_patch == row % patches, column_frame == row // patches + REACH
-        )
-        return jnp.where(hit, 1.0, 0.0).astype(jnp.bfloat16)
-
-    select_ref[...] = select(own_rows, 0)
-    select_mine_ref[...] = select(share, member * share)
-    for frame in range(frame_dev * patches // share):
-        row = frame * share
-
-        @pl.when(member == frame)
-        def _():
-            for at in range(share):
-                mine = (row + at) % patches
-                pos_mine_ref[at : at + 1, :] = pos_all_ref[mine : mine + 1, :]
+    row = lax.broadcasted_iota(jnp.int32, (own_rows, rows), 0)
+    natural = jnp.zeros((own_rows, rows), jnp.int32)
+    for index, first_row in enumerate(firsts):
+        natural = jnp.where(row // share == index, first_row + row % share, natural)
+    row_patch, row_frame = natural % patches, natural // patches
+    hit = jnp.logical_and(column_patch == row_patch, column_frame == row_frame + REACH)
+    select_ref[...] = jnp.where(hit, 1.0, 0.0).astype(jnp.bfloat16)
 
     def block_of(frame):
         inside = jnp.logical_and(frame >= 0, frame < frames)
@@ -166,7 +165,6 @@
     for frame in range(window):
         found = block_of(device * frame_dev - REACH + frame)
         column_block = jnp.where(column_frame == frame, found, column_block)
-    row_frame = lax.broadcasted_iota(jnp.int32, (own_rows, rows), 0) // patches
     row_block = jnp.full((own_rows, rows), -2, jnp.int32)
     for frame in range(frame_dev):
         row_block = jnp.where(row_frame == frame, block_of(device * frame_dev + frame), row_block)
@@ -204,49 +202,61 @@
             keep(scaled_ref.at[index], both[:channels])
             natural_ref[index] = both[channels:]
 
-    offset_ref[0] = natural_ref[0]
-
     def place(slot):
         to, at = pl.ds(slot, 1), pl.ds(order_ref[slot], 1)
         cross_ref[to, :] = natural_cross_ref[at, :]
         level_ref[to, :] = natural_level_ref[at, :]
         for index in range(1, 3):
-            offset_ref[index, to, :] = natural_ref[index, at, :]
+            offset_ref[index - 1, to, :] = natural_ref[index, at, :]
+
+    def place_own(index, within):
+        to = pl.ds(index * share + within, 1)
+        at = pl.ds((firsts[index] + within) % patches, 1)
+        own_offset_ref[to, :] = natural_ref[0, at, :]
+        own_cross_ref[to, :] = natural_cross_ref[at, :]
+        own_level_ref[to, :] = natural_level_ref[at, :]
+        if index == 0:
+            pos_mine_ref[to, :] = pos_all_ref[at, :]
 
     if patches <= 16:
         for slot in range(patches):
             place(slot)
     else:
         pl.loop(0, patches)(place)
+    for index in range(len(firsts)):
+        if share <= 16:
+            for within in range(share):
+                place_own(index, within)
+        else:
+            pl.loop(0, share)(functools.partial(place_own, index))
     first.wait()
 
 
 def attend_kernel(
     partial_ref,
-    embed_ref,
     scaled_ref,
     offset_ref,
     gram_ref,
     cross_ref,
     level_ref,
-    natural_cross_ref,
-    natural_level_ref,
-    pos_mine_ref,
+    own_offset_ref,
+    own_cross_ref,
+    own_level_ref,
     select_ref,
-    select_mine_ref,
     bias_ref,
     first_ref,
     out_weight_hbm,
-    mixed_ref,
     mine_ref,
-    second_ref,
-    sem,
+    keep_ref,
+    *rest,
 ):
+    *send_refs, second_ref, sem = rest
     half = first_ref.shape[0]
     arrival = pltpu.make_async_copy(out_weight_hbm.at[pl.ds(half, half)], second_ref, sem)
     arrival.start()
     everyone, slots, window, channels = partial_ref.shape
-    group, share, model = mixed_ref.shape
+    share, model = keep_ref.shape
+    group = 1 + len(send_refs)
     seqs = everyone // group
     patches = seqs * slots
     rows = patches * window
@@ -257,6 +267,7 @@
         total = total + partial_ref[other * seqs : (other + 1) * seqs].astype(jnp.float32)
     latents = total.reshape(rows, channels).astype(jnp.bfloat16)
     own = dot(select_ref[...], latents).astype(jnp.bfloat16)
+    mine_ref[...] = own[:share]
 
     def apply(part, table):
         return dot(jnp.concatenate([part, part], axis=1), table)
@@ -264,9 +275,6 @@
     def by_row(table):
         wide = jnp.broadcast_to(table[:, None], (patches, window, table.shape[1]))
         return wide.reshape(rows, table.shape[1])
-
-    def by_patch(table):
-        return jnp.concatenate([table] * (group * share // patches), axis=0)
 
     def scale_of(part, cross, level):
         slope = apply(part, gram_ref[...]) + cross
@@ -275,14 +283,13 @@
         return lax.rsqrt(mean + 1e-06)
 
     scale = scale_of(latents, by_row(cross_ref[...]), by_row(level_ref[...]))
-    own_scale = scale_of(own, by_patch(natural_cross_ref[...]), by_patch(natural_level_ref[...]))
-    own_scale = own_scale * (HS**-0.5)
+    own_scale = scale_of(own, own_cross_ref[...], own_level_ref[...]) * (HS**-0.5)
 
     def project(index):
-        flat = apply(latents, scaled_ref[index]) + by_row(offset_ref[index])
+        flat = apply(latents, scaled_ref[index]) + by_row(offset_ref[index - 1])
         return (flat * scale).astype(jnp.bfloat16)
 
-    query = (apply(own, scaled_ref[0]) + by_patch(offset_ref[0])).astype(jnp.bfloat16)
+    query = (apply(own, scaled_ref[0]) + own_offset_ref[...]).astype(jnp.bfloat16)
     key, value = project(1), project(2)
     bias = bias_ref[...]
     heads = []
@@ -295,23 +302,37 @@
         expo = jnp.exp(scores - jnp.max(scores, axis=-1, keepdims=True))
         probs = (expo / jnp.sum(expo, axis=-1, keepdims=True)).astype(jnp.bfloat16)
         heads.append(dot(probs, value[:, at]).astype(jnp.bfloat16))
-    mine = dot(select_mine_ref[...], latents).astype(jnp.bfloat16)
-    mine_ref[...] = dot(mine, embed_ref[...]) + pos_mine_ref[...]
     heads = jnp.concatenate(heads, axis=1)
     arrival.wait()
     for at in range(0, model, STRIP):
         here = slice(at, at + STRIP)
         mixed = dot(heads[:, :half], first_ref[:, here]) + dot(heads[:, half:], second_ref[:, here])
-        mixed = mixed.astype(jnp.bfloat16)
-        for other in range(group):
-            mixed_ref[other, :, here] = mixed[other * share : (other + 1) * share]
-
-
-def sum_kernel(mine_ref, mixed_ref, out_ref):
-    total = mine_ref[...]
-    for member in range(mixed_ref.shape[0]):
-        total = total + mixed_ref[member].astype(jnp.float32)
+        keep_ref[:, here] = mixed[:share]
+        for index, send_ref in enumerate(send_refs):
+            part = mixed[(index + 1) * share : (index + 2) * share]
+            send_ref[:, here] = part.astype(jnp.bfloat16)
+
+
+def residual_kernel(mine_ref, embed_ref, pos_ref, out_ref):
+    out_ref[...] = dot(mine_ref[...], embed_ref[...]) + pos_ref[...]
+
+
+def sum_kernel(residual_ref, keep_ref, *refs):
+    *others, out_ref = refs
+    total = residual_ref[...] + keep_ref[...]
+    for other in others:
+        total = total + other[...].astype(jnp.float32)
     out_ref[...] = total.astype(jnp.bfloat16)
+
+
+def to_member(block, along, across):
+    mps, roles = lax.axis_size("mp"), lax.axis_size("role")
+    route = [
+        (mp * roles + role, ((mp + along) % mps) * roles + (role + across) % roles)
+        for mp in range(mps)
+        for role in range(roles)
+    ]
+    return lax.ppermute(block, GROUP, route)
 
 
 def on_device(
@@ -331,6 +352,7 @@
     out_weight = pltpu.with_memory_space_constraint(out_weight, pltpu.HBM)
     seqs = lax.axis_size("seq")
     group = lax.axis_size(GROUP)
+    mps, roles = lax.axis_size("mp"), lax.axis_size("role")
     patches = seqs * slots
     frame_dev = frames // seqs
     window = frame_dev + 2 * REACH
@@ -371,19 +393,19 @@
         tiled=True,
     )
 
-    products = pl.pallas_call(
-        functools.partial(weights_kernel, frame_dev, window),
+    *products, pos_mine, select, bias, first = pl.pallas_call(
+        functools.partial(weights_kernel, frame_dev, window, mps, roles),
         out_shape=(
             array((3, 2 * channels, cols), bf16),
-            array((3, patches, cols), f32),
+            array((2, patches, cols), f32),
             array((2 * channels, channels), bf16),
             array((patches, channels), f32),
             array((patches, channels), f32),
-            array((patches, channels), f32),
-            array((patches, channels), f32),
+            array((own_rows, cols), f32),
+            array((own_rows, channels), f32),
+            array((own_rows, channels), f32),
             array((share, model), f32),
             array((own_rows, rows), bf16),
-            array((share, rows), bf16),
             array((own_rows, rows), f32),
             array((cols // 2, model), bf16),
         ),
@@ -391,6 +413,8 @@
         out_specs=(VMEM,) * 12,
         scratch_shapes=[
             pltpu.VMEM((3, patches, cols), f32),
+            pltpu.VMEM((patches, channels), f32),
+            pltpu.VMEM((patches, channels), f32),
             pltpu.VMEM((patches, model), f32),
             pltpu.VMEM((3, model, cols), bf16),
             pltpu.SemaphoreType.DMA((3 * (model // min(model, DEPTH)),)),
@@ -413,11 +437,15 @@
         out_weight,
     )
 
-    mixed, mine = pl.pallas_call(
+    mine, keep, *sent = pl.pallas_call(
         attend_kernel,
-        out_shape=(array((group, share, model), bf16), array((share, model), f32)),
-        in_specs=[VMEM] * 14 + [HBM],
-        out_specs=(VMEM, VMEM),
+        out_shape=(
+            array((share, channels), bf16),
+            array((share, model), f32),
+            *[array((share, model), bf16)] * (group - 1),
+        ),
+        in_specs=[VMEM] * 12 + [HBM],
+        out_specs=(VMEM,) * (1 + group),
         scratch_shapes=[
             pltpu.VMEM((cols - cols // 2, model), bf16),
             pltpu.SemaphoreType.DMA(()),
@@ -426,19 +454,38 @@
         name="attend",
     )(
         moved,
-        embed_weight,
         *products,
+        select,
+        bias,
+        first,
         out_weight,
     )
-    mixed = lax.all_to_all(mixed, GROUP, split_axis=0, concat_axis=0, tiled=True)
+    small = pltpu.CompilerParams(vmem_limit_bytes=8 * MIB)
+    places = [(along, across) for along in range(mps) for across in range(roles)][1:]
+    routed = list(zip(places, sent))
+    routed.sort(key=lambda item: item[0][0] == 0)
+    received = [to_member(block, *place) for place, block in routed]
+    residual = pl.pallas_call(
+        residual_kernel,
+        out_shape=array((share, model), f32),
+        in_specs=[VMEM] * 3,
+        out_specs=VMEM,
+        compiler_params=small,
+        cost_estimate=pl.CostEstimate(
+            flops=2 * share * channels * model,
+            bytes_accessed=2 * channels * model,
+            transcendentals=0,
+        ),
+        name="residual",
+    )(mine, embed_weight, pos_mine)
     return pl.pallas_call(
         sum_kernel,
         out_shape=array((share, model), bf16),
-        in_specs=[VMEM] * 2,
+        in_specs=[VMEM] * (1 + group),
         out_specs=VMEM,
-        compiler_params=pltpu.CompilerParams(vmem_limit_bytes=8 * MIB),
+        compiler_params=small,
         name="final_sum",
-    )(mine, mixed)
+    )(residual, keep, *received)
 
 
 def solution(mesh):

time: 26.2 us -> 23.9 us (0.912)
  blocking collectives: 6.67 us -> 0 us
  starting transfers between devices: 7.32 us -> 9.52 us
  waiting for transfers between devices: 1.61 us -> 2.95 us
  Pallas kernels: 10.3 us -> 11.1 us
    all_to_all x1 -> x0, blocking collectives: 6.67 us -> none  [on_device(): lax.all_to_all(mixed, GROUP, split_axis=0, concat_axis=0, tiled=True)]
    ppermute x0 -> x3, starting transfers between devices: none -> 2.21 us  [to_member(): return lax.ppermute(block, GROUP, route)]
    ppermute x0 -> x3, waiting for transfers between devices: none -> 1.83 us  [to_member(): return lax.ppermute(block, GROUP, route)]
    pallas_call x2 -> x3, Pallas kernels: 7.83 us -> 8.7 us  [the longest x1 6.17 us: on_device(): pl.pallas_call(functools.partial(weights_kernel, frame_dev, window, mps,...]
    all_to_all x1, waiting for transfers between devices: 1.61 us -> 1.12 us  [on_device(): lax.all_to_all(windows, SCATTERED, split_axis=0, concat_axis=0, tiled=True)]
  transfers between devices with their start and end apart: 1 -> 4, of which waited for: 1 -> 3; matrix products, arithmetic and copies ran while one was open for 0% -> 0% of each run, Pallas kernels for 22% -> 27%
where the time goes in v9:
time: 23.9 us; the launch traced here: 23.7 us
  Pallas kernels  11.1 us (46%)
  starting transfers between devices  9.52 us (40%)
  waiting for transfers between devices  2.95 us (12%)
    all_to_all x1, starting transfers between devices, on_device(): lax.all_to_all(windows, SCATTERED, split_axis=0, concat_axis=0, tiled=True)  7.32 us
    pallas_call x1, Pallas kernels, on_device(): pl.pallas_call(functools.partial(weights_kernel, frame_dev, window, mps,...  6.17 us
    pallas_call x1, Pallas kernels, on_device(): pl.pallas_call(attend_kernel, out_shape=(array((share, channels), bf16),...  2.33 us
    ppermute x3, starting transfers between devices, to_member(): return lax.ppermute(block, GROUP, route)  2.21 us
    ppermute x3, waiting for transfers between devices, to_member(): return lax.ppermute(block, GROUP, route)  1.83 us
    pallas_call x1, Pallas kernels, on_device(): pl.pallas_call(functools.partial(latent_kernel, frame_dev), out_shape=arr...  1.8 us
    all_to_all x1, waiting for transfers between devices, on_device(): lax.all_to_all(windows, SCATTERED, split_axis=0, concat_axis=0, tiled=True)  1.12 us
    pallas_call x1, Pallas kernels, on_device(): pl.pallas_call(sum_kernel, out_shape=array((share, model), bf16), in_spec...  0.64 us
  transfers between devices with their start and end apart: 4, of which 3 were waited for; matrix products, arithmetic and copies ran while one was open for 0% of the time, Pallas kernels for 27%

profile of v9, /device:TPU:0, one launch (start us, length us, event | category | flops | bytes accessed | tf_op | source)
XLA Modules:
  0.0 23.7 jit_solution(7481766886054323950)
XLA Ops:
  0.0 0.0 copy-start
  0.0 0.0 copy-start.2
  0.0 0.0 copy-start.1
  0.0 0.0 copy-start.4
  0.0 0.0 copy-start.3
  0.0 1.8 %partial_latents.1 = bf16[32,1,8,128]{3,2,1,0:T(8,128)(2,1)} custom-call(bf16[1,16,768]{2,1,0:T(8,128)(2,1)} %hidden_hbm.1, bf16[768,128]{1,0:T(8,128)(2,1)} %weight_hbm.1), custom_call_target="tpu_custom_call" | custom-call | flops 20000000000 | bytes 40000000 | tf_op jit(solution)/shard_map/partial_latents/pallas_call | solution.py:366
  1.8 7.3 %all-to-all-start = ((bf16[32,1,8,128]{3,2,1,0:T(8,128)(2,1)}), bf16[32,1,8,128]{3,2,1,0:T(8,128)(2,1)S(1)}, u32[]{:S(2)}, u32[]{:S(2)}) async-start(bf16[32,1,8,128]{3,2,1,0:T(8,128)(2,1)} %partial_latents.1), calls=%async_computation | async-start | bytes 131072 | tf_op jit(solution)/shard_map/all_to_all | solution.py:388
  9.1 0.0 copy-done
  9.2 0.0 copy-done.2
  9.2 0.0 copy-done.1
  9.2 0.0 copy-done.4
  9.2 0.0 copy-done.3
  9.2 6.2 %weight_products.1 = (bf16[3,256,512]{2,1,0:T(8,128)(2,1)S(1)}, f32[2,8,512]{2,1,0:T(8,128)S(1)}, bf16[256,128]{1,0:T(8,128)(2,1)S(1)}, f32[8,128]{1,0:T(8,128)S...) custom-call(s32[8]{0:T(128)S(1)} %copy-done.3, ...), custom_call_target="tpu_custom_call" | custom-call | flops 1283457024 | bytes 9437184 | tf_op jit(solution)/shard_map/weight_products/pallas_call | solution.py:396
  15.4 1.1 %all-to-all-done.partial_ref = bf16[32,1,8,128]{3,2,1,0:T(8,128)(2,1)S(1)} async-done(((bf16[32,1,8,128]{3,2,1,0:T(8,128)(2,1)}), bf16[32,1,8,128]{3,2,1,0:T(8,128)(2,1)S(1)}, u32[]{:S(2)}, u32[]{:S(2)}) %all-to-all-start) | async-done | bytes 65568 | tf_op jit(solution)/shard_map/all_to_all | solution.py:388
  16.5 2.3 %attend.1 = (bf16[4,128]{1,0:T(4,128)(2,1)S(1)}, f32[4,3072]{1,0:T(4,128)S(1)}, bf16[4,3072]{1,0:T(4,128)(2,1)S(1)}, bf16[4,3072]{1,0:T(4,128)(2,1)S(1)}, bf16[4,3072]{1,0:T(4,128)(2,1)S(1)}) custom-call(bf16[32,1,8,128]{3,2,1,0:T(8,128)(2,1)S(1)} %all-to-all-done.partial_ref, bf16[3,256,512]{2,1,0:T(8,128)(2,1)S(1)} %get-tuple-element.22.scaled_ref, ...), custom_call_target="tpu_custom_call" | custom-call | tf_op jit(solution)/shard_map/attend/pallas_call | solution.py:440
  18.8 0.7 %collective-permute-start = (bf16[4,3072]{1,0:T(4,128)(2,1)S(1)}, bf16[4,3072]{1,0:T(4,128)(2,1)S(1)}, u32[]{:S(2)}, u32[]{:S(2)}) collective-permute-start(bf16[4,3072]{1,0:T(4,128)(2,1)S(1)} %get-tuple-element.36), channel_id=1, source_target_pairs={{0,2},{1,3},{2,0},{3,1},{4,6},{5,7},{6,4},{7,5},{8,10},{9,11},{10,... | collective-permute-start | bytes 73736 | tf_op jit(solution)/shard_map/ppermute | solution.py:335
  19.6 0.4 %collective-permute-start.1 = (bf16[4,3072]{1,0:T(4,128)(2,1)S(1)}, bf16[4,3072]{1,0:T(4,128)(2,1)S(1)}, u32[]{:S(2)}, u32[]{:S(2)}) collective-permute-start(bf16[4,3072]{1,0:T(4,128)(2,1)S(1)} %get-tuple-element.37), channel_id=1, source_target_pairs={{0,3},{1,2},{2,1},{3,0},{4,7},{5,6},{6,5},{7,4},{8,11},{9,10},{10,... | collective-permute-start | bytes 73736 | tf_op jit(solution)/shard_map/ppermute | solution.py:335
  19.9 1.1 %collective-permute-start.2 = (bf16[4,3072]{1,0:T(4,128)(2,1)S(1)}, bf16[4,3072]{1,0:T(4,128)(2,1)S(1)}, u32[]{:S(2)}, u32[]{:S(2)}) collective-permute-start(bf16[4,3072]{1,0:T(4,128)(2,1)S(1)} %get-tuple-element.38), channel_id=1, source_target_pairs={{0,1},{1,0},{2,3},{3,2},{4,5},{5,4},{6,7},{7,6},{8,9},{9,8},{10,11... | collective-permute-start | bytes 73736 | tf_op jit(solution)/shard_map/ppermute | solution.py:335
  21.0 0.2 residual.1.residual_ref
  21.2 1.6 %collective-permute-done.refs_0_ = bf16[4,3072]{1,0:T(4,128)(2,1)S(1)} collective-permute-done((bf16[4,3072]{1,0:T(4,128)(2,1)S(1)}, bf16[4,3072]{1,0:T(4,128)(2,1)S(1)}, u32[]{:S(2)}, u32[]{:S(2)}) %collective-permute-start) | collective-permute-done | bytes 24608 | tf_op jit(solution)/shard_map/ppermute | solution.py:335
  22.9 0.2 collective-permute-done.1.refs_1_
  23.1 0.0 collective-permute-done.2.refs_2_
  23.1 0.6 %final_sum.1 = bf16[4,3072]{1,0:T(4,128)(2,1)} custom-call(f32[4,3072]{1,0:T(4,128)S(1)} %residual.1.residual_ref, f32[4,3072]{1,0:T(4,128)S(1)} %get-tuple-element.35.keep_ref, bf16[4,3072]{1,0:T(4,128)(2,1)S(1)} %collective-permute-done.refs_0_, bf16[4,3072]{1,0:T(4,128)(2,1)S(1)} %collective-permute-done.1.refs_1_, ...), custom_call_target="tpu_custom_call" | custom-call | tf_op jit(solution)/shard_map/final_sum/pallas_call | solution.py:481
Async XLA Ops:
  0.0 9.1 %copy-start = (bf16[128,3072]{1,0:T(8,128)(2,1)S(1)}, bf16[128,3072]{1,0:T(8,128)(2,1)}, u32[]{:S(2)}) copy-start(bf16[128,3072]{1,0:T(8,128)(2,1)} %embed_ref.3) | copy-start | bytes 2359300
  0.0 9.2 %copy-start.2 = (bf16[3072]{0:T(1024)(128)(2,1)S(1)}, bf16[3072]{0:T(1024)(128)(2,1)}, u32[]{:S(2)}) copy-start(bf16[3072]{0:T(1024)(128)(2,1)} %param.15) | copy-start | bytes 18436
  0.0 9.2 %copy-start.1 = (bf16[8,3072]{1,0:T(8,128)(2,1)S(1)}, bf16[8,3072]{1,0:T(8,128)(2,1)}, u32[]{:S(2)}) copy-start(bf16[8,3072]{1,0:T(8,128)(2,1)} %pos_ref.1) | copy-start | bytes 147460
  0.0 9.2 %copy-start.4 = (s32[16]{0:T(128)S(1)}, s32[16]{0:T(128)}, u32[]{:S(2)}) copy-start(s32[16]{0:T(128)} %block_ref.1) | copy-start | bytes 196
  0.0 9.2 %copy-start.3 = (s32[8]{0:T(128)S(1)}, s32[8]{0:T(128)}, u32[]{:S(2)}) copy-start(s32[8]{0:T(128)} %order_ref.1) | copy-start | bytes 100
  1.8 14.7 %all-to-all-start = ((bf16[32,1,8,128]{3,2,1,0:T(8,128)(2,1)}), bf16[32,1,8,128]{3,2,1,0:T(8,128)(2,1)S(1)}, u32[]{:S(2)}, u32[]{:S(2)}) async-start(bf16[32,1,8,128]{3,2,1,0:T(8,128)(2,1)} %partial_latents.1), calls=%async_computation | async-start | bytes 131072 | tf_op jit(solution)/shard_map/all_to_all | solution.py:388
  18.8 4.1 %collective-permute-start = (bf16[4,3072]{1,0:T(4,128)(2,1)S(1)}, bf16[4,3072]{1,0:T(4,128)(2,1)S(1)}, u32[]{:S(2)}, u32[]{:S(2)}) collective-permute-start(bf16[4,3072]{1,0:T(4,128)(2,1)S(1)} %get-tuple-element.36), channel_id=1, source_target_pairs={{0,2},{1,3},{2,0},{3,1},{4,6},{5,7},{6,4},{7,5},{8,10},{9,11},{10,... | collective-permute-start | bytes 73736 | tf_op jit(solution)/shard_map/ppermute | solution.py:335
  19.6 3.5 %collective-permute-start.1 = (bf16[4,3072]{1,0:T(4,128)(2,1)S(1)}, bf16[4,3072]{1,0:T(4,128)(2,1)S(1)}, u32[]{:S(2)}, u32[]{:S(2)}) collective-permute-start(bf16[4,3072]{1,0:T(4,128)(2,1)S(1)} %get-tuple-element.37), channel_id=1, source_target_pairs={{0,3},{1,2},{2,1},{3,0},{4,7},{5,6},{6,5},{7,4},{8,11},{9,10},{10,... | collective-permute-start | bytes 73736 | tf_op jit(solution)/shard_map/ppermute | solution.py:335
  19.9 3.1 %collective-permute-start.2 = (bf16[4,3072]{1,0:T(4,128)(2,1)S(1)}, bf16[4,3072]{1,0:T(4,128)(2,1)S(1)}, u32[]{:S(2)}, u32[]{:S(2)}) collective-permute-start(bf16[4,3072]{1,0:T(4,128)(2,1)S(1)} %get-tuple-element.38), channel_id=1, source_target_pairs={{0,1},{1,0},{2,3},{3,2},{4,5},{5,4},{6,7},{7,6},{8,9},{9,8},{10,11... | collective-permute-start | bytes 73736 | tf_op jit(solution)/shard_map/ppermute | solution.py:335

commit v10 on v9

--- a/solution.py
+++ b/solution.py
@@ -189,6 +189,40 @@
     level = jnp.sum(pos * pos, axis=-1, keepdims=True) / channels
     natural_level_ref[...] = jnp.broadcast_to(level, (patches, channels))
 
+    def each(count, place):
+        if count <= 16:
+            for at in range(count):
+                place(at)
+        else:
+            pl.loop(0, count)(place)
+
+    def own_row(index, within):
+        to = pl.ds(index * share + within, 1)
+        return to, pl.ds((firsts[index] + within) % patches, 1)
+
+    def place_slot(slot):
+        to, at = pl.ds(slot, 1), pl.ds(order_ref[slot], 1)
+        cross_ref[to, :] = natural_cross_ref[at, :]
+        level_ref[to, :] = natural_level_ref[at, :]
+
+    def place_own(index, within):
+        to, at = own_row(index, within)
+        own_cross_ref[to, :] = natural_cross_ref[at, :]
+        own_level_ref[to, :] = natural_level_ref[at, :]
+        if index == 0:
+            pos_mine_ref[to, :] = pos_all_ref[at, :]
+
+    def place_query(index, within):
+        to, at = own_row(index, within)
+        own_offset_ref[to, :] = natural_ref[0, at, :]
+
+    def place_pair(index, slot):
+        offset_ref[index - 1, pl.ds(slot, 1), :] = natural_ref[index, pl.ds(order_ref[slot], 1), :]
+
+    each(patches, place_slot)
+    for index in range(len(firsts)):
+        each(share, functools.partial(place_own, index))
+
     for part, (index, at) in enumerate(parts):
         arrival(part).wait()
         if part + AHEAD < len(parts):
@@ -201,34 +235,11 @@
         if at + deep == model:
             keep(scaled_ref.at[index], both[:channels])
             natural_ref[index] = both[channels:]
-
-    def place(slot):
-        to, at = pl.ds(slot, 1), pl.ds(order_ref[slot], 1)
-        cross_ref[to, :] = natural_cross_ref[at, :]
-        level_ref[to, :] = natural_level_ref[at, :]
-        for index in range(1, 3):
-            offset_ref[index - 1, to, :] = natural_ref[index, at, :]
-
-    def place_own(index, within):
-        to = pl.ds(index * share + within, 1)
-        at = pl.ds((firsts[index] + within) % patches, 1)
-        own_offset_ref[to, :] = natural_ref[0, at, :]
-        own_cross_ref[to, :] = natural_cross_ref[at, :]
-        own_level_ref[to, :] = natural_level_ref[at, :]
-        if index == 0:
-            pos_mine_ref[to, :] = pos_all_ref[at, :]
-
-    if patches <= 16:
-        for slot in range(patches):
-            place(slot)
-    else:
-        pl.loop(0, patches)(place)
-    for index in range(len(firsts)):
-        if share <= 16:
-            for within in range(share):
-                place_own(index, within)
-        else:
-            pl.loop(0, share)(functools.partial(place_own, index))
+            if index == 0:
+                for member in range(len(firsts)):
+                    each(share, functools.partial(place_query, member))
+            else:
+                each(patches, functools.partial(place_pair, index))
     first.wait()
 
 
@@ -267,7 +278,6 @@
         total = total + partial_ref[other * seqs : (other + 1) * seqs].astype(jnp.float32)
     latents = total.reshape(rows, channels).astype(jnp.bfloat16)
     own = dot(select_ref[...], latents).astype(jnp.bfloat16)
-    mine_ref[...] = own[:share]
 
     def apply(part, table):
         return dot(jnp.concatenate([part, part], axis=1), table)
@@ -311,6 +321,7 @@
         for index, send_ref in enumerate(send_refs):
             part = mixed[(index + 1) * share : (index + 2) * share]
             send_ref[:, here] = part.astype(jnp.bfloat16)
+    mine_ref[...] = own[:share]
 
 
 def residual_kernel(mine_ref, embed_ref, pos_ref, out_ref):

time: 23.9 us -> 24 us (level)
  no operation moved by 1% of the time
where the time goes in v10:
time: 24 us; the launch traced here: 23.8 us
  Pallas kernels  11.3 us (47%)
  starting transfers between devices  9.52 us (40%)
  waiting for transfers between devices  2.92 us (12%)
    all_to_all x1, starting transfers between devices, on_device(): lax.all_to_all(windows, SCATTERED, split_axis=0, concat_axis=0, tiled=True)  7.32 us
    pallas_call x1, Pallas kernels, on_device(): pl.pallas_call(functools.partial(weights_kernel, frame_dev, window, mps,...  6.33 us
    pallas_call x1, Pallas kernels, on_device(): pl.pallas_call(attend_kernel, out_shape=(array((share, channels), bf16),...  2.33 us
    ppermute x3, starting transfers between devices, to_member(): return lax.ppermute(block, GROUP, route)  2.21 us
    ppermute x3, waiting for transfers between devices, to_member(): return lax.ppermute(block, GROUP, route)  1.96 us
    pallas_call x1, Pallas kernels, on_device(): pl.pallas_call(functools.partial(latent_kernel, frame_dev), out_shape=arr...  1.8 us
    all_to_all x1, waiting for transfers between devices, on_device(): lax.all_to_all(windows, SCATTERED, split_axis=0, concat_axis=0, tiled=True)  0.95 us
    pallas_call x1, Pallas kernels, on_device(): pl.pallas_call(sum_kernel, out_shape=array((share, model), bf16), in_spec...  0.64 us
  transfers between devices with their start and end apart: 4, of which 3 were waited for; matrix products, arithmetic and copies ran while one was open for 0% of the time, Pallas kernels for 27%

profile of v10, /device:TPU:0, one launch (start us, length us, event | category | flops | bytes accessed | tf_op | source)
XLA Modules:
  0.0 23.8 jit_solution(3622514606616981434)
XLA Ops:
  0.0 0.0 copy-start
  0.0 0.0 copy-start.2
  0.0 0.0 copy-start.1
  0.0 0.0 copy-start.4
  0.0 0.0 copy-start.3
  0.0 1.8 %partial_latents.1 = bf16[32,1,8,128]{3,2,1,0:T(8,128)(2,1)} custom-call(bf16[1,16,768]{2,1,0:T(8,128)(2,1)} %hidden_hbm.1, bf16[768,128]{1,0:T(8,128)(2,1)} %weight_hbm.1), custom_call_target="tpu_custom_call" | custom-call | flops 20000000000 | bytes 40000000 | tf_op jit(solution)/shard_map/partial_latents/pallas_call | solution.py:377
  1.8 7.3 %all-to-all-start = ((bf16[32,1,8,128]{3,2,1,0:T(8,128)(2,1)}), bf16[32,1,8,128]{3,2,1,0:T(8,128)(2,1)S(1)}, u32[]{:S(2)}, u32[]{:S(2)}) async-start(bf16[32,1,8,128]{3,2,1,0:T(8,128)(2,1)} %partial_latents.1), calls=%async_computation | async-start | bytes 131072 | tf_op jit(solution)/shard_map/all_to_all | solution.py:399
  9.1 0.0 copy-done
  9.2 0.0 copy-done.2
  9.2 0.0 copy-done.1
  9.2 0.0 copy-done.4
  9.2 0.0 copy-done.3
  9.2 6.3 %weight_products.1 = (bf16[3,256,512]{2,1,0:T(8,128)(2,1)S(1)}, f32[2,8,512]{2,1,0:T(8,128)S(1)}, bf16[256,128]{1,0:T(8,128)(2,1)S(1)}, f32[8,128]{1,0:T(8,128)S...) custom-call(s32[8]{0:T(128)S(1)} %copy-done.3, ...), custom_call_target="tpu_custom_call" | custom-call | flops 1283457024 | bytes 9437184 | tf_op jit(solution)/shard_map/weight_products/pallas_call | solution.py:407
  15.5 1.0 %all-to-all-done.partial_ref = bf16[32,1,8,128]{3,2,1,0:T(8,128)(2,1)S(1)} async-done(((bf16[32,1,8,128]{3,2,1,0:T(8,128)(2,1)}), bf16[32,1,8,128]{3,2,1,0:T(8,128)(2,1)S(1)}, u32[]{:S(2)}, u32[]{:S(2)}) %all-to-all-start) | async-done | bytes 65568 | tf_op jit(solution)/shard_map/all_to_all | solution.py:399
  16.5 2.3 %attend.1 = (bf16[4,128]{1,0:T(4,128)(2,1)S(1)}, f32[4,3072]{1,0:T(4,128)S(1)}, bf16[4,3072]{1,0:T(4,128)(2,1)S(1)}, bf16[4,3072]{1,0:T(4,128)(2,1)S(1)}, bf16[4,3072]{1,0:T(4,128)(2,1)S(1)}) custom-call(bf16[32,1,8,128]{3,2,1,0:T(8,128)(2,1)S(1)} %all-to-all-done.partial_ref, bf16[3,256,512]{2,1,0:T(8,128)(2,1)S(1)} %get-tuple-element.22.scaled_ref, ...), custom_call_target="tpu_custom_call" | custom-call | tf_op jit(solution)/shard_map/attend/pallas_call | solution.py:451
  18.8 0.9 %collective-permute-start = (bf16[4,3072]{1,0:T(4,128)(2,1)S(1)}, bf16[4,3072]{1,0:T(4,128)(2,1)S(1)}, u32[]{:S(2)}, u32[]{:S(2)}) collective-permute-start(bf16[4,3072]{1,0:T(4,128)(2,1)S(1)} %get-tuple-element.36), channel_id=1, source_target_pairs={{0,2},{1,3},{2,0},{3,1},{4,6},{5,7},{6,4},{7,5},{8,10},{9,11},{10,... | collective-permute-start | bytes 73736 | tf_op jit(solution)/shard_map/ppermute | solution.py:346
  19.7 0.2 collective-permute-start.1
  19.9 1.1 %collective-permute-start.2 = (bf16[4,3072]{1,0:T(4,128)(2,1)S(1)}, bf16[4,3072]{1,0:T(4,128)(2,1)S(1)}, u32[]{:S(2)}, u32[]{:S(2)}) collective-permute-start(bf16[4,3072]{1,0:T(4,128)(2,1)S(1)} %get-tuple-element.38), channel_id=1, source_target_pairs={{0,1},{1,0},{2,3},{3,2},{4,5},{5,4},{6,7},{7,6},{8,9},{9,8},{10,11... | collective-permute-start | bytes 73736 | tf_op jit(solution)/shard_map/ppermute | solution.py:346
  21.0 0.2 residual.1.residual_ref
  21.2 1.5 %collective-permute-done.refs_0_ = bf16[4,3072]{1,0:T(4,128)(2,1)S(1)} collective-permute-done((bf16[4,3072]{1,0:T(4,128)(2,1)S(1)}, bf16[4,3072]{1,0:T(4,128)(2,1)S(1)}, u32[]{:S(2)}, u32[]{:S(2)}) %collective-permute-start) | collective-permute-done | bytes 24608 | tf_op jit(solution)/shard_map/ppermute | solution.py:346
  22.7 0.5 %collective-permute-done.1.refs_1_ = bf16[4,3072]{1,0:T(4,128)(2,1)S(1)} collective-permute-done((bf16[4,3072]{1,0:T(4,128)(2,1)S(1)}, bf16[4,3072]{1,0:T(4,128)(2,1)S(1)}, u32[]{:S(2)}, u32[]{:S(2)}) %collective-permute-start.1) | collective-permute-done | bytes 24608 | tf_op jit(solution)/shard_map/ppermute | solution.py:346
  23.2 0.0 collective-permute-done.2.refs_2_
  23.2 0.6 %final_sum.1 = bf16[4,3072]{1,0:T(4,128)(2,1)} custom-call(f32[4,3072]{1,0:T(4,128)S(1)} %residual.1.residual_ref, f32[4,3072]{1,0:T(4,128)S(1)} %get-tuple-element.35.keep_ref, bf16[4,3072]{1,0:T(4,128)(2,1)S(1)} %collective-permute-done.refs_0_, bf16[4,3072]{1,0:T(4,128)(2,1)S(1)} %collective-permute-done.1.refs_1_, ...), custom_call_target="tpu_custom_call" | custom-call | tf_op jit(solution)/shard_map/final_sum/pallas_call | solution.py:492
Async XLA Ops:
  0.0 9.1 %copy-start = (bf16[128,3072]{1,0:T(8,128)(2,1)S(1)}, bf16[128,3072]{1,0:T(8,128)(2,1)}, u32[]{:S(2)}) copy-start(bf16[128,3072]{1,0:T(8,128)(2,1)} %embed_ref.3) | copy-start | bytes 2359300
  0.0 9.2 %copy-start.2 = (bf16[3072]{0:T(1024)(128)(2,1)S(1)}, bf16[3072]{0:T(1024)(128)(2,1)}, u32[]{:S(2)}) copy-start(bf16[3072]{0:T(1024)(128)(2,1)} %param.15) | copy-start | bytes 18436
  0.0 9.2 %copy-start.1 = (bf16[8,3072]{1,0:T(8,128)(2,1)S(1)}, bf16[8,3072]{1,0:T(8,128)(2,1)}, u32[]{:S(2)}) copy-start(bf16[8,3072]{1,0:T(8,128)(2,1)} %pos_ref.1) | copy-start | bytes 147460
  0.0 9.2 %copy-start.4 = (s32[16]{0:T(128)S(1)}, s32[16]{0:T(128)}, u32[]{:S(2)}) copy-start(s32[16]{0:T(128)} %block_ref.1) | copy-start | bytes 196
  0.0 9.2 %copy-start.3 = (s32[8]{0:T(128)S(1)}, s32[8]{0:T(128)}, u32[]{:S(2)}) copy-start(s32[8]{0:T(128)} %order_ref.1) | copy-start | bytes 100
  1.8 14.7 %all-to-all-start = ((bf16[32,1,8,128]{3,2,1,0:T(8,128)(2,1)}), bf16[32,1,8,128]{3,2,1,0:T(8,128)(2,1)S(1)}, u32[]{:S(2)}, u32[]{:S(2)}) async-start(bf16[32,1,8,128]{3,2,1,0:T(8,128)(2,1)} %partial_latents.1), calls=%async_computation | async-start | bytes 131072 | tf_op jit(solution)/shard_map/all_to_all | solution.py:399
  18.8 3.9 %collective-permute-start = (bf16[4,3072]{1,0:T(4,128)(2,1)S(1)}, bf16[4,3072]{1,0:T(4,128)(2,1)S(1)}, u32[]{:S(2)}, u32[]{:S(2)}) collective-permute-start(bf16[4,3072]{1,0:T(4,128)(2,1)S(1)} %get-tuple-element.36), channel_id=1, source_target_pairs={{0,2},{1,3},{2,0},{3,1},{4,6},{5,7},{6,4},{7,5},{8,10},{9,11},{10,... | collective-permute-start | bytes 73736 | tf_op jit(solution)/shard_map/ppermute | solution.py:346
  19.7 3.5 %collective-permute-start.1 = (bf16[4,3072]{1,0:T(4,128)(2,1)S(1)}, bf16[4,3072]{1,0:T(4,128)(2,1)S(1)}, u32[]{:S(2)}, u32[]{:S(2)}) collective-permute-start(bf16[4,3072]{1,0:T(4,128)(2,1)S(1)} %get-tuple-element.37), channel_id=1, source_target_pairs={{0,3},{1,2},{2,1},{3,0},{4,7},{5,6},{6,5},{7,4},{8,11},{9,10},{10,... | collective-permute-start | bytes 73736 | tf_op jit(solution)/shard_map/ppermute | solution.py:346
  19.9 3.3 %collective-permute-start.2 = (bf16[4,3072]{1,0:T(4,128)(2,1)S(1)}, bf16[4,3072]{1,0:T(4,128)(2,1)S(1)}, u32[]{:S(2)}, u32[]{:S(2)}) collective-permute-start(bf16[4,3072]{1,0:T(4,128)(2,1)S(1)} %get-tuple-element.38), channel_id=1, source_target_pairs={{0,1},{1,0},{2,3},{3,2},{4,5},{5,4},{6,7},{7,6},{8,9},{9,8},{10,11... | collective-permute-start | bytes 73736 | tf_op jit(solution)/shard_map/ppermute | solution.py:346

commit v11 on v7

--- a/solution.py
+++ b/solution.py
@@ -15,7 +15,7 @@
 LANES = 128
 STEP_ROWS = 256
 DEPTH = 1024
-AHEAD = 4
+AHEAD = 9
 STRIP = 512
 MIB = 1024 * 1024
 VMEM = pl.BlockSpec(memory_space=pltpu.VMEM)
@@ -121,8 +121,9 @@
     first = pltpu.make_async_copy(
         out_weight_hbm.at[pl.ds(0, first_ref.shape[0])], first_ref, first_sem
     )
-    for part in range(AHEAD):
+    for part in range(min(AHEAD, len(parts))):
         arrival(part).start()
+    first.start()
 
     pos = pos_ref[...].astype(jnp.float32)
     pos_all_ref[...] = pos
@@ -195,8 +196,6 @@
         arrival(part).wait()
         if part + AHEAD < len(parts):
             arrival(part + AHEAD).start()
-        if part + AHEAD == len(parts) - 1:
-            first.start()
         here = slice(at, at + deep)
         product = dot(left[:, here], weight_ref[index, here])
         both = product if at == 0 else both + product
@@ -222,8 +221,8 @@
 
 
 def attend_kernel(
+    roles,
     partial_ref,
-    embed_ref,
     scaled_ref,
     offset_ref,
     gram_ref,
@@ -231,22 +230,23 @@
     level_ref,
     natural_cross_ref,
     natural_level_ref,
-    pos_mine_ref,
     select_ref,
     select_mine_ref,
     bias_ref,
     first_ref,
     out_weight_hbm,
-    mixed_ref,
     mine_ref,
-    second_ref,
-    sem,
+    keep_ref,
+    *rest,
 ):
+    *send_refs, second_ref, sem = rest
     half = first_ref.shape[0]
     arrival = pltpu.make_async_copy(out_weight_hbm.at[pl.ds(half, half)], second_ref, sem)
     arrival.start()
     everyone, slots, window, channels = partial_ref.shape
-    group, share, model = mixed_ref.shape
+    share, model = keep_ref.shape
+    group = 1 + len(send_refs)
+    mps = group // roles
     seqs = everyone // group
     patches = seqs * slots
     rows = patches * window
@@ -295,23 +295,51 @@
         expo = jnp.exp(scores - jnp.max(scores, axis=-1, keepdims=True))
         probs = (expo / jnp.sum(expo, axis=-1, keepdims=True)).astype(jnp.bfloat16)
         heads.append(dot(probs, value[:, at]).astype(jnp.bfloat16))
-    mine = dot(select_mine_ref[...], latents).astype(jnp.bfloat16)
-    mine_ref[...] = dot(mine, embed_ref[...]) + pos_mine_ref[...]
+    mine_ref[...] = dot(select_mine_ref[...], latents).astype(jnp.bfloat16)
     heads = jnp.concatenate(heads, axis=1)
     arrival.wait()
+    mp, role = lax.axis_index("mp"), lax.axis_index("role")
+    members = [
+        ((mp + along) % mps) * roles + (role + across) % roles
+        for along in range(mps)
+        for across in range(roles)
+    ]
     for at in range(0, model, STRIP):
         here = slice(at, at + STRIP)
         mixed = dot(heads[:, :half], first_ref[:, here]) + dot(heads[:, half:], second_ref[:, here])
-        mixed = mixed.astype(jnp.bfloat16)
-        for other in range(group):
-            mixed_ref[other, :, here] = mixed[other * share : (other + 1) * share]
-
-
-def sum_kernel(mine_ref, mixed_ref, out_ref):
-    total = mine_ref[...]
-    for member in range(mixed_ref.shape[0]):
-        total = total + mixed_ref[member].astype(jnp.float32)
+        parts = [mixed[index * share : (index + 1) * share] for index in range(group)]
+
+        def of_member(member):
+            found = parts[0]
+            for index in range(1, group):
+                found = jnp.where(member == index, parts[index], found)
+            return found
+
+        keep_ref[:, here] = of_member(members[0])
+        for member, send_ref in zip(members[1:], send_refs):
+            send_ref[:, here] = of_member(member).astype(jnp.bfloat16)
+
+
+def residual_kernel(mine_ref, embed_ref, pos_ref, out_ref):
+    out_ref[...] = dot(mine_ref[...], embed_ref[...]) + pos_ref[...]
+
+
+def sum_kernel(residual_ref, keep_ref, *refs):
+    *others, out_ref = refs
+    total = residual_ref[...] + keep_ref[...]
+    for other in others:
+        total = total + other[...].astype(jnp.float32)
     out_ref[...] = total.astype(jnp.bfloat16)
+
+
+def to_member(block, along, across):
+    mps, roles = lax.axis_size("mp"), lax.axis_size("role")
+    route = [
+        (mp * roles + role, ((mp + along) % mps) * roles + (role + across) % roles)
+        for mp in range(mps)
+        for role in range(roles)
+    ]
+    return lax.ppermute(block, GROUP, route)
 
 
 def on_device(
@@ -331,6 +359,7 @@
     out_weight = pltpu.with_memory_space_constraint(out_weight, pltpu.HBM)
     seqs = lax.axis_size("seq")
     group = lax.axis_size(GROUP)
+    mps, roles = lax.axis_size("mp"), lax.axis_size("role")
     patches = seqs * slots
     frame_dev = frames // seqs
     window = frame_dev + 2 * REACH
@@ -371,7 +400,7 @@
         tiled=True,
     )
 
-    products = pl.pallas_call(
+    *products, pos_mine, select, select_mine, bias, first = pl.pallas_call(
         functools.partial(weights_kernel, frame_dev, window),
         out_shape=(
             array((3, 2 * channels, cols), bf16),
@@ -413,11 +442,15 @@
         out_weight,
     )
 
-    mixed, mine = pl.pallas_call(
-        attend_kernel,
-        out_shape=(array((group, share, model), bf16), array((share, model), f32)),
-        in_specs=[VMEM] * 14 + [HBM],
-        out_specs=(VMEM, VMEM),
+    mine, keep, *sent = pl.pallas_call(
+        functools.partial(attend_kernel, roles),
+        out_shape=(
+            array((share, channels), bf16),
+            array((share, model), f32),
+            *[array((share, model), bf16)] * (group - 1),
+        ),
+        in_specs=[VMEM] * 12 + [HBM],
+        out_specs=(VMEM,) * (1 + group),
         scratch_shapes=[
             pltpu.VMEM((cols - cols // 2, model), bf16),
             pltpu.SemaphoreType.DMA(()),
@@ -426,19 +459,39 @@
         name="attend",
     )(
         moved,
-        embed_weight,
         *products,
+        select,
+        select_mine,
+        bias,
+        first,
         out_weight,
     )
-    mixed = lax.all_to_all(mixed, GROUP, split_axis=0, concat_axis=0, tiled=True)
+    small = pltpu.CompilerParams(vmem_limit_bytes=8 * MIB)
+    places = [(along, across) for along in range(mps) for across in range(roles)][1:]
+    routed = list(zip(places, sent))
+    routed.sort(key=lambda item: item[0][0] == 0)
+    received = [to_member(block, *place) for place, block in routed]
+    residual = pl.pallas_call(
+        residual_kernel,
+        out_shape=array((share, model), f32),
+        in_specs=[VMEM] * 3,
+        out_specs=VMEM,
+        compiler_params=small,
+        cost_estimate=pl.CostEstimate(
+            flops=2 * share * channels * model,
+            bytes_accessed=2 * channels * model,
+            transcendentals=0,
+        ),
+        name="residual",
+    )(mine, embed_weight, pos_mine)
     return pl.pallas_call(
         sum_kernel,
         out_shape=array((share, model), bf16),
-        in_specs=[VMEM] * 2,
+        in_specs=[VMEM] * (1 + group),
         out_specs=VMEM,
-        compiler_params=pltpu.CompilerParams(vmem_limit_bytes=8 * MIB),
+        compiler_params=small,
         name="final_sum",
-    )(mine, mixed)
+    )(residual, keep, *received)
 
 
 def solution(mesh):

time: 26.2 us -> 23.5 us (0.90)
  blocking collectives: 6.67 us -> 0 us
  starting transfers between devices: 7.32 us -> 9.52 us
  waiting for transfers between devices: 1.61 us -> 3.6 us
    all_to_all x1 -> x0, blocking collectives: 6.67 us -> none  [on_device(): lax.all_to_all(mixed, GROUP, split_axis=0, concat_axis=0, tiled=True)]
    ppermute x0 -> x3, starting transfers between devices: none -> 2.21 us  [to_member(): return lax.ppermute(block, GROUP, route)]
    ppermute x0 -> x3, waiting for transfers between devices: none -> 1.8 us  [to_member(): return lax.ppermute(block, GROUP, route)]
    pallas_call x1 -> x2, Pallas kernels: 2.15 us -> 2.2 us  [the longest x1 1.99 us: on_device(): pl.pallas_call(functools.partial(attend_kernel, roles), out_shape=(array(...]
  transfers between devices with their start and end apart: 1 -> 4, of which waited for: 1 -> 3; matrix products, arithmetic and copies ran while one was open for 0% -> 0% of each run, Pallas kernels for 22% -> 24%
where the time goes in v11:
time: 23.5 us; the launch traced here: 23.3 us
  Pallas kernels  10.1 us (43%)
  starting transfers between devices  9.52 us (41%)
  waiting for transfers between devices  3.6 us (15%)
    all_to_all x1, starting transfers between devices, on_device(): lax.all_to_all(windows, SCATTERED, split_axis=0, concat_axis=0, tiled=True)  7.32 us
    pallas_call x1, Pallas kernels, on_device(): pl.pallas_call(functools.partial(weights_kernel, frame_dev, window), out_...  5.48 us
    ppermute x3, starting transfers between devices, to_member(): return lax.ppermute(block, GROUP, route)  2.21 us
    pallas_call x1, Pallas kernels, on_device(): pl.pallas_call(functools.partial(attend_kernel, roles), out_shape=(array(...  1.99 us
    all_to_all x1, waiting for transfers between devices, on_device(): lax.all_to_all(windows, SCATTERED, split_axis=0, concat_axis=0, tiled=True)  1.8 us
    pallas_call x1, Pallas kernels, on_device(): pl.pallas_call(functools.partial(latent_kernel, frame_dev), out_shape=arr...  1.8 us
    ppermute x3, waiting for transfers between devices, to_member(): return lax.ppermute(block, GROUP, route)  1.8 us
    pallas_call x1, Pallas kernels, on_device(): pl.pallas_call(sum_kernel, out_shape=array((share, model), bf16), in_spec...  0.64 us
  transfers between devices with their start and end apart: 4, of which 3 were waited for; matrix products, arithmetic and copies ran while one was open for 0% of the time, Pallas kernels for 24%

profile of v11, /device:TPU:0, one launch (start us, length us, event | category | flops | bytes accessed | tf_op | source)
XLA Modules:
  0.0 23.3 jit_solution(8303401225929727591)
XLA Ops:
  0.0 0.0 copy-start
  0.0 0.0 copy-start.2
  0.0 0.0 copy-start.1
  0.0 0.0 copy-start.4
  0.0 0.0 copy-start.3
  0.0 1.8 %partial_latents.1 = bf16[32,1,8,128]{3,2,1,0:T(8,128)(2,1)} custom-call(bf16[1,16,768]{2,1,0:T(8,128)(2,1)} %hidden_hbm.1, bf16[768,128]{1,0:T(8,128)(2,1)} %weight_hbm.1), custom_call_target="tpu_custom_call" | custom-call | flops 20000000000 | bytes 40000000 | tf_op jit(solution)/shard_map/partial_latents/pallas_call | solution.py:373
  1.8 7.3 %all-to-all-start = ((bf16[32,1,8,128]{3,2,1,0:T(8,128)(2,1)}), bf16[32,1,8,128]{3,2,1,0:T(8,128)(2,1)S(1)}, u32[]{:S(2)}, u32[]{:S(2)}) async-start(bf16[32,1,8,128]{3,2,1,0:T(8,128)(2,1)} %partial_latents.1), calls=%async_computation | async-start | bytes 131072 | tf_op jit(solution)/shard_map/all_to_all | solution.py:395
  9.1 0.0 copy-done
  9.2 0.0 copy-done.2
  9.2 0.0 copy-done.1
  9.2 0.0 copy-done.4
  9.2 0.0 copy-done.3
  9.2 5.5 %weight_products.1 = (bf16[3,256,512]{2,1,0:T(8,128)(2,1)S(1)}, f32[3,8,512]{2,1,0:T(8,128)S(1)}, bf16[256,128]{1,0:T(8,128)(2,1)S(1)}, f32[8,128]{1,0:T(8,128)S...) custom-call(s32[8]{0:T(128)S(1)} %copy-done.3, ...), custom_call_target="tpu_custom_call" | custom-call | flops 1283457024 | bytes 9437184 | tf_op jit(solution)/shard_map/weight_products/pallas_call | solution.py:403
  14.7 1.8 %all-to-all-done.partial_ref = bf16[32,1,8,128]{3,2,1,0:T(8,128)(2,1)S(1)} async-done(((bf16[32,1,8,128]{3,2,1,0:T(8,128)(2,1)}), bf16[32,1,8,128]{3,2,1,0:T(8,128)(2,1)S(1)}, u32[]{:S(2)}, u32[]{:S(2)}) %all-to-all-start) | async-done | bytes 65568 | tf_op jit(solution)/shard_map/all_to_all | solution.py:395
  16.5 2.0 %attend.1 = (bf16[4,128]{1,0:T(4,128)(2,1)S(1)}, f32[4,3072]{1,0:T(4,128)S(1)}, bf16[4,3072]{1,0:T(4,128)(2,1)S(1)}, bf16[4,3072]{1,0:T(4,128)(2,1)S(1)}, bf16[4,3072]{1,0:T(4,128)(2,1)S(1)}) custom-call(bf16[32,1,8,128]{3,2,1,0:T(8,128)(2,1)S(1)} %all-to-all-done.partial_ref, bf16[3,256,512]{2,1,0:T(8,128)(2,1)S(1)} %get-tuple-element.22.scaled_ref, ...), custom_call_target="tpu_custom_call" | custom-call | tf_op jit(solution)/shard_map/attend/pallas_call | solution.py:445
  18.5 0.7 %collective-permute-start = (bf16[4,3072]{1,0:T(4,128)(2,1)S(1)}, bf16[4,3072]{1,0:T(4,128)(2,1)S(1)}, u32[]{:S(2)}, u32[]{:S(2)}) collective-permute-start(bf16[4,3072]{1,0:T(4,128)(2,1)S(1)} %get-tuple-element.36), channel_id=1, source_target_pairs={{0,2},{1,3},{2,0},{3,1},{4,6},{5,7},{6,4},{7,5},{8,10},{9,11},{10,... | collective-permute-start | bytes 73736 | tf_op jit(solution)/shard_map/ppermute | solution.py:342
  19.2 0.4 %collective-permute-start.1 = (bf16[4,3072]{1,0:T(4,128)(2,1)S(1)}, bf16[4,3072]{1,0:T(4,128)(2,1)S(1)}, u32[]{:S(2)}, u32[]{:S(2)}) collective-permute-start(bf16[4,3072]{1,0:T(4,128)(2,1)S(1)} %get-tuple-element.37), channel_id=1, source_target_pairs={{0,3},{1,2},{2,1},{3,0},{4,7},{5,6},{6,5},{7,4},{8,11},{9,10},{10,... | collective-permute-start | bytes 73736 | tf_op jit(solution)/shard_map/ppermute | solution.py:342
  19.6 1.1 %collective-permute-start.2 = (bf16[4,3072]{1,0:T(4,128)(2,1)S(1)}, bf16[4,3072]{1,0:T(4,128)(2,1)S(1)}, u32[]{:S(2)}, u32[]{:S(2)}) collective-permute-start(bf16[4,3072]{1,0:T(4,128)(2,1)S(1)} %get-tuple-element.38), channel_id=1, source_target_pairs={{0,1},{1,0},{2,3},{3,2},{4,5},{5,4},{6,7},{7,6},{8,9},{9,8},{10,11... | collective-permute-start | bytes 73736 | tf_op jit(solution)/shard_map/ppermute | solution.py:342
  20.7 0.2 residual.1.residual_ref
  20.9 1.7 %collective-permute-done.refs_0_ = bf16[4,3072]{1,0:T(4,128)(2,1)S(1)} collective-permute-done((bf16[4,3072]{1,0:T(4,128)(2,1)S(1)}, bf16[4,3072]{1,0:T(4,128)(2,1)S(1)}, u32[]{:S(2)}, u32[]{:S(2)}) %collective-permute-start) | collective-permute-done | bytes 24608 | tf_op jit(solution)/shard_map/ppermute | solution.py:342
  22.6 0.1 collective-permute-done.1.refs_1_
  22.7 0.0 collective-permute-done.2.refs_2_
  22.7 0.6 %final_sum.1 = bf16[4,3072]{1,0:T(4,128)(2,1)} custom-call(f32[4,3072]{1,0:T(4,128)S(1)} %residual.1.residual_ref, f32[4,3072]{1,0:T(4,128)S(1)} %get-tuple-element.35.keep_ref, bf16[4,3072]{1,0:T(4,128)(2,1)S(1)} %collective-permute-done.refs_0_, bf16[4,3072]{1,0:T(4,128)(2,1)S(1)} %collective-permute-done.1.refs_1_, ...), custom_call_target="tpu_custom_call" | custom-call | tf_op jit(solution)/shard_map/final_sum/pallas_call | solution.py:487
Async XLA Ops:
  0.0 9.1 %copy-start = (bf16[128,3072]{1,0:T(8,128)(2,1)S(1)}, bf16[128,3072]{1,0:T(8,128)(2,1)}, u32[]{:S(2)}) copy-start(bf16[128,3072]{1,0:T(8,128)(2,1)} %embed_ref.3) | copy-start | bytes 2359300
  0.0 9.2 %copy-start.2 = (bf16[3072]{0:T(1024)(128)(2,1)S(1)}, bf16[3072]{0:T(1024)(128)(2,1)}, u32[]{:S(2)}) copy-start(bf16[3072]{0:T(1024)(128)(2,1)} %param.15) | copy-start | bytes 18436
  0.0 9.2 %copy-start.1 = (bf16[8,3072]{1,0:T(8,128)(2,1)S(1)}, bf16[8,3072]{1,0:T(8,128)(2,1)}, u32[]{:S(2)}) copy-start(bf16[8,3072]{1,0:T(8,128)(2,1)} %pos_ref.1) | copy-start | bytes 147460
  0.0 9.2 %copy-start.4 = (s32[16]{0:T(128)S(1)}, s32[16]{0:T(128)}, u32[]{:S(2)}) copy-start(s32[16]{0:T(128)} %block_ref.1) | copy-start | bytes 196
  0.0 9.2 %copy-start.3 = (s32[8]{0:T(128)S(1)}, s32[8]{0:T(128)}, u32[]{:S(2)}) copy-start(s32[8]{0:T(128)} %order_ref.1) | copy-start | bytes 100
  1.8 14.7 %all-to-all-start = ((bf16[32,1,8,128]{3,2,1,0:T(8,128)(2,1)}), bf16[32,1,8,128]{3,2,1,0:T(8,128)(2,1)S(1)}, u32[]{:S(2)}, u32[]{:S(2)}) async-start(bf16[32,1,8,128]{3,2,1,0:T(8,128)(2,1)} %partial_latents.1), calls=%async_computation | async-start | bytes 131072 | tf_op jit(solution)/shard_map/all_to_all | solution.py:395
  18.5 4.1 %collective-permute-start = (bf16[4,3072]{1,0:T(4,128)(2,1)S(1)}, bf16[4,3072]{1,0:T(4,128)(2,1)S(1)}, u32[]{:S(2)}, u32[]{:S(2)}) collective-permute-start(bf16[4,3072]{1,0:T(4,128)(2,1)S(1)} %get-tuple-element.36), channel_id=1, source_target_pairs={{0,2},{1,3},{2,0},{3,1},{4,6},{5,7},{6,4},{7,5},{8,10},{9,11},{10,... | collective-permute-start | bytes 73736 | tf_op jit(solution)/shard_map/ppermute | solution.py:342
  19.2 3.5 %collective-permute-start.1 = (bf16[4,3072]{1,0:T(4,128)(2,1)S(1)}, bf16[4,3072]{1,0:T(4,128)(2,1)S(1)}, u32[]{:S(2)}, u32[]{:S(2)}) collective-permute-start(bf16[4,3072]{1,0:T(4,128)(2,1)S(1)} %get-tuple-element.37), channel_id=1, source_target_pairs={{0,3},{1,2},{2,1},{3,0},{4,7},{5,6},{6,5},{7,4},{8,11},{9,10},{10,... | collective-permute-start | bytes 73736 | tf_op jit(solution)/shard_map/ppermute | solution.py:342
  19.6 3.1 %collective-permute-start.2 = (bf16[4,3072]{1,0:T(4,128)(2,1)S(1)}, bf16[4,3072]{1,0:T(4,128)(2,1)S(1)}, u32[]{:S(2)}, u32[]{:S(2)}) collective-permute-start(bf16[4,3072]{1,0:T(4,128)(2,1)S(1)} %get-tuple-element.38), channel_id=1, source_target_pairs={{0,1},{1,0},{2,3},{3,2},{4,5},{5,4},{6,7},{7,6},{8,9},{9,8},{10,11... | collective-permute-start | bytes 73736 | tf_op jit(solution)/shard_map/ppermute | solution.py:342

commit v12 on v11

--- a/solution.py
+++ b/solution.py
@@ -468,9 +468,7 @@
     )
     small = pltpu.CompilerParams(vmem_limit_bytes=8 * MIB)
     places = [(along, across) for along in range(mps) for across in range(roles)][1:]
-    routed = list(zip(places, sent))
-    routed.sort(key=lambda item: item[0][0] == 0)
-    received = [to_member(block, *place) for place, block in routed]
+    received = [to_member(block, *place) for place, block in zip(places, sent)]
     residual = pl.pallas_call(
         residual_kernel,
         out_shape=array((share, model), f32),

time: 23.5 us -> 23.6 us (level)
  waiting for transfers between devices: 3.6 us -> 3.94 us
  starting transfers between devices: 9.52 us -> 9.25 us
    ppermute x3, waiting for transfers between devices: 1.8 us -> 2.14 us  [to_member(): return lax.ppermute(block, GROUP, route)]
    ppermute x3, starting transfers between devices: 2.21 us -> 1.93 us  [to_member(): return lax.ppermute(block, GROUP, route)]
where the time goes in v12:
time: 23.6 us; the launch traced here: 23.4 us
  Pallas kernels  10.1 us (43%)
  starting transfers between devices  9.25 us (39%)
  waiting for transfers between devices  3.94 us (17%)
    all_to_all x1, starting transfers between devices, on_device(): lax.all_to_all(windows, SCATTERED, split_axis=0, concat_axis=0, tiled=True)  7.32 us
    pallas_call x1, Pallas kernels, on_device(): pl.pallas_call(functools.partial(weights_kernel, frame_dev, window), out_...  5.48 us
    ppermute x3, waiting for transfers between devices, to_member(): return lax.ppermute(block, GROUP, route)  2.14 us
    pallas_call x1, Pallas kernels, on_device(): pl.pallas_call(functools.partial(attend_kernel, roles), out_shape=(array(...  1.99 us
    ppermute x3, starting transfers between devices, to_member(): return lax.ppermute(block, GROUP, route)  1.93 us
    all_to_all x1, waiting for transfers between devices, on_device(): lax.all_to_all(windows, SCATTERED, split_axis=0, concat_axis=0, tiled=True)  1.8 us
    pallas_call x1, Pallas kernels, on_device(): pl.pallas_call(functools.partial(latent_kernel, frame_dev), out_shape=arr...  1.8 us
    pallas_call x1, Pallas kernels, on_device(): pl.pallas_call(sum_kernel, out_shape=array((share, model), bf16), in_spec...  0.63 us
  transfers between devices with their start and end apart: 4, of which 3 were waited for; matrix products, arithmetic and copies ran while one was open for 0% of the time, Pallas kernels for 24%

profile of v12, /device:TPU:0, one launch (start us, length us, event | category | flops | bytes accessed | tf_op | source)
XLA Modules:
  0.0 23.4 jit_solution(2929258073256956478)
XLA Ops:
  0.0 0.0 copy-start
  0.0 0.0 copy-start.2
  0.0 0.0 copy-start.1
  0.0 0.0 copy-start.4
  0.0 0.0 copy-start.3
  0.0 1.8 %partial_latents.1 = bf16[32,1,8,128]{3,2,1,0:T(8,128)(2,1)} custom-call(bf16[1,16,768]{2,1,0:T(8,128)(2,1)} %hidden_hbm.1, bf16[768,128]{1,0:T(8,128)(2,1)} %weight_hbm.1), custom_call_target="tpu_custom_call" | custom-call | flops 20000000000 | bytes 40000000 | tf_op jit(solution)/shard_map/partial_latents/pallas_call | solution.py:373
  1.8 7.3 %all-to-all-start = ((bf16[32,1,8,128]{3,2,1,0:T(8,128)(2,1)}), bf16[32,1,8,128]{3,2,1,0:T(8,128)(2,1)S(1)}, u32[]{:S(2)}, u32[]{:S(2)}) async-start(bf16[32,1,8,128]{3,2,1,0:T(8,128)(2,1)} %partial_latents.1), calls=%async_computation | async-start | bytes 131072 | tf_op jit(solution)/shard_map/all_to_all | solution.py:395
  9.1 0.0 copy-done
  9.2 0.0 copy-done.2
  9.2 0.0 copy-done.1
  9.2 0.0 copy-done.4
  9.2 0.0 copy-done.3
  9.2 5.5 %weight_products.1 = (bf16[3,256,512]{2,1,0:T(8,128)(2,1)S(1)}, f32[3,8,512]{2,1,0:T(8,128)S(1)}, bf16[256,128]{1,0:T(8,128)(2,1)S(1)}, f32[8,128]{1,0:T(8,128)S...) custom-call(s32[8]{0:T(128)S(1)} %copy-done.3, ...), custom_call_target="tpu_custom_call" | custom-call | flops 1283457024 | bytes 9437184 | tf_op jit(solution)/shard_map/weight_products/pallas_call | solution.py:403
  14.7 1.8 %all-to-all-done.partial_ref = bf16[32,1,8,128]{3,2,1,0:T(8,128)(2,1)S(1)} async-done(((bf16[32,1,8,128]{3,2,1,0:T(8,128)(2,1)}), bf16[32,1,8,128]{3,2,1,0:T(8,128)(2,1)S(1)}, u32[]{:S(2)}, u32[]{:S(2)}) %all-to-all-start) | async-done | bytes 65568 | tf_op jit(solution)/shard_map/all_to_all | solution.py:395
  16.5 2.0 %attend.1 = (bf16[4,128]{1,0:T(4,128)(2,1)S(1)}, f32[4,3072]{1,0:T(4,128)S(1)}, bf16[4,3072]{1,0:T(4,128)(2,1)S(1)}, bf16[4,3072]{1,0:T(4,128)(2,1)S(1)}, bf16[4,3072]{1,0:T(4,128)(2,1)S(1)}) custom-call(bf16[32,1,8,128]{3,2,1,0:T(8,128)(2,1)S(1)} %all-to-all-done.partial_ref, bf16[3,256,512]{2,1,0:T(8,128)(2,1)S(1)} %get-tuple-element.22.scaled_ref, ...), custom_call_target="tpu_custom_call" | custom-call | tf_op jit(solution)/shard_map/attend/pallas_call | solution.py:445
  18.5 0.1 collective-permute-start
  18.6 0.7 %collective-permute-start.1 = (bf16[4,3072]{1,0:T(4,128)(2,1)S(1)}, bf16[4,3072]{1,0:T(4,128)(2,1)S(1)}, u32[]{:S(2)}, u32[]{:S(2)}) collective-permute-start(bf16[4,3072]{1,0:T(4,128)(2,1)S(1)} %get-tuple-element.37), channel_id=1, source_target_pairs={{0,2},{1,3},{2,0},{3,1},{4,6},{5,7},{6,4},{7,5},{8,10},{9,11},{10,... | collective-permute-start | bytes 73736 | tf_op jit(solution)/shard_map/ppermute | solution.py:342
  19.3 1.2 %collective-permute-start.2 = (bf16[4,3072]{1,0:T(4,128)(2,1)S(1)}, bf16[4,3072]{1,0:T(4,128)(2,1)S(1)}, u32[]{:S(2)}, u32[]{:S(2)}) collective-permute-start(bf16[4,3072]{1,0:T(4,128)(2,1)S(1)} %get-tuple-element.38), channel_id=1, source_target_pairs={{0,3},{1,2},{2,1},{3,0},{4,7},{5,6},{6,5},{7,4},{8,11},{9,10},{10,... | collective-permute-start | bytes 73736 | tf_op jit(solution)/shard_map/ppermute | solution.py:342
  20.4 0.2 residual.1.residual_ref
  20.6 0.0 collective-permute-done.refs_0_
  20.6 2.0 %collective-permute-done.1.refs_1_ = bf16[4,3072]{1,0:T(4,128)(2,1)S(1)} collective-permute-done((bf16[4,3072]{1,0:T(4,128)(2,1)S(1)}, bf16[4,3072]{1,0:T(4,128)(2,1)S(1)}, u32[]{:S(2)}, u32[]{:S(2)}) %collective-permute-start.1) | collective-permute-done | bytes 24608 | tf_op jit(solution)/shard_map/ppermute | solution.py:342
  22.7 0.1 collective-permute-done.2.refs_2_
  22.8 0.6 %final_sum.1 = bf16[4,3072]{1,0:T(4,128)(2,1)} custom-call(f32[4,3072]{1,0:T(4,128)S(1)} %residual.1.residual_ref, f32[4,3072]{1,0:T(4,128)S(1)} %get-tuple-element.35.keep_ref, bf16[4,3072]{1,0:T(4,128)(2,1)S(1)} %collective-permute-done.refs_0_, bf16[4,3072]{1,0:T(4,128)(2,1)S(1)} %collective-permute-done.1.refs_1_, ...), custom_call_target="tpu_custom_call" | custom-call | tf_op jit(solution)/shard_map/final_sum/pallas_call | solution.py:485
Async XLA Ops:
  0.0 9.1 %copy-start = (bf16[128,3072]{1,0:T(8,128)(2,1)S(1)}, bf16[128,3072]{1,0:T(8,128)(2,1)}, u32[]{:S(2)}) copy-start(bf16[128,3072]{1,0:T(8,128)(2,1)} %embed_ref.3) | copy-start | bytes 2359300
  0.0 9.2 %copy-start.2 = (bf16[3072]{0:T(1024)(128)(2,1)S(1)}, bf16[3072]{0:T(1024)(128)(2,1)}, u32[]{:S(2)}) copy-start(bf16[3072]{0:T(1024)(128)(2,1)} %param.15) | copy-start | bytes 18436
  0.0 9.2 %copy-start.1 = (bf16[8,3072]{1,0:T(8,128)(2,1)S(1)}, bf16[8,3072]{1,0:T(8,128)(2,1)}, u32[]{:S(2)}) copy-start(bf16[8,3072]{1,0:T(8,128)(2,1)} %pos_ref.1) | copy-start | bytes 147460
  0.0 9.2 %copy-start.4 = (s32[16]{0:T(128)S(1)}, s32[16]{0:T(128)}, u32[]{:S(2)}) copy-start(s32[16]{0:T(128)} %block_ref.1) | copy-start | bytes 196
  0.0 9.2 %copy-start.3 = (s32[8]{0:T(128)S(1)}, s32[8]{0:T(128)}, u32[]{:S(2)}) copy-start(s32[8]{0:T(128)} %order_ref.1) | copy-start | bytes 100
  1.8 14.7 %all-to-all-start = ((bf16[32,1,8,128]{3,2,1,0:T(8,128)(2,1)}), bf16[32,1,8,128]{3,2,1,0:T(8,128)(2,1)S(1)}, u32[]{:S(2)}, u32[]{:S(2)}) async-start(bf16[32,1,8,128]{3,2,1,0:T(8,128)(2,1)} %partial_latents.1), calls=%async_computation | async-start | bytes 131072 | tf_op jit(solution)/shard_map/all_to_all | solution.py:395
  18.5 2.2 %collective-permute-start = (bf16[4,3072]{1,0:T(4,128)(2,1)S(1)}, bf16[4,3072]{1,0:T(4,128)(2,1)S(1)}, u32[]{:S(2)}, u32[]{:S(2)}) collective-permute-start(bf16[4,3072]{1,0:T(4,128)(2,1)S(1)} %get-tuple-element.36), channel_id=1, source_target_pairs={{0,1},{1,0},{2,3},{3,2},{4,5},{5,4},{6,7},{7,6},{8,9},{9,8},{10,11... | collective-permute-start | bytes 73736 | tf_op jit(solution)/shard_map/ppermute | solution.py:342
  18.6 4.1 %collective-permute-start.1 = (bf16[4,3072]{1,0:T(4,128)(2,1)S(1)}, bf16[4,3072]{1,0:T(4,128)(2,1)S(1)}, u32[]{:S(2)}, u32[]{:S(2)}) collective-permute-start(bf16[4,3072]{1,0:T(4,128)(2,1)S(1)} %get-tuple-element.37), channel_id=1, source_target_pairs={{0,2},{1,3},{2,0},{3,1},{4,6},{5,7},{6,4},{7,5},{8,10},{9,11},{10,... | collective-permute-start | bytes 73736 | tf_op jit(solution)/shard_map/ppermute | solution.py:342
  19.3 3.5 %collective-permute-start.2 = (bf16[4,3072]{1,0:T(4,128)(2,1)S(1)}, bf16[4,3072]{1,0:T(4,128)(2,1)S(1)}, u32[]{:S(2)}, u32[]{:S(2)}) collective-permute-start(bf16[4,3072]{1,0:T(4,128)(2,1)S(1)} %get-tuple-element.38), channel_id=1, source_target_pairs={{0,3},{1,2},{2,1},{3,0},{4,7},{5,6},{6,5},{7,4},{8,11},{9,10},{10,... | collective-permute-start | bytes 73736 | tf_op jit(solution)/shard_map/ppermute | solution.py:342

commit v13 on v12

--- a/solution.py
+++ b/solution.py
@@ -42,21 +42,29 @@
     slots, frames, depth = hidden_ref.shape
     everyone, _, window, channels = out_ref.shape
     seqs = frames // frame_dev
-    arrivals = [pltpu.make_async_copy(hidden_hbm, hidden_ref, in_sems.at[0])]
-    for index, at in enumerate(range(0, depth, LANES)):
-        piece = pl.ds(at, LANES)
+    hidden = pltpu.make_async_copy(hidden_hbm, hidden_ref, in_sems.at[0])
+    deep = depth // 3 if depth % (3 * LANES) == 0 else depth
+    arrivals = []
+    for index, at in enumerate(range(0, depth, deep)):
+        piece = pl.ds(at, deep)
         arrivals.append(
             pltpu.make_async_copy(
                 weight_hbm.at[piece], weight_ref.at[piece], in_sems.at[index + 1]
             )
         )
+    hidden.start()
     for copy in arrivals:
         copy.start()
     padded_ref[...] = jnp.zeros_like(padded_ref)
-    for copy in arrivals:
+    hidden.wait()
+    partial = [jnp.zeros((frames, channels), jnp.float32)] * slots
+    for index, copy in enumerate(arrivals):
         copy.wait()
+        here = slice(index * deep, (index + 1) * deep)
+        for slot in range(slots):
+            partial[slot] = partial[slot] + dot(hidden_ref[slot, :, here], weight_ref[here])
     for slot in range(slots):
-        padded_ref[slot, REACH : REACH + frames] = dot(hidden_ref[slot], weight_ref[...])
+        padded_ref[slot, REACH : REACH + frames] = partial[slot]
     pieces = [
         padded_ref[:, to * frame_dev : to * frame_dev + window].astype(out_ref.dtype)
         for to in range(seqs)

time: 23.6 us -> 23.8 us (level)
  no operation moved by 1% of the time
where the time goes in v13:
time: 23.8 us; the launch traced here: 23.6 us
  Pallas kernels  10.3 us (43%)
  starting transfers between devices  9.25 us (39%)
  waiting for transfers between devices  3.94 us (17%)
    all_to_all x1, starting transfers between devices, on_device(): lax.all_to_all(windows, SCATTERED, split_axis=0, concat_axis=0, tiled=True)  7.32 us
    pallas_call x1, Pallas kernels, on_device(): pl.pallas_call(functools.partial(weights_kernel, frame_dev, window), out_...  5.49 us
    ppermute x3, waiting for transfers between devices, to_member(): return lax.ppermute(block, GROUP, route)  2.14 us
    pallas_call x1, Pallas kernels, on_device(): pl.pallas_call(functools.partial(attend_kernel, roles), out_shape=(array(...  1.99 us
    pallas_call x1, Pallas kernels, on_device(): pl.pallas_call(functools.partial(latent_kernel, frame_dev), out_shape=arr...  1.95 us
    ppermute x3, starting transfers between devices, to_member(): return lax.ppermute(block, GROUP, route)  1.93 us
    all_to_all x1, waiting for transfers between devices, on_device(): lax.all_to_all(windows, SCATTERED, split_axis=0, concat_axis=0, tiled=True)  1.8 us
    pallas_call x1, Pallas kernels, on_device(): pl.pallas_call(sum_kernel, out_shape=array((share, model), bf16), in_spec...  0.63 us
  transfers between devices with their start and end apart: 4, of which 3 were waited for; matrix products, arithmetic and copies ran while one was open for 0% of the time, Pallas kernels for 24%

profile of v13, /device:TPU:0, one launch (start us, length us, event | category | flops | bytes accessed | tf_op | source)
XLA Modules:
  0.0 23.6 jit_solution(17205844759438463278)
XLA Ops:
  0.0 0.0 copy-start
  0.0 0.0 copy-start.2
  0.0 0.0 copy-start.1
  0.0 0.0 copy-start.4
  0.0 0.0 copy-start.3
  0.0 2.0 %partial_latents.1 = bf16[32,1,8,128]{3,2,1,0:T(8,128)(2,1)} custom-call(bf16[1,16,768]{2,1,0:T(8,128)(2,1)} %hidden_hbm.1, bf16[768,128]{1,0:T(8,128)(2,1)} %weight_hbm.1), custom_call_target="tpu_custom_call" | custom-call | flops 20000000000 | bytes 40000000 | tf_op jit(solution)/shard_map/partial_latents/pallas_call | solution.py:381
  2.0 7.3 %all-to-all-start = ((bf16[32,1,8,128]{3,2,1,0:T(8,128)(2,1)}), bf16[32,1,8,128]{3,2,1,0:T(8,128)(2,1)S(1)}, u32[]{:S(2)}, u32[]{:S(2)}) async-start(bf16[32,1,8,128]{3,2,1,0:T(8,128)(2,1)} %partial_latents.1), calls=%async_computation | async-start | bytes 131072 | tf_op jit(solution)/shard_map/all_to_all | solution.py:403
  9.3 0.0 copy-done
  9.3 0.0 copy-done.2
  9.3 0.0 copy-done.1
  9.3 0.0 copy-done.4
  9.3 0.0 copy-done.3
  9.3 5.5 %weight_products.1 = (bf16[3,256,512]{2,1,0:T(8,128)(2,1)S(1)}, f32[3,8,512]{2,1,0:T(8,128)S(1)}, bf16[256,128]{1,0:T(8,128)(2,1)S(1)}, f32[8,128]{1,0:T(8,128)S...) custom-call(s32[8]{0:T(128)S(1)} %copy-done.3, ...), custom_call_target="tpu_custom_call" | custom-call | flops 1283457024 | bytes 9437184 | tf_op jit(solution)/shard_map/weight_products/pallas_call | solution.py:411
  14.8 1.8 %all-to-all-done.partial_ref = bf16[32,1,8,128]{3,2,1,0:T(8,128)(2,1)S(1)} async-done(((bf16[32,1,8,128]{3,2,1,0:T(8,128)(2,1)}), bf16[32,1,8,128]{3,2,1,0:T(8,128)(2,1)S(1)}, u32[]{:S(2)}, u32[]{:S(2)}) %all-to-all-start) | async-done | bytes 65568 | tf_op jit(solution)/shard_map/all_to_all | solution.py:403
  16.6 2.0 %attend.1 = (bf16[4,128]{1,0:T(4,128)(2,1)S(1)}, f32[4,3072]{1,0:T(4,128)S(1)}, bf16[4,3072]{1,0:T(4,128)(2,1)S(1)}, bf16[4,3072]{1,0:T(4,128)(2,1)S(1)}, bf16[4,3072]{1,0:T(4,128)(2,1)S(1)}) custom-call(bf16[32,1,8,128]{3,2,1,0:T(8,128)(2,1)S(1)} %all-to-all-done.partial_ref, bf16[3,256,512]{2,1,0:T(8,128)(2,1)S(1)} %get-tuple-element.22.scaled_ref, ...), custom_call_target="tpu_custom_call" | custom-call | tf_op jit(solution)/shard_map/attend/pallas_call | solution.py:453
  18.6 0.1 collective-permute-start
  18.7 0.7 %collective-permute-start.1 = (bf16[4,3072]{1,0:T(4,128)(2,1)S(1)}, bf16[4,3072]{1,0:T(4,128)(2,1)S(1)}, u32[]{:S(2)}, u32[]{:S(2)}) collective-permute-start(bf16[4,3072]{1,0:T(4,128)(2,1)S(1)} %get-tuple-element.37), channel_id=1, source_target_pairs={{0,2},{1,3},{2,0},{3,1},{4,6},{5,7},{6,4},{7,5},{8,10},{9,11},{10,... | collective-permute-start | bytes 73736 | tf_op jit(solution)/shard_map/ppermute | solution.py:350
  19.4 1.2 %collective-permute-start.2 = (bf16[4,3072]{1,0:T(4,128)(2,1)S(1)}, bf16[4,3072]{1,0:T(4,128)(2,1)S(1)}, u32[]{:S(2)}, u32[]{:S(2)}) collective-permute-start(bf16[4,3072]{1,0:T(4,128)(2,1)S(1)} %get-tuple-element.38), channel_id=1, source_target_pairs={{0,3},{1,2},{2,1},{3,0},{4,7},{5,6},{6,5},{7,4},{8,11},{9,10},{10,... | collective-permute-start | bytes 73736 | tf_op jit(solution)/shard_map/ppermute | solution.py:350
  20.6 0.2 residual.1.residual_ref
  20.8 0.0 collective-permute-done.refs_0_
  20.8 2.0 %collective-permute-done.1.refs_1_ = bf16[4,3072]{1,0:T(4,128)(2,1)S(1)} collective-permute-done((bf16[4,3072]{1,0:T(4,128)(2,1)S(1)}, bf16[4,3072]{1,0:T(4,128)(2,1)S(1)}, u32[]{:S(2)}, u32[]{:S(2)}) %collective-permute-start.1) | collective-permute-done | bytes 24608 | tf_op jit(solution)/shard_map/ppermute | solution.py:350
  22.8 0.1 collective-permute-done.2.refs_2_
  22.9 0.6 %final_sum.1 = bf16[4,3072]{1,0:T(4,128)(2,1)} custom-call(f32[4,3072]{1,0:T(4,128)S(1)} %residual.1.residual_ref, f32[4,3072]{1,0:T(4,128)S(1)} %get-tuple-element.35.keep_ref, bf16[4,3072]{1,0:T(4,128)(2,1)S(1)} %collective-permute-done.refs_0_, bf16[4,3072]{1,0:T(4,128)(2,1)S(1)} %collective-permute-done.1.refs_1_, ...), custom_call_target="tpu_custom_call" | custom-call | tf_op jit(solution)/shard_map/final_sum/pallas_call | solution.py:493
Async XLA Ops:
  0.0 9.3 %copy-start = (bf16[128,3072]{1,0:T(8,128)(2,1)S(1)}, bf16[128,3072]{1,0:T(8,128)(2,1)}, u32[]{:S(2)}) copy-start(bf16[128,3072]{1,0:T(8,128)(2,1)} %embed_ref.3) | copy-start | bytes 2359300
  0.0 9.3 %copy-start.2 = (bf16[3072]{0:T(1024)(128)(2,1)S(1)}, bf16[3072]{0:T(1024)(128)(2,1)}, u32[]{:S(2)}) copy-start(bf16[3072]{0:T(1024)(128)(2,1)} %param.15) | copy-start | bytes 18436
  0.0 9.3 %copy-start.1 = (bf16[8,3072]{1,0:T(8,128)(2,1)S(1)}, bf16[8,3072]{1,0:T(8,128)(2,1)}, u32[]{:S(2)}) copy-start(bf16[8,3072]{1,0:T(8,128)(2,1)} %pos_ref.1) | copy-start | bytes 147460
  0.0 9.3 %copy-start.4 = (s32[16]{0:T(128)S(1)}, s32[16]{0:T(128)}, u32[]{:S(2)}) copy-start(s32[16]{0:T(128)} %block_ref.1) | copy-start | bytes 196
  0.0 9.3 %copy-start.3 = (s32[8]{0:T(128)S(1)}, s32[8]{0:T(128)}, u32[]{:S(2)}) copy-start(s32[8]{0:T(128)} %order_ref.1) | copy-start | bytes 100
  2.0 14.7 %all-to-all-start = ((bf16[32,1,8,128]{3,2,1,0:T(8,128)(2,1)}), bf16[32,1,8,128]{3,2,1,0:T(8,128)(2,1)S(1)}, u32[]{:S(2)}, u32[]{:S(2)}) async-start(bf16[32,1,8,128]{3,2,1,0:T(8,128)(2,1)} %partial_latents.1), calls=%async_computation | async-start | bytes 131072 | tf_op jit(solution)/shard_map/all_to_all | solution.py:403
  18.6 2.2 %collective-permute-start = (bf16[4,3072]{1,0:T(4,128)(2,1)S(1)}, bf16[4,3072]{1,0:T(4,128)(2,1)S(1)}, u32[]{:S(2)}, u32[]{:S(2)}) collective-permute-start(bf16[4,3072]{1,0:T(4,128)(2,1)S(1)} %get-tuple-element.36), channel_id=1, source_target_pairs={{0,1},{1,0},{2,3},{3,2},{4,5},{5,4},{6,7},{7,6},{8,9},{9,8},{10,11... | collective-permute-start | bytes 73736 | tf_op jit(solution)/shard_map/ppermute | solution.py:350
  18.7 4.1 %collective-permute-start.1 = (bf16[4,3072]{1,0:T(4,128)(2,1)S(1)}, bf16[4,3072]{1,0:T(4,128)(2,1)S(1)}, u32[]{:S(2)}, u32[]{:S(2)}) collective-permute-start(bf16[4,3072]{1,0:T(4,128)(2,1)S(1)} %get-tuple-element.37), channel_id=1, source_target_pairs={{0,2},{1,3},{2,0},{3,1},{4,6},{5,7},{6,4},{7,5},{8,10},{9,11},{10,... | collective-permute-start | bytes 73736 | tf_op jit(solution)/shard_map/ppermute | solution.py:350
  19.4 3.5 %collective-permute-start.2 = (bf16[4,3072]{1,0:T(4,128)(2,1)S(1)}, bf16[4,3072]{1,0:T(4,128)(2,1)S(1)}, u32[]{:S(2)}, u32[]{:S(2)}) collective-permute-start(bf16[4,3072]{1,0:T(4,128)(2,1)S(1)} %get-tuple-element.38), channel_id=1, source_target_pairs={{0,3},{1,2},{2,1},{3,0},{4,7},{5,6},{6,5},{7,4},{8,11},{9,10},{10,... | collective-permute-start | bytes 73736 | tf_op jit(solution)/shard_map/ppermute | solution.py:350

commit v14 on v12

--- a/solution.py
+++ b/solution.py
@@ -239,7 +239,7 @@
     keep_ref,
     *rest,
 ):
-    *send_refs, second_ref, sem = rest
+    *send_refs, early_ref, second_ref, sem = rest
     half = first_ref.shape[0]
     arrival = pltpu.make_async_copy(out_weight_hbm.at[pl.ds(half, half)], second_ref, sem)
     arrival.start()
@@ -295,6 +295,12 @@
         expo = jnp.exp(scores - jnp.max(scores, axis=-1, keepdims=True))
         probs = (expo / jnp.sum(expo, axis=-1, keepdims=True)).astype(jnp.bfloat16)
         heads.append(dot(probs, value[:, at]).astype(jnp.bfloat16))
+        if (head + 1) * HS == half:
+            done = jnp.concatenate(heads, axis=1)
+            for first in range(0, model, STRIP):
+                here = slice(first, first + STRIP)
+                early_ref[:, here] = dot(done, first_ref[:, here])
+            heads = []
     mine_ref[...] = dot(select_mine_ref[...], latents).astype(jnp.bfloat16)
     heads = jnp.concatenate(heads, axis=1)
     arrival.wait()
@@ -306,7 +312,7 @@
     ]
     for at in range(0, model, STRIP):
         here = slice(at, at + STRIP)
-        mixed = dot(heads[:, :half], first_ref[:, here]) + dot(heads[:, half:], second_ref[:, here])
+        mixed = early_ref[:, here] + dot(heads, second_ref[:, here])
         parts = [mixed[index * share : (index + 1) * share] for index in range(group)]
 
         def of_member(member):
@@ -452,6 +458,7 @@
         in_specs=[VMEM] * 12 + [HBM],
         out_specs=(VMEM,) * (1 + group),
         scratch_shapes=[
+            pltpu.VMEM((own_rows, model), f32),
             pltpu.VMEM((cols - cols // 2, model), bf16),
             pltpu.SemaphoreType.DMA(()),
         ],

time: 23.6 us -> 23.6 us (level)
  no operation moved by 1% of the time
where the time goes in v14:
time: 23.6 us; the launch traced here: 23.4 us
  Pallas kernels  10.1 us (43%)
  starting transfers between devices  9.25 us (39%)
  waiting for transfers between devices  3.94 us (17%)
    all_to_all x1, starting transfers between devices, on_device(): lax.all_to_all(windows, SCATTERED, split_axis=0, concat_axis=0, tiled=True)  7.32 us
    pallas_call x1, Pallas kernels, on_device(): pl.pallas_call(functools.partial(weights_kernel, frame_dev, window), out_...  5.48 us
    ppermute x3, waiting for transfers between devices, to_member(): return lax.ppermute(block, GROUP, route)  2.14 us
    pallas_call x1, Pallas kernels, on_device(): pl.pallas_call(functools.partial(attend_kernel, roles), out_shape=(array(...  1.96 us
    ppermute x3, starting transfers between devices, to_member(): return lax.ppermute(block, GROUP, route)  1.93 us
    all_to_all x1, waiting for transfers between devices, on_device(): lax.all_to_all(windows, SCATTERED, split_axis=0, concat_axis=0, tiled=True)  1.8 us
    pallas_call x1, Pallas kernels, on_device(): pl.pallas_call(functools.partial(latent_kernel, frame_dev), out_shape=arr...  1.8 us
    pallas_call x1, Pallas kernels, on_device(): pl.pallas_call(sum_kernel, out_shape=array((share, model), bf16), in_spec...  0.63 us
  transfers between devices with their start and end apart: 4, of which 3 were waited for; matrix products, arithmetic and copies ran while one was open for 0% of the time, Pallas kernels for 24%

profile of v14, /device:TPU:0, one launch (start us, length us, event | category | flops | bytes accessed | tf_op | source)
XLA Modules:
  0.0 23.4 jit_solution(11884318224658681134)
XLA Ops:
  0.0 0.0 copy-start
  0.0 0.0 copy-start.2
  0.0 0.0 copy-start.1
  0.0 0.0 copy-start.4
  0.0 0.0 copy-start.3
  0.0 1.8 %partial_latents.1 = bf16[32,1,8,128]{3,2,1,0:T(8,128)(2,1)} custom-call(bf16[1,16,768]{2,1,0:T(8,128)(2,1)} %hidden_hbm.1, bf16[768,128]{1,0:T(8,128)(2,1)} %weight_hbm.1), custom_call_target="tpu_custom_call" | custom-call | flops 20000000000 | bytes 40000000 | tf_op jit(solution)/shard_map/partial_latents/pallas_call | solution.py:379
  1.8 7.3 %all-to-all-start = ((bf16[32,1,8,128]{3,2,1,0:T(8,128)(2,1)}), bf16[32,1,8,128]{3,2,1,0:T(8,128)(2,1)S(1)}, u32[]{:S(2)}, u32[]{:S(2)}) async-start(bf16[32,1,8,128]{3,2,1,0:T(8,128)(2,1)} %partial_latents.1), calls=%async_computation | async-start | bytes 131072 | tf_op jit(solution)/shard_map/all_to_all | solution.py:401
  9.1 0.0 copy-done
  9.2 0.0 copy-done.2
  9.2 0.0 copy-done.1
  9.2 0.0 copy-done.4
  9.2 0.0 copy-done.3
  9.2 5.5 %weight_products.1 = (bf16[3,256,512]{2,1,0:T(8,128)(2,1)S(1)}, f32[3,8,512]{2,1,0:T(8,128)S(1)}, bf16[256,128]{1,0:T(8,128)(2,1)S(1)}, f32[8,128]{1,0:T(8,128)S...) custom-call(s32[8]{0:T(128)S(1)} %copy-done.3, ...), custom_call_target="tpu_custom_call" | custom-call | flops 1283457024 | bytes 9437184 | tf_op jit(solution)/shard_map/weight_products/pallas_call | solution.py:409
  14.7 1.8 %all-to-all-done.partial_ref = bf16[32,1,8,128]{3,2,1,0:T(8,128)(2,1)S(1)} async-done(((bf16[32,1,8,128]{3,2,1,0:T(8,128)(2,1)}), bf16[32,1,8,128]{3,2,1,0:T(8,128)(2,1)S(1)}, u32[]{:S(2)}, u32[]{:S(2)}) %all-to-all-start) | async-done | bytes 65568 | tf_op jit(solution)/shard_map/all_to_all | solution.py:401
  16.5 2.0 %attend.1 = (bf16[4,128]{1,0:T(4,128)(2,1)S(1)}, f32[4,3072]{1,0:T(4,128)S(1)}, bf16[4,3072]{1,0:T(4,128)(2,1)S(1)}, bf16[4,3072]{1,0:T(4,128)(2,1)S(1)}, bf16[4,3072]{1,0:T(4,128)(2,1)S(1)}) custom-call(bf16[32,1,8,128]{3,2,1,0:T(8,128)(2,1)S(1)} %all-to-all-done.partial_ref, bf16[3,256,512]{2,1,0:T(8,128)(2,1)S(1)} %get-tuple-element.22.scaled_ref, ...), custom_call_target="tpu_custom_call" | custom-call | tf_op jit(solution)/shard_map/attend/pallas_call | solution.py:451
  18.5 0.1 collective-permute-start
  18.5 0.7 %collective-permute-start.1 = (bf16[4,3072]{1,0:T(4,128)(2,1)S(1)}, bf16[4,3072]{1,0:T(4,128)(2,1)S(1)}, u32[]{:S(2)}, u32[]{:S(2)}) collective-permute-start(bf16[4,3072]{1,0:T(4,128)(2,1)S(1)} %get-tuple-element.37), channel_id=1, source_target_pairs={{0,2},{1,3},{2,0},{3,1},{4,6},{5,7},{6,4},{7,5},{8,10},{9,11},{10,... | collective-permute-start | bytes 73736 | tf_op jit(solution)/shard_map/ppermute | solution.py:348
  19.2 1.2 %collective-permute-start.2 = (bf16[4,3072]{1,0:T(4,128)(2,1)S(1)}, bf16[4,3072]{1,0:T(4,128)(2,1)S(1)}, u32[]{:S(2)}, u32[]{:S(2)}) collective-permute-start(bf16[4,3072]{1,0:T(4,128)(2,1)S(1)} %get-tuple-element.38), channel_id=1, source_target_pairs={{0,3},{1,2},{2,1},{3,0},{4,7},{5,6},{6,5},{7,4},{8,11},{9,10},{10,... | collective-permute-start | bytes 73736 | tf_op jit(solution)/shard_map/ppermute | solution.py:348
  20.4 0.2 residual.1.residual_ref
  20.6 0.0 collective-permute-done.refs_0_
  20.6 2.0 %collective-permute-done.1.refs_1_ = bf16[4,3072]{1,0:T(4,128)(2,1)S(1)} collective-permute-done((bf16[4,3072]{1,0:T(4,128)(2,1)S(1)}, bf16[4,3072]{1,0:T(4,128)(2,1)S(1)}, u32[]{:S(2)}, u32[]{:S(2)}) %collective-permute-start.1) | collective-permute-done | bytes 24608 | tf_op jit(solution)/shard_map/ppermute | solution.py:348
  22.6 0.1 collective-permute-done.2.refs_2_
  22.7 0.6 %final_sum.1 = bf16[4,3072]{1,0:T(4,128)(2,1)} custom-call(f32[4,3072]{1,0:T(4,128)S(1)} %residual.1.residual_ref, f32[4,3072]{1,0:T(4,128)S(1)} %get-tuple-element.35.keep_ref, bf16[4,3072]{1,0:T(4,128)(2,1)S(1)} %collective-permute-done.refs_0_, bf16[4,3072]{1,0:T(4,128)(2,1)S(1)} %collective-permute-done.1.refs_1_, ...), custom_call_target="tpu_custom_call" | custom-call | tf_op jit(solution)/shard_map/final_sum/pallas_call | solution.py:492
Async XLA Ops:
  0.0 9.1 %copy-start = (bf16[128,3072]{1,0:T(8,128)(2,1)S(1)}, bf16[128,3072]{1,0:T(8,128)(2,1)}, u32[]{:S(2)}) copy-start(bf16[128,3072]{1,0:T(8,128)(2,1)} %embed_ref.3) | copy-start | bytes 2359300
  0.0 9.2 %copy-start.2 = (bf16[3072]{0:T(1024)(128)(2,1)S(1)}, bf16[3072]{0:T(1024)(128)(2,1)}, u32[]{:S(2)}) copy-start(bf16[3072]{0:T(1024)(128)(2,1)} %param.15) | copy-start | bytes 18436
  0.0 9.2 %copy-start.1 = (bf16[8,3072]{1,0:T(8,128)(2,1)S(1)}, bf16[8,3072]{1,0:T(8,128)(2,1)}, u32[]{:S(2)}) copy-start(bf16[8,3072]{1,0:T(8,128)(2,1)} %pos_ref.1) | copy-start | bytes 147460
  0.0 9.2 %copy-start.4 = (s32[16]{0:T(128)S(1)}, s32[16]{0:T(128)}, u32[]{:S(2)}) copy-start(s32[16]{0:T(128)} %block_ref.1) | copy-start | bytes 196
  0.0 9.2 %copy-start.3 = (s32[8]{0:T(128)S(1)}, s32[8]{0:T(128)}, u32[]{:S(2)}) copy-start(s32[8]{0:T(128)} %order_ref.1) | copy-start | bytes 100
  1.8 14.7 %all-to-all-start = ((bf16[32,1,8,128]{3,2,1,0:T(8,128)(2,1)}), bf16[32,1,8,128]{3,2,1,0:T(8,128)(2,1)S(1)}, u32[]{:S(2)}, u32[]{:S(2)}) async-start(bf16[32,1,8,128]{3,2,1,0:T(8,128)(2,1)} %partial_latents.1), calls=%async_computation | async-start | bytes 131072 | tf_op jit(solution)/shard_map/all_to_all | solution.py:401
  18.5 2.2 %collective-permute-start = (bf16[4,3072]{1,0:T(4,128)(2,1)S(1)}, bf16[4,3072]{1,0:T(4,128)(2,1)S(1)}, u32[]{:S(2)}, u32[]{:S(2)}) collective-permute-start(bf16[4,3072]{1,0:T(4,128)(2,1)S(1)} %get-tuple-element.36), channel_id=1, source_target_pairs={{0,1},{1,0},{2,3},{3,2},{4,5},{5,4},{6,7},{7,6},{8,9},{9,8},{10,11... | collective-permute-start | bytes 73736 | tf_op jit(solution)/shard_map/ppermute | solution.py:348
  18.5 4.1 %collective-permute-start.1 = (bf16[4,3072]{1,0:T(4,128)(2,1)S(1)}, bf16[4,3072]{1,0:T(4,128)(2,1)S(1)}, u32[]{:S(2)}, u32[]{:S(2)}) collective-permute-start(bf16[4,3072]{1,0:T(4,128)(2,1)S(1)} %get-tuple-element.37), channel_id=1, source_target_pairs={{0,2},{1,3},{2,0},{3,1},{4,6},{5,7},{6,4},{7,5},{8,10},{9,11},{10,... | collective-permute-start | bytes 73736 | tf_op jit(solution)/shard_map/ppermute | solution.py:348
  19.2 3.5 %collective-permute-start.2 = (bf16[4,3072]{1,0:T(4,128)(2,1)S(1)}, bf16[4,3072]{1,0:T(4,128)(2,1)S(1)}, u32[]{:S(2)}, u32[]{:S(2)}) collective-permute-start(bf16[4,3072]{1,0:T(4,128)(2,1)S(1)} %get-tuple-element.38), channel_id=1, source_target_pairs={{0,3},{1,2},{2,1},{3,0},{4,7},{5,6},{6,5},{7,4},{8,11},{9,10},{10,... | collective-permute-start | bytes 73736 | tf_op jit(solution)/shard_map/ppermute | solution.py:348

commit v15 on v12

--- a/solution.py
+++ b/solution.py
@@ -11,7 +11,7 @@
 MOSTB = 4
 REACH = MOSTB - 1
 GROUP = ("mp", "role")
-SCATTERED = ("role", "mp", "seq")
+SCATTERED = ("mp", "role", "seq")
 LANES = 128
 STEP_ROWS = 256
 DEPTH = 1024

time: 23.6 us -> 23.6 us (level)
  no operation moved by 1% of the time
where the time goes in v15:
time: 23.6 us; the launch traced here: 23.4 us
  Pallas kernels  10.1 us (43%)
  starting transfers between devices  9.24 us (39%)
  waiting for transfers between devices  3.96 us (17%)
    all_to_all x1, starting transfers between devices, on_device(): lax.all_to_all(windows, SCATTERED, split_axis=0, concat_axis=0, tiled=True)  7.32 us
    pallas_call x1, Pallas kernels, on_device(): pl.pallas_call(functools.partial(weights_kernel, frame_dev, window), out_...  5.48 us
    ppermute x3, waiting for transfers between devices, to_member(): return lax.ppermute(block, GROUP, route)  2.22 us
    pallas_call x1, Pallas kernels, on_device(): pl.pallas_call(functools.partial(attend_kernel, roles), out_shape=(array(...  1.99 us
    ppermute x3, starting transfers between devices, to_member(): return lax.ppermute(block, GROUP, route)  1.93 us
    pallas_call x1, Pallas kernels, on_device(): pl.pallas_call(functools.partial(latent_kernel, frame_dev), out_shape=arr...  1.8 us
    all_to_all x1, waiting for transfers between devices, on_device(): lax.all_to_all(windows, SCATTERED, split_axis=0, concat_axis=0, tiled=True)  1.74 us
    pallas_call x1, Pallas kernels, on_device(): pl.pallas_call(sum_kernel, out_shape=array((share, model), bf16), in_spec...  0.63 us
  transfers between devices with their start and end apart: 4, of which 3 were waited for; matrix products, arithmetic and copies ran while one was open for 0% of the time, Pallas kernels for 24%

profile of v15, /device:TPU:0, one launch (start us, length us, event | category | flops | bytes accessed | tf_op | source)
XLA Modules:
  0.0 23.4 jit_solution(14176977378234218100)
XLA Ops:
  0.0 0.0 copy-start
  0.0 0.0 copy-start.2
  0.0 0.0 copy-start.1
  0.0 0.0 copy-start.4
  0.0 0.0 copy-start.3
  0.0 1.8 %partial_latents.1 = bf16[32,1,8,128]{3,2,1,0:T(8,128)(2,1)} custom-call(bf16[1,16,768]{2,1,0:T(8,128)(2,1)} %hidden_hbm.1, bf16[768,128]{1,0:T(8,128)(2,1)} %weight_hbm.1), custom_call_target="tpu_custom_call" | custom-call | flops 20000000000 | bytes 40000000 | tf_op jit(solution)/shard_map/partial_latents/pallas_call | solution.py:373
  1.8 7.3 %all-to-all-start = ((bf16[32,1,8,128]{3,2,1,0:T(8,128)(2,1)}), bf16[32,1,8,128]{3,2,1,0:T(8,128)(2,1)S(1)}, u32[]{:S(2)}, u32[]{:S(2)}) async-start(bf16[32,1,8,128]{3,2,1,0:T(8,128)(2,1)} %partial_latents.1), calls=%async_computation | async-start | bytes 131072 | tf_op jit(solution)/shard_map/all_to_all | solution.py:395
  9.1 0.0 copy-done
  9.2 0.0 copy-done.2
  9.2 0.0 copy-done.1
  9.2 0.0 copy-done.4
  9.2 0.0 copy-done.3
  9.2 5.5 %weight_products.1 = (bf16[3,256,512]{2,1,0:T(8,128)(2,1)S(1)}, f32[3,8,512]{2,1,0:T(8,128)S(1)}, bf16[256,128]{1,0:T(8,128)(2,1)S(1)}, f32[8,128]{1,0:T(8,128)S...) custom-call(s32[8]{0:T(128)S(1)} %copy-done.3, ...), custom_call_target="tpu_custom_call" | custom-call | flops 1283457024 | bytes 9437184 | tf_op jit(solution)/shard_map/weight_products/pallas_call | solution.py:403
  14.7 1.7 %all-to-all-done.partial_ref = bf16[32,1,8,128]{3,2,1,0:T(8,128)(2,1)S(1)} async-done(((bf16[32,1,8,128]{3,2,1,0:T(8,128)(2,1)}), bf16[32,1,8,128]{3,2,1,0:T(8,128)(2,1)S(1)}, u32[]{:S(2)}, u32[]{:S(2)}) %all-to-all-start) | async-done | bytes 65568 | tf_op jit(solution)/shard_map/all_to_all | solution.py:395
  16.4 2.0 %attend.1 = (bf16[4,128]{1,0:T(4,128)(2,1)S(1)}, f32[4,3072]{1,0:T(4,128)S(1)}, bf16[4,3072]{1,0:T(4,128)(2,1)S(1)}, bf16[4,3072]{1,0:T(4,128)(2,1)S(1)}, bf16[4,3072]{1,0:T(4,128)(2,1)S(1)}) custom-call(bf16[32,1,8,128]{3,2,1,0:T(8,128)(2,1)S(1)} %all-to-all-done.partial_ref, bf16[3,256,512]{2,1,0:T(8,128)(2,1)S(1)} %get-tuple-element.22.scaled_ref, ...), custom_call_target="tpu_custom_call" | custom-call | tf_op jit(solution)/shard_map/attend/pallas_call | solution.py:445
  18.4 0.2 collective-permute-start
  18.6 0.7 %collective-permute-start.1 = (bf16[4,3072]{1,0:T(4,128)(2,1)S(1)}, bf16[4,3072]{1,0:T(4,128)(2,1)S(1)}, u32[]{:S(2)}, u32[]{:S(2)}) collective-permute-start(bf16[4,3072]{1,0:T(4,128)(2,1)S(1)} %get-tuple-element.37), channel_id=1, source_target_pairs={{0,2},{1,3},{2,0},{3,1},{4,6},{5,7},{6,4},{7,5},{8,10},{9,11},{10,... | collective-permute-start | bytes 73736 | tf_op jit(solution)/shard_map/ppermute | solution.py:342
  19.3 1.1 %collective-permute-start.2 = (bf16[4,3072]{1,0:T(4,128)(2,1)S(1)}, bf16[4,3072]{1,0:T(4,128)(2,1)S(1)}, u32[]{:S(2)}, u32[]{:S(2)}) collective-permute-start(bf16[4,3072]{1,0:T(4,128)(2,1)S(1)} %get-tuple-element.38), channel_id=1, source_target_pairs={{0,3},{1,2},{2,1},{3,0},{4,7},{5,6},{6,5},{7,4},{8,11},{9,10},{10,... | collective-permute-start | bytes 73736 | tf_op jit(solution)/shard_map/ppermute | solution.py:342
  20.3 0.2 residual.1.residual_ref
  20.6 0.0 collective-permute-done.refs_0_
  20.6 2.1 %collective-permute-done.1.refs_1_ = bf16[4,3072]{1,0:T(4,128)(2,1)S(1)} collective-permute-done((bf16[4,3072]{1,0:T(4,128)(2,1)S(1)}, bf16[4,3072]{1,0:T(4,128)(2,1)S(1)}, u32[]{:S(2)}, u32[]{:S(2)}) %collective-permute-start.1) | collective-permute-done | bytes 24608 | tf_op jit(solution)/shard_map/ppermute | solution.py:342
  22.7 0.1 collective-permute-done.2.refs_2_
  22.8 0.6 %final_sum.1 = bf16[4,3072]{1,0:T(4,128)(2,1)} custom-call(f32[4,3072]{1,0:T(4,128)S(1)} %residual.1.residual_ref, f32[4,3072]{1,0:T(4,128)S(1)} %get-tuple-element.35.keep_ref, bf16[4,3072]{1,0:T(4,128)(2,1)S(1)} %collective-permute-done.refs_0_, bf16[4,3072]{1,0:T(4,128)(2,1)S(1)} %collective-permute-done.1.refs_1_, ...), custom_call_target="tpu_custom_call" | custom-call | tf_op jit(solution)/shard_map/final_sum/pallas_call | solution.py:485
Async XLA Ops:
  0.0 9.1 %copy-start = (bf16[128,3072]{1,0:T(8,128)(2,1)S(1)}, bf16[128,3072]{1,0:T(8,128)(2,1)}, u32[]{:S(2)}) copy-start(bf16[128,3072]{1,0:T(8,128)(2,1)} %embed_ref.3) | copy-start | bytes 2359300
  0.0 9.2 %copy-start.2 = (bf16[3072]{0:T(1024)(128)(2,1)S(1)}, bf16[3072]{0:T(1024)(128)(2,1)}, u32[]{:S(2)}) copy-start(bf16[3072]{0:T(1024)(128)(2,1)} %param.15) | copy-start | bytes 18436
  0.0 9.2 %copy-start.1 = (bf16[8,3072]{1,0:T(8,128)(2,1)S(1)}, bf16[8,3072]{1,0:T(8,128)(2,1)}, u32[]{:S(2)}) copy-start(bf16[8,3072]{1,0:T(8,128)(2,1)} %pos_ref.1) | copy-start | bytes 147460
  0.0 9.2 %copy-start.4 = (s32[16]{0:T(128)S(1)}, s32[16]{0:T(128)}, u32[]{:S(2)}) copy-start(s32[16]{0:T(128)} %block_ref.1) | copy-start | bytes 196
  0.0 9.2 %copy-start.3 = (s32[8]{0:T(128)S(1)}, s32[8]{0:T(128)}, u32[]{:S(2)}) copy-start(s32[8]{0:T(128)} %order_ref.1) | copy-start | bytes 100
  1.8 14.6 %all-to-all-start = ((bf16[32,1,8,128]{3,2,1,0:T(8,128)(2,1)}), bf16[32,1,8,128]{3,2,1,0:T(8,128)(2,1)S(1)}, u32[]{:S(2)}, u32[]{:S(2)}) async-start(bf16[32,1,8,128]{3,2,1,0:T(8,128)(2,1)} %partial_latents.1), calls=%async_computation | async-start | bytes 131072 | tf_op jit(solution)/shard_map/all_to_all | solution.py:395
  18.4 2.1 %collective-permute-start = (bf16[4,3072]{1,0:T(4,128)(2,1)S(1)}, bf16[4,3072]{1,0:T(4,128)(2,1)S(1)}, u32[]{:S(2)}, u32[]{:S(2)}) collective-permute-start(bf16[4,3072]{1,0:T(4,128)(2,1)S(1)} %get-tuple-element.36), channel_id=1, source_target_pairs={{0,1},{1,0},{2,3},{3,2},{4,5},{5,4},{6,7},{7,6},{8,9},{9,8},{10,11... | collective-permute-start | bytes 73736 | tf_op jit(solution)/shard_map/ppermute | solution.py:342
  18.6 4.1 %collective-permute-start.1 = (bf16[4,3072]{1,0:T(4,128)(2,1)S(1)}, bf16[4,3072]{1,0:T(4,128)(2,1)S(1)}, u32[]{:S(2)}, u32[]{:S(2)}) collective-permute-start(bf16[4,3072]{1,0:T(4,128)(2,1)S(1)} %get-tuple-element.37), channel_id=1, source_target_pairs={{0,2},{1,3},{2,0},{3,1},{4,6},{5,7},{6,4},{7,5},{8,10},{9,11},{10,... | collective-permute-start | bytes 73736 | tf_op jit(solution)/shard_map/ppermute | solution.py:342
  19.3 3.5 %collective-permute-start.2 = (bf16[4,3072]{1,0:T(4,128)(2,1)S(1)}, bf16[4,3072]{1,0:T(4,128)(2,1)S(1)}, u32[]{:S(2)}, u32[]{:S(2)}) collective-permute-start(bf16[4,3072]{1,0:T(4,128)(2,1)S(1)} %get-tuple-element.38), channel_id=1, source_target_pairs={{0,3},{1,2},{2,1},{3,0},{4,7},{5,6},{6,5},{7,4},{8,11},{9,10},{10,... | collective-permute-start | bytes 73736 | tf_op jit(solution)/shard_map/ppermute | solution.py:342
